TPU v7x, 32 devices: a whole 2x2x4 slice. The times are simulated.
32 devices in a mesh: dp: 16 (over z, x, core), grp: 2 (over y).
Axes of the slice: x: 2, y: 2, z: 4, core: 2. Of those that a mesh axis runs over, the one named last changes fastest.
Arguments:
- pixels: bfloat16 [1024, 16, 16, 768], P('dp', 'grp'), may hold values from -2.5 to 2.5
- frame_bounds: int32 [1024, 2], P('dp'), may hold values from 96 to 256, as said below
- clip_frames: int32 [256], replicated, may hold values from 1 to 17, 1024 in all
- codes: int32 [1024, 16, 16], P('dp', 'grp'), may hold values from 0 to 63999
- projections: float32 [2, 768, 256], P(None, 'dp'), may hold values from -0.21875 to 0.21875
- blocks: float32 [4, 256, 256], P(None, 'dp'), may hold values from -0.375 to 0.375
- fsq_maps: float32 [2, 256, 6], P(None, 'dp'), may hold values from -0.6 to 0.6
- gains: float32 [2, 256], P(None, 'dp'), may hold values from 0.5 to 1.5
- disc_first: float32 [48, 64], P(None, 'dp'), may hold values from -0.875 to 0.875
- disc_mid: float32 [2048, 128], P('dp'), may hold values from -0.25 to 0.25
- disc_last: float32 [128, 256], P(None, 'dp'), may hold values from -1 to 1
- disc_head: float32 [256], P('dp'), may hold values from -0.25 to 0.25
- moment_projections: float32 [2, 768, 256], P(None, 'dp'), may hold values from -7.8125e-07 to 7.8125e-07
- moment_blocks: float32 [4, 256, 256], P(None, 'dp'), may hold values from -7.8125e-07 to 7.8125e-07
- moment_fsq_maps: float32 [2, 256, 6], P(None, 'dp'), may hold values from -2.2097087e-05 to 2.2097087e-05
- moment_gains: float32 [2, 256], P(None, 'dp'), may hold values from -1.171875e-05 to 1.171875e-05
- moment_disc_first: float32 [48, 64], P(None, 'dp'), may hold values from -0.0015 to 0.0015
- moment_disc_mid: float32 [2048, 128], P('dp'), may hold values from -0.0015 to 0.0015
- moment_disc_last: float32 [128, 256], P(None, 'dp'), may hold values from -0.0015 to 0.0015
- moment_disc_head: float32 [256], P('dp'), may hold values from -0.006 to 0.006
- square_projections: float32 [2, 768, 256], P(None, 'dp'), may hold values from 3.8146973e-13 to 1.5258789e-12
- square_blocks: float32 [4, 256, 256], P(None, 'dp'), may hold values from 3.8146973e-13 to 1.5258789e-12
- square_fsq_maps: float32 [2, 256, 6], P(None, 'dp'), may hold values from 5.859375e-11 to 9.765625e-10
- square_gains: float32 [2, 256], P(None, 'dp'), may hold values from 9.155274e-11 to 3.0517577e-10
- square_disc_first: float32 [48, 64], P(None, 'dp'), may hold values from 3e-07 to 5e-06
- square_disc_mid: float32 [2048, 128], P('dp'), may hold values from 3e-07 to 5e-06
- square_disc_last: float32 [128, 256], P(None, 'dp'), may hold values from 3e-07 to 5e-06
- square_disc_head: float32 [256], P('dp'), may hold values from 5e-06 to 8e-05
Outputs:
- new_moment_projections: float32 [2, 768, 256], P(None, 'dp')
- new_moment_blocks: float32 [4, 256, 256], P(None, 'dp')
- new_moment_fsq_maps: float32 [2, 256, 6], P(None, 'dp')
- new_moment_gains: float32 [2, 256], P(None, 'dp')
- new_moment_disc_first: float32 [48, 64], P(None, 'dp')
- new_moment_disc_mid: float32 [2048, 128], P('dp')
- new_moment_disc_last: float32 [128, 256], P(None, 'dp')
- new_moment_disc_head: float32 [256], P('dp')
- new_square_projections: float32 [2, 768, 256], P(None, 'dp')
- new_square_blocks: float32 [4, 256, 256], P(None, 'dp')
- new_square_fsq_maps: float32 [2, 256, 6], P(None, 'dp')
- new_square_gains: float32 [2, 256], P(None, 'dp')
- new_square_disc_first: float32 [48, 64], P(None, 'dp')
- new_square_disc_mid: float32 [2048, 128], P('dp')
- new_square_disc_last: float32 [128, 256], P(None, 'dp')
- new_square_disc_head: float32 [256], P('dp')
- new_projections: float32 [2, 768, 256], P(None, 'dp')
- new_blocks: float32 [4, 256, 256], P(None, 'dp')
- new_fsq_maps: float32 [2, 256, 6], P(None, 'dp')
- new_gains: float32 [2, 256], P(None, 'dp')
- new_disc_first: float32 [48, 64], P(None, 'dp')
- new_disc_mid: float32 [2048, 128], P('dp')
- new_disc_last: float32 [128, 256], P(None, 'dp')
- new_disc_head: float32 [256], P('dp')
- loss_terms: float32 [2], replicated
- adversarial_sums: float32 [2], replicated
- perplexity: float32 [], replicated
Inputs may be any that keep to these rules, and one draw needn't show every extreme that they name: `frame_bounds`: height and width bounds of a valid top-left rectangle; some frame has both at 256.
All inputs are finite; a program needn't handle non-finite values.
Results may differ from a plain program's by a relative error of at most 0.0019.
The roundings to bfloat16 on the way count: a program that leaves them out, or rounds other values in their place, can miss the bound.
Values may be sent and summed in bfloat16 or wider, within the bound.
No kernel may reach another device: no remote copies, remote signals or barrier semaphores. Data moves between devices by JAX's collectives and lax.ppermute only.
A program may use at most 896 MiB of HBM per device.

v0:
```python
import jax
import jax.numpy as jnp
from jax import lax
from jax.sharding import PartitionSpec as P

CODES = 64000
MICRO = 2
STEP = 10


EPS_NORM = 1e-06
BETA_ONE = 0.9
BETA_TWO = 0.95
ADAM_EPS = 1e-08
DECAY = 0.1
RATE_MATRIX = 0.04
RATE_GAIN = 0.25
GEN_WEIGHT = 0.02
HALVES = (3.5, 3.5, 3.5, 2.0, 2.0, 2.0)
LEVELS = (8, 8, 8, 5, 5, 5)


def passed_along(x, axis, by):
    size = lax.axis_size(axis)
    pairs = [(i, i + by) for i in range(size) if 0 <= i + by < size]
    return lax.ppermute(x, axis, pairs)


def mat_dot(operand, weights):
    return jnp.dot(operand, weights, preferred_element_type=jnp.float32)


def dot_lead(operand, other):
    return lax.dot_general(
        operand, other, (((0,), (0,)), ((), ())), preferred_element_type=jnp.float32
    )


def dot_trail(operand, other):
    return lax.dot_general(
        operand, other, (((1,), (1,)), ((), ())), preferred_element_type=jnp.float32
    )


def silu_slope(preact):
    sigmoid = jax.nn.sigmoid(preact)
    return sigmoid * (1.0 + preact * (1.0 - sigmoid))


def frame_weights(bounds, clip_frames, first_frame):
    clip_ends = jnp.cumsum(clip_frames)
    frame_index = first_frame + jnp.arange(bounds.shape[0], dtype=jnp.int32)
    clip_of = jnp.sum((clip_ends[None, :] <= frame_index[:, None]).astype(jnp.int32), axis=1)
    picked = jnp.sum(
        jnp.where(
            clip_of[:, None] == jnp.arange(clip_frames.shape[0], dtype=jnp.int32)[None, :],
            clip_frames[None, :],
            0,
        ),
        axis=1,
    )
    return 1.0 / picked.astype(jnp.float32)


def pixel_mask(bounds, row_start, band_rows, width):
    places = jnp.arange(width, dtype=jnp.int32)
    subpatch = places // 48
    within = places % 48
    down = subpatch // 4 * 4 + within // 12
    across = subpatch % 4 * 4 + within % 12 // 3
    pixel_rows = (row_start + jnp.arange(band_rows, dtype=jnp.int32))[:, None] * 16 + down[None, :]
    pixel_cols = jnp.arange(16, dtype=jnp.int32)[:, None] * 16 + across[None, :]
    inside = (pixel_rows[None, :, None, :] < bounds[:, 0][:, None, None, None]) & (
        pixel_cols[None, None, :, :] < bounds[:, 1][:, None, None, None]
    )
    return inside.astype(jnp.float32)


def code_values(codes):
    parts = []
    remains = codes
    for levels, halves in zip(LEVELS, HALVES):
        parts.append(((remains % levels).astype(jnp.float32) - halves) / halves)
        remains = remains // levels
    return jnp.stack(parts, axis=-1)


def block_forward(stream, gain_row, first_mat, second_mat):
    scaling = lax.rsqrt(jnp.mean(stream * stream, axis=-1, keepdims=True) + EPS_NORM)
    normed = (stream * scaling * gain_row).astype(jnp.bfloat16)
    inside = mat_dot(normed, first_mat)
    acted = jax.nn.silu(inside).astype(jnp.bfloat16)
    return (stream + mat_dot(acted, second_mat), (stream, scaling, normed, inside, acted))


def block_backward(grad_out, saved, gain_row, first_mat, second_mat):
    stream, scaling, normed, inside, acted = saved
    grad_low = grad_out.astype(jnp.bfloat16)
    grad_second = dot_lead(acted, grad_low)
    grad_inside = (dot_trail(grad_low, second_mat) * silu_slope(inside)).astype(jnp.bfloat16)
    grad_first = dot_lead(normed, grad_inside)
    grad_normed = dot_trail(grad_inside, first_mat)
    normal = stream * scaling
    grad_gain = jnp.sum(grad_normed * normal, axis=0)
    grad_normal = grad_normed * gain_row
    grad_stream = scaling * (
        grad_normal - normal * jnp.mean(grad_normal * normal, axis=-1, keepdims=True)
    )
    return (grad_out + grad_stream, grad_gain, grad_first, grad_second)


def judge_forward(inputs, weights):
    first_conv, mid_conv, last_conv, head_map = weights
    frames, band_rows = (inputs.shape[0], inputs.shape[1])
    count_rows = frames * band_rows * 16
    patches = inputs.reshape(count_rows * 16, 48)
    pre_one = mat_dot(patches, first_conv).reshape(count_rows, -1)
    act_one = jax.nn.silu(pre_one).astype(jnp.bfloat16)
    layout = act_one.reshape(frames, band_rows, 16, -1)
    incoming = passed_along(layout[:, 0], "grp", -1)
    below = jnp.concatenate([layout[:, 1:], incoming[:, None]], axis=1).reshape(count_rows, -1)
    joined = jnp.concatenate([act_one, below], axis=-1)
    pre_two = mat_dot(joined, mid_conv)
    act_two = jax.nn.silu(pre_two).astype(jnp.bfloat16)
    pre_three = mat_dot(act_two, last_conv)
    act_three = jax.nn.silu(pre_three).astype(jnp.bfloat16)
    scores = mat_dot(act_three, head_map)
    return (
        scores,
        (patches, pre_one, joined, pre_two, act_two, pre_three, act_three, frames, band_rows),
    )


def judge_backward(grad_scores, saved, weights):
    first_conv, mid_conv, last_conv, head_map = weights
    patches, pre_one, joined, pre_two, act_two, pre_three, act_three, frames, band_rows = saved
    grad_head = jnp.dot(grad_scores, act_three.astype(jnp.float32))
    grad_three = (
        grad_scores[:, None] * head_map.astype(jnp.float32)[None, :] * silu_slope(pre_three)
    ).astype(jnp.bfloat16)
    grad_last = dot_lead(act_two, grad_three)
    grad_two = (dot_trail(grad_three, last_conv) * silu_slope(pre_two)).astype(jnp.bfloat16)
    grad_mid = dot_lead(joined, grad_two)
    grad_joined = dot_trail(grad_two, mid_conv)
    half_width = grad_joined.shape[1] // 2
    own_part = grad_joined[:, :half_width]
    below_part = (
        grad_joined[:, half_width:].astype(jnp.bfloat16).reshape(frames, band_rows, 16, half_width)
    )
    returned = passed_along(below_part[:, band_rows - 1], "grp", 1)
    moved = jnp.concatenate([returned[:, None], below_part[:, : band_rows - 1]], axis=1).reshape(
        -1, half_width
    )
    grad_one = ((own_part + moved.astype(jnp.float32)) * silu_slope(pre_one)).astype(jnp.bfloat16)
    grad_small = grad_one.reshape(patches.shape[0], first_conv.shape[1])
    grad_first = dot_lead(patches, grad_small)
    grad_input = dot_trail(grad_small, first_conv).reshape(grad_one.shape[0], -1)
    return ((grad_first, grad_mid, grad_last, grad_head), grad_input)


def micro_step(pixels, coded, weight_mask, gathered, total_weight, count_all):
    project, matrices, fsq_pair, gain_pair, first_conv, mid_conv, last_conv, head_map = gathered
    judge_weights = (first_conv, mid_conv, last_conv, head_map)
    pixel_rows = pixels.reshape(-1, pixels.shape[-1])
    stream = mat_dot(pixel_rows, project[0])
    middle, enc_saved = block_forward(stream, gain_pair[0], matrices[0], matrices[1])
    middle_low = middle.astype(jnp.bfloat16)
    latent = mat_dot(middle_low, fsq_pair[0])
    values = coded.reshape(-1, 6).astype(jnp.bfloat16)
    start = dot_trail(values, fsq_pair[1])
    output, dec_saved = block_forward(start, gain_pair[1], matrices[2], matrices[3])
    output_low = output.astype(jnp.bfloat16)
    recon = dot_trail(output_low, project[1])
    fake = recon.astype(jnp.bfloat16)
    real_scores, real_saved = judge_forward(pixels, judge_weights)
    fake_scores, fake_saved = judge_forward(fake.reshape(pixels.shape), judge_weights)
    diff = recon - pixel_rows.astype(jnp.float32)
    smooth = jnp.sqrt(diff * diff + 1.0)
    mask_rows = weight_mask.reshape(pixel_rows.shape)
    l1_sum = jnp.sum(mask_rows * smooth)
    gen_sum = jnp.sum(-fake_scores)
    disc_sum = jnp.sum(jax.nn.softplus(1.0 - real_scores)) + jnp.sum(
        jax.nn.softplus(1.0 + fake_scores)
    )
    real_grads, unused_real = judge_backward(
        -jax.nn.sigmoid(1.0 - real_scores) / count_all, real_saved, judge_weights
    )
    fake_grads, unused_fake = judge_backward(
        jax.nn.sigmoid(1.0 + fake_scores) / count_all, fake_saved, judge_weights
    )
    unused_grads, fake_input = judge_backward(
        jnp.full_like(fake_scores, -GEN_WEIGHT / count_all), fake_saved, judge_weights
    )
    grad_recon = mask_rows * diff / smooth / total_weight + fake_input
    grad_low = grad_recon.astype(jnp.bfloat16)
    grad_out_proj = dot_lead(grad_low, output_low)
    grad_output = mat_dot(grad_low, project[1])
    grad_start, gain_dec, grad_mat_two, grad_mat_three = block_backward(
        grad_output, dec_saved, gain_pair[1], matrices[2], matrices[3]
    )
    start_low = grad_start.astype(jnp.bfloat16)
    grad_fsq_out = dot_lead(start_low, values)
    grad_values = mat_dot(start_low, fsq_pair[1])
    tangent = jnp.tanh(latent)
    grad_latent = (grad_values * (1.0 - tangent * tangent)).astype(jnp.bfloat16)
    grad_fsq_in = dot_lead(middle_low, grad_latent)
    grad_middle = dot_trail(grad_latent, fsq_pair[0])
    grad_stream, gain_enc, grad_mat_zero, grad_mat_one = block_backward(
        grad_middle, enc_saved, gain_pair[0], matrices[0], matrices[1]
    )
    grad_in_proj = dot_lead(pixel_rows, grad_stream.astype(jnp.bfloat16))
    grads = (
        jnp.stack([grad_in_proj, grad_out_proj]),
        jnp.stack([grad_mat_zero, grad_mat_one, grad_mat_two, grad_mat_three]),
        jnp.stack([grad_fsq_in, grad_fsq_out]),
        jnp.stack([gain_enc, gain_dec]),
        real_grads[0] + fake_grads[0],
        real_grads[1] + fake_grads[1],
        real_grads[2] + fake_grads[2],
        real_grads[3] + fake_grads[3],
    )
    return (grads, jnp.stack([l1_sum, gen_sum, disc_sum]))


def adamw(master, moment, square, grad, rate, decay):
    new_moment = BETA_ONE * moment + (1.0 - BETA_ONE) * grad
    new_square = BETA_TWO * square + (1.0 - BETA_TWO) * grad * grad
    update = (
        new_moment
        / (1.0 - BETA_ONE**STEP)
        / (jnp.sqrt(new_square / (1.0 - BETA_TWO**STEP)) + ADAM_EPS)
    )
    return (new_moment, new_square, master - rate * (update + decay * master))


def add_tuples(first_tuple, second_tuple):
    return tuple(
        (left_item + right_item for left_item, right_item in zip(first_tuple, second_tuple))
    )


def on_device(
    pixels,
    frame_bounds,
    clip_frames,
    codes,
    projections,
    blocks,
    fsq_maps,
    gains,
    disc_first,
    disc_mid,
    disc_last,
    disc_head,
    moment_projections,
    moment_blocks,
    moment_fsq_maps,
    moment_gains,
    moment_disc_first,
    moment_disc_mid,
    moment_disc_last,
    moment_disc_head,
    square_projections,
    square_blocks,
    square_fsq_maps,
    square_gains,
    square_disc_first,
    square_disc_mid,
    square_disc_last,
    square_disc_head,
):
    masters = (projections, blocks, fsq_maps, gains, disc_first, disc_mid, disc_last, disc_head)
    moments = (
        moment_projections,
        moment_blocks,
        moment_fsq_maps,
        moment_gains,
        moment_disc_first,
        moment_disc_mid,
        moment_disc_last,
        moment_disc_head,
    )
    squares = (
        square_projections,
        square_blocks,
        square_fsq_maps,
        square_gains,
        square_disc_first,
        square_disc_mid,
        square_disc_last,
        square_disc_head,
    )
    frames, band_rows, width = (pixels.shape[0], pixels.shape[1], pixels.shape[-1])
    weighting = frame_weights(frame_bounds, clip_frames, lax.axis_index("dp") * frames)
    weight_mask = (
        pixel_mask(frame_bounds, lax.axis_index("grp") * band_rows, band_rows, width)
        * weighting[:, None, None, None]
    )
    counts = jax.ops.segment_sum(
        jnp.ones((codes.size,), jnp.float32), codes.reshape(-1), num_segments=CODES
    )
    total_weight, counts = lax.psum((jnp.sum(weight_mask), counts), ("dp", "grp"))
    count_all = float(frames * lax.axis_size("dp") * 256)
    coded = code_values(codes)
    shards = tuple((weight.astype(jnp.bfloat16) for weight in masters))
    gathered = None
    per_micro = frames // MICRO
    totals = None
    losses = jnp.zeros((3,), jnp.float32)
    for number in range(MICRO):
        gathered = (
            lax.all_gather(shards[0], "dp", axis=1, tiled=True),
            lax.all_gather(shards[1], "dp", axis=1, tiled=True),
            lax.all_gather(shards[2], "dp", axis=1, tiled=True),
            lax.all_gather(shards[3], "dp", axis=1, tiled=True),
            lax.all_gather(shards[4], "dp", axis=1, tiled=True),
            lax.all_gather(shards[5], "dp", axis=0, tiled=True),
            lax.all_gather(shards[6], "dp", axis=1, tiled=True),
            lax.all_gather(shards[7], "dp", axis=0, tiled=True),
        )
        lower = number * per_micro
        upper = lower + per_micro
        grads, loss_part = micro_step(
            pixels[lower:upper],
            coded[lower:upper],
            weight_mask[lower:upper],
            gathered,
            total_weight,
            count_all,
        )
        losses = losses + loss_part
        shares = (
            lax.psum_scatter(grads[0], "dp", scatter_dimension=1, tiled=True),
            lax.psum_scatter(grads[1], "dp", scatter_dimension=1, tiled=True),
            lax.psum_scatter(grads[2], "dp", scatter_dimension=1, tiled=True),
            lax.psum_scatter(grads[3], "dp", scatter_dimension=1, tiled=True),
            lax.psum_scatter(grads[4], "dp", scatter_dimension=1, tiled=True),
            lax.psum_scatter(grads[5], "dp", scatter_dimension=0, tiled=True),
            lax.psum_scatter(grads[6], "dp", scatter_dimension=1, tiled=True),
            lax.psum_scatter(grads[7], "dp", scatter_dimension=0, tiled=True),
        )
        totals = shares if totals is None else add_tuples(totals, shares)
    totals = lax.psum(
        (totals[0], totals[1], totals[2], totals[3], totals[4], totals[5], totals[6], totals[7]),
        "grp",
    )
    losses = lax.psum(losses, ("dp", "grp"))
    results = [
        adamw(
            masters[number],
            moments[number],
            squares[number],
            totals[number],
            RATE_GAIN if number == 3 else RATE_MATRIX,
            0.0 if number == 3 else DECAY,
        )
        for number in range(8)
    ]
    shares_all = counts / jnp.sum(counts)
    perplexity = jnp.exp(-jnp.sum(jax.scipy.special.xlogy(shares_all, shares_all)))
    loss_terms = jnp.stack([losses[0], total_weight])
    adversarial_sums = jnp.stack([losses[1], losses[2]])
    return (
        results[0][0],
        results[1][0],
        results[2][0],
        results[3][0],
        results[4][0],
        results[5][0],
        results[6][0],
        results[7][0],
        results[0][1],
        results[1][1],
        results[2][1],
        results[3][1],
        results[4][1],
        results[5][1],
        results[6][1],
        results[7][1],
        results[0][2],
        results[1][2],
        results[2][2],
        results[3][2],
        results[4][2],
        results[5][2],
        results[6][2],
        results[7][2],
        loss_terms,
        adversarial_sums,
        perplexity,
    )


def solution(mesh):
    placed = (
        P("dp", "grp", None, None),
        P("dp", None),
        P(),
        P("dp", "grp", None),
        P(None, "dp", None),
        P(None, "dp", None),
        P(None, "dp", None),
        P(None, "dp"),
        P(None, "dp"),
        P("dp", None),
        P(None, "dp"),
        P("dp"),
        P(None, "dp", None),
        P(None, "dp", None),
        P(None, "dp", None),
        P(None, "dp"),
        P(None, "dp"),
        P("dp", None),
        P(None, "dp"),
        P("dp"),
        P(None, "dp", None),
        P(None, "dp", None),
        P(None, "dp", None),
        P(None, "dp"),
        P(None, "dp"),
        P("dp", None),
        P(None, "dp"),
        P("dp"),
    )
    return jax.shard_map(
        on_device,
        mesh=mesh,
        in_specs=placed,
        out_specs=(
            P(None, "dp", None),
            P(None, "dp", None),
            P(None, "dp", None),
            P(None, "dp"),
            P(None, "dp"),
            P("dp", None),
            P(None, "dp"),
            P("dp"),
            P(None, "dp", None),
            P(None, "dp", None),
            P(None, "dp", None),
            P(None, "dp"),
            P(None, "dp"),
            P("dp", None),
            P(None, "dp"),
            P("dp"),
            P(None, "dp", None),
            P(None, "dp", None),
            P(None, "dp", None),
            P(None, "dp"),
            P(None, "dp"),
            P("dp", None),
            P(None, "dp"),
            P("dp"),
            P(),
            P(),
            P(),
        ),
        check_vma=False,
    )
```

profile of v0, /device:TPU:0, one launch (start us, length us, event | category | flops | bytes accessed | tf_op | source)
XLA Modules:
  0.0 2069.2 jit_solution(16503356303766443870)
XLA Ops:
  9.0 24.6 %all_gather.34 = bf16[4,256,256]{2,1,0:T(8,128)(2,1)S(1)} all-gather(bf16[4,16,256]{2,1,0:T(8,128)(2,1)S(1)} %convert_element_type.342), channel_id=1, replica_groups=mesh['dp'=16,'grp'=2] {'dp'}, dimensions={1}, use_global_device_ids=true | all-gather | bytes 557056 | tf_op jit(solution)/shard_map/all_gather | solution.py:313
  101.9 19.8 fusion.207
  121.7 20.1 all_gather.35
  167.2 24.2 %reshape_reshape.7 = bf16[65536,48]{1,0:T(8,128)(2,1)} reshape(bf16[4096,768]{1,0:T(8,128)(2,1)} %get-tuple-element.217) | data formatting | bytes 12582912 | tf_op jit(solution)/shard_map/reshape;reshape | solution.py:116
  229.9 28.3 %reshape.425 = f32[32,8,16,1024]{3,2,1,0:T(8,128)} reshape(f32[65536,64]{1,0:T(8,128)} %fusion.214) | data formatting | bytes 33554432 | tf_op jit(solution)/shard_map/reshape | solution.py:117
  272.2 24.2 %reshape.438 = bf16[65536,48]{1,0:T(8,128)(2,1)} reshape(bf16[32,8,16,768]{3,2,1,0:T(8,128)(2,1)} %copy-done) | data formatting | bytes 12582912 | tf_op jit(solution)/shard_map/reshape | solution.py:116
  315.8 28.3 %reshape.440 = f32[32,8,16,1024]{3,2,1,0:T(8,128)} reshape(f32[65536,64]{1,0:T(8,128)} %fusion.221) | data formatting | bytes 33554432 | tf_op jit(solution)/shard_map/reshape | solution.py:117
  380.7 24.2 %reshape_reshape.6 = bf16[65536,48]{1,0:T(8,128)(2,1)} reshape(bf16[4096,768]{1,0:T(8,128)(2,1)} %get-tuple-element.221) | data formatting | bytes 12582912 | tf_op jit(solution)/shard_map/reshape;reshape | solution.py:116
  424.4 28.3 %reshape.417 = f32[32,8,16,1024]{3,2,1,0:T(8,128)} reshape(f32[65536,64]{1,0:T(8,128)} %fusion.212) | data formatting | bytes 33554432 | tf_op jit(solution)/shard_map/reshape | solution.py:117
  466.4 24.6 %reshape.430 = bf16[65536,48]{1,0:T(8,128)(2,1)} reshape(bf16[32,8,16,768]{3,2,1,0:T(8,128)(2,1)} %get-tuple-element.219) | data formatting | bytes 12582912 | tf_op jit(solution)/shard_map/reshape | solution.py:116
  510.4 28.3 %reshape.432 = f32[32,8,16,1024]{3,2,1,0:T(8,128)} reshape(f32[65536,64]{1,0:T(8,128)} %fusion.216) | data formatting | bytes 33554432 | tf_op jit(solution)/shard_map/reshape | solution.py:117
  552.9 43.9 %scatter_custom_fusion = f32[64000]{0:T(1024)} fusion(s32[8192]{0:T(1024)S(1)} %reshape.456, f32[8192]{0:T(1024)S(1)} %broadcast.549, f32[]{:T(128)} %constant.290.clone.1), kind=kCustom, calls=%fused_computation.250 | custom fusion | flops 8192 | bytes 256004 | tf_op jit(solution)/shard_map/scatter-add | solution.py:299
  604.6 28.5 %reshape.424 = f32[4096,1024]{1,0:T(8,128)} reshape(f32[65536,64]{1,0:T(8,128)} %fusion.214) | data formatting | bytes 33554432 | tf_op jit(solution)/shard_map/reshape | solution.py:117
  640.9 28.3 %reshape.439 = f32[4096,1024]{1,0:T(8,128)} reshape(f32[65536,64]{1,0:T(8,128)} %fusion.221) | data formatting | bytes 33554432 | tf_op jit(solution)/shard_map/reshape | solution.py:117
  676.9 28.3 %reshape.416 = f32[4096,1024]{1,0:T(8,128)} reshape(f32[65536,64]{1,0:T(8,128)} %fusion.212) | data formatting | bytes 33554432 | tf_op jit(solution)/shard_map/reshape | solution.py:117
  712.9 28.3 %reshape.431 = f32[4096,1024]{1,0:T(8,128)} reshape(f32[65536,64]{1,0:T(8,128)} %fusion.216) | data formatting | bytes 33554432 | tf_op jit(solution)/shard_map/reshape | solution.py:117
  742.7 29.8 %all-reduce = bf16[256]{0:T(256)(128)(2,1)S(1)} all-reduce(bf16[256]{0:T(256)(128)(2,1)S(1)} %dynamic-update-slice), channel_id=1, replica_groups=mesh['dp'=16,'grp'=2] {'dp'}, use_global_device_ids=true, to_apply=%add | all-reduce | flops 256 | bytes 1024
  1202.9 107.5 %all-reduce.4 = (f32[]{:T(128)}, f32[3]{0:T(128)S(1)}) all-reduce(f32[]{:T(128)} %get-tuple-element.222, f32[3]{0:T(128)S(1)} %maximum_add_fusion.4), channel_id=1, replica_groups=mesh['dp'=16,'grp'=2] {'dp','grp'}, use_global_device_ids=true, to_apply=%region_6.7 | all-reduce | flops 4 | bytes 32 | tf_op jit(solution)/shard_map/psum | solution.py:302
  1337.8 29.0 %fusion.5 = (bf16[4096,1024]{1,0:T(8,128)(2,1)}, bf16[4096,1024]{1,0:T(8,128)(2,1)}) fusion(f32[4096,2048]{1,0:T(8,128)} %fusion.220, bf16[32,8,16,1024]{3,2,1,0:T(8,128)(2,1)} %pad_maximum_fusion.18, f32[4096,1024]{1,0:T(8,128)} %reshape.416, bf16[32,8,16,1024]{3,2,1,0:T(8,128)(2,1)} %pad_maximum_fusion.13, f32[4096,2048]{1,0:T(8,128)} %fusion.68), kind=kLoop, calls=%fused_computation.13 | loop fusion | flops 62914560 | bytes 83886080 | tf_op jit(solution)/shard_map/convert_element_type | solution.py:154
  1366.8 22.1 %reshape.420 = bf16[65536,64]{1,0:T(8,128)(2,1)} reshape(bf16[4096,1024]{1,0:T(8,128)(2,1)} %get-tuple-element.215) | data formatting | bytes 16777216 | tf_op jit(solution)/shard_map/reshape | solution.py:155
  1405.4 27.0 %reshape.421 = f32[4096,768]{1,0:T(8,128)} reshape(f32[65536,48]{1,0:T(8,128)} %fusion.213) | data formatting | bytes 25165824 | tf_op jit(solution)/shard_map/reshape | solution.py:157
  1447.0 29.0 %fusion.1 = (bf16[4096,1024]{1,0:T(8,128)(2,1)}, bf16[4096,1024]{1,0:T(8,128)(2,1)}) fusion(f32[4096,2048]{1,0:T(8,128)} %fusion.225, bf16[32,8,16,1024]{3,2,1,0:T(8,128)(2,1)} %pad_maximum_fusion.21, f32[4096,1024]{1,0:T(8,128)} %reshape.424, bf16[32,8,16,1024]{3,2,1,0:T(8,128)(2,1)} %pad_maximum_fusion.15, f32[4096,2048]{1,0:T(8,128)} %fusion.67), kind=kLoop, calls=%fused_computation.5 | loop fusion | flops 62914560 | bytes 83886080 | tf_op jit(solution)/shard_map/convert_element_type | solution.py:154
  1476.0 22.1 %reshape.428 = bf16[65536,64]{1,0:T(8,128)(2,1)} reshape(bf16[4096,1024]{1,0:T(8,128)(2,1)} %get-tuple-element.213) | data formatting | bytes 16777216 | tf_op jit(solution)/shard_map/reshape | solution.py:155
  1514.8 27.0 %reshape.429 = f32[4096,768]{1,0:T(8,128)} reshape(f32[65536,48]{1,0:T(8,128)} %fusion.215) | data formatting | bytes 25165824 | tf_op jit(solution)/shard_map/reshape | solution.py:157
  1541.8 35.8 %fusion.14 = (bf16[4096,768]{1,0:T(8,128)(2,1)}, bf16[4096,768]{1,0:T(8,128)(2,1)}) fusion(f32[4096,768]{1,0:T(8,128)} %reshape.429, f32[32,8,16,768]{3,2,1,0:T(8,128)} %get-tuple-element.210, f32[4096,768]{1,0:T(8,128)} %get-tuple-element.259, f32[]{:T(128)} %get-tuple-element.174, bf16[32,8,16,768]{3,2,1,0:T(8,128)(2,1)} %copy-done, ...), kind=kLoop, calls=%fused_computation.48 | loop fusion | flops 56623104 | bytes 100663296 | tf_op jit(solution)/shard_map/convert_element_type | solution.py:195
  1736.9 22.1 %reshape.443 = bf16[65536,64]{1,0:T(8,128)(2,1)} reshape(bf16[4096,1024]{1,0:T(8,128)(2,1)} %fusion.3) | data formatting | bytes 16777216 | tf_op jit(solution)/shard_map/reshape | solution.py:155
  1789.5 22.1 %reshape.435 = bf16[65536,64]{1,0:T(8,128)(2,1)} reshape(bf16[4096,1024]{1,0:T(8,128)(2,1)} %fusion.7) | data formatting | bytes 16777216 | tf_op jit(solution)/shard_map/reshape | solution.py:155
  1825.3 22.1 %reshape.437 = bf16[65536,64]{1,0:T(8,128)(2,1)} reshape(bf16[4096,1024]{1,0:T(8,128)(2,1)} %get-tuple-element.214) | data formatting | bytes 16777216 | tf_op jit(solution)/shard_map/reshape | solution.py:155
  1847.5 22.3 %reshape.445 = bf16[65536,64]{1,0:T(8,128)(2,1)} reshape(bf16[4096,1024]{1,0:T(8,128)(2,1)} %get-tuple-element.212) | data formatting | bytes 16777216 | tf_op jit(solution)/shard_map/reshape | solution.py:155
  1915.4 58.5 %all-reduce.5 = (f32[48,64]{1,0:T(8,128)S(1)}, f32[256]{0:T(256)S(1)}) all-reduce(f32[48,64]{1,0:T(8,128)S(1)} %fusion.69, f32[256]{0:T(256)S(1)} %add_add_fusion), channel_id=14, replica_groups=mesh['dp'=16,'grp'=2] {'dp'}, use_global_device_ids=true, to_apply=%region_30.31.clone | all-reduce | flops 3328 | bytes 26624
  1986.1 44.9 %reduce-scatter.11.cloned.1.call-done = f32[4,16,256]{2,1,0:T(8,128)} async-done(((f32[4,256,256]{2,1,0:T(8,128)}), f32[4,16,256]{2,1,0:T(8,128)}) %reduce-scatter.11.cloned.1.call-update) | async-done | bytes 65552 | tf_op jit(solution)/shard_map/reduce_scatter | solution.py:334
  2034.0 21.6 %all-reduce.16.cloned.1.call-done = (f32[2,48,256]{2,1,0:T(8,128)}, f32[4,16,256]{2,1,0:T(8,128)}, f32[128,128]{1,0:T(8,128)}) async-done(((f32[2,48,256]{2,1,0:T(8,128)}, f32[4,16,256]{2,1,0:T(8,128)}, f32[128,128]{1,0:T(8,128)}), (f32[2,48,256]{2,1,0:T(8,128)}, f32[4,16,256]{2,1,0:T(8,128)}, f32[128,128]{1,0:T(8,128)})) %all-reduce.16.cloned.1.call-update) | async-done | bytes 229392 | tf_op jit(solution)/shard_map/psum | solution.py:343
  (653 shorter events, 1067.9 us)
Async XLA Ops:
  8.0 864.9 %all-reduce.12.cloned.1.call-start = ((), (), s32[]{:S(2)}) async-start(), calls=%async_computation.5 | async-start | bytes 516096 | tf_op jit(solution)/shard_map/psum | solution.py:302
  33.6 327.6 %copy-start.64 = (bf16[4,256,256]{2,1,0:T(8,128)(2,1)}, bf16[4,256,256]{2,1,0:T(8,128)(2,1)S(1)}, u32[]{:S(2)}) copy-start(bf16[4,256,256]{2,1,0:T(8,128)(2,1)S(1)} %all_gather.34) | copy-start | bytes 1572868
  53.1 305.7 %copy-start.123 = (bf16[1,256,6]{1,2,0:T(8,128)(2,1)}, bf16[1,256,6]{1,2,0:T(8,128)(2,1)S(1)}, u32[]{:S(2)}) copy-start(bf16[1,256,6]{1,2,0:T(8,128)(2,1)S(1)} %copy.419) | copy-start | bytes 9220
  82.7 276.9 %copy-start.106 = (f32[1,256]{1,0:T(1,128)}, f32[1,256]{1,0:T(1,128)S(1)}, u32[]{:S(2)}) copy-start(f32[1,256]{1,0:T(1,128)S(1)} %get-tuple-element.242) | copy-start | bytes 3076
  141.8 222.0 %copy-start.47 = (bf16[2,768,256]{2,1,0:T(8,128)(2,1)}, bf16[2,768,256]{2,1,0:T(8,128)(2,1)S(1)}, u32[]{:S(2)}) copy-start(bf16[2,768,256]{2,1,0:T(8,128)(2,1)S(1)} %all_gather.35) | copy-start | bytes 2359300
  210.4 280.6 %copy-start.96 = (bf16[16,4,48]{2,1,0:T(4,128)(2,1)}, bf16[16,4,48]{2,1,0:T(4,128)(2,1)S(1)}, u32[]{:S(2)}) copy-start(bf16[16,4,48]{2,1,0:T(4,128)(2,1)S(1)} %all-gather.1) | copy-start | bytes 18436
  270.7 606.8 %collective-permute-start.2 = (bf16[32,16,1024]{2,1,0:T(8,128)(2,1)}, bf16[32,16,1024]{2,1,0:T(8,128)(2,1)}, u32[]{:S(2)}, u32[]{:S(2)}) collective-permute-start(bf16[32,16,1024]{2,1,0:T(8,128)(2,1)} %slice_bitcast_fusion.7), channel_id=1, source_target_pairs={{1,0},{3,2},{5,4},{7,6},{9,8},{11,10},{13,12},{15,14},{17,16},{19,... | collective-permute-start | bytes 3145736 | tf_op jit(solution)/shard_map/ppermute | solution.py:26
  356.7 543.7 %collective-permute-start.7 = (bf16[32,16,1024]{2,1,0:T(8,128)(2,1)}, bf16[32,16,1024]{2,1,0:T(8,128)(2,1)}, u32[]{:S(2)}, u32[]{:S(2)}) collective-permute-start(bf16[32,16,1024]{2,1,0:T(8,128)(2,1)} %slice_bitcast_fusion.2), channel_id=1, source_target_pairs={{1,0},{3,2},{5,4},{7,6},{9,8},{11,10},{13,12},{15,14},{17,16},{19,... | collective-permute-start | bytes 3145736 | tf_op jit(solution)/shard_map/ppermute | solution.py:26
  465.1 458.3 %collective-permute-start = (bf16[32,16,1024]{2,1,0:T(8,128)(2,1)}, bf16[32,16,1024]{2,1,0:T(8,128)(2,1)}, u32[]{:S(2)}, u32[]{:S(2)}) collective-permute-start(bf16[32,16,1024]{2,1,0:T(8,128)(2,1)} %slice_bitcast_fusion.9), channel_id=1, source_target_pairs={{1,0},{3,2},{5,4},{7,6},{9,8},{11,10},{13,12},{15,14},{17,16},{19,... | collective-permute-start | bytes 3145736 | tf_op jit(solution)/shard_map/ppermute | solution.py:26
  551.3 394.4 %collective-permute-start.4 = (bf16[32,16,1024]{2,1,0:T(8,128)(2,1)}, bf16[32,16,1024]{2,1,0:T(8,128)(2,1)}, u32[]{:S(2)}, u32[]{:S(2)}) collective-permute-start(bf16[32,16,1024]{2,1,0:T(8,128)(2,1)} %slice_bitcast_fusion.5), channel_id=1, source_target_pairs={{1,0},{3,2},{5,4},{7,6},{9,8},{11,10},{13,12},{15,14},{17,16},{19,... | collective-permute-start | bytes 3145736 | tf_op jit(solution)/shard_map/ppermute | solution.py:26
  596.8 1377.3 %reduce-scatter.19.cloned.1.call-start = ((), (), s32[]{:S(2)}) async-start(), calls=%async_computation.10 | async-start | bytes 139264
  1155.8 553.7 %collective-permute-start.8 = (bf16[32,16,1024]{2,1,0:T(8,128)(2,1)}, bf16[32,16,1024]{2,1,0:T(8,128)(2,1)}, u32[]{:S(2)}, u32[]{:S(2)}) collective-permute-start(bf16[32,16,1024]{2,1,0:T(8,128)(2,1)} %slice_bitcast_fusion.1), channel_id=1, source_target_pairs={{0,1},{2,3},{4,5},{6,7},{8,9},{10,11},{12,13},{14,15},{16,17},{18,... | collective-permute-start | bytes 3145736 | tf_op jit(solution)/shard_map/ppermute | solution.py:26
  1164.9 598.8 %collective-permute-start.5 = (bf16[32,16,1024]{2,1,0:T(8,128)(2,1)}, bf16[32,16,1024]{2,1,0:T(8,128)(2,1)}, u32[]{:S(2)}, u32[]{:S(2)}) collective-permute-start(bf16[32,16,1024]{2,1,0:T(8,128)(2,1)} %slice_bitcast_fusion.4), channel_id=1, source_target_pairs={{0,1},{2,3},{4,5},{6,7},{8,9},{10,11},{12,13},{14,15},{16,17},{18,... | collective-permute-start | bytes 3145736 | tf_op jit(solution)/shard_map/ppermute | solution.py:26
  1167.2 151.0 %collective-permute-start.1 = (bf16[32,16,1024]{2,1,0:T(8,128)(2,1)}, bf16[32,16,1024]{2,1,0:T(8,128)(2,1)}, u32[]{:S(2)}, u32[]{:S(2)}) collective-permute-start(bf16[32,16,1024]{2,1,0:T(8,128)(2,1)} %slice_bitcast_fusion.8), channel_id=1, source_target_pairs={{0,1},{2,3},{4,5},{6,7},{8,9},{10,11},{12,13},{14,15},{16,17},{18,... | collective-permute-start | bytes 3145736 | tf_op jit(solution)/shard_map/ppermute | solution.py:26
  1169.5 160.9 %collective-permute-start.6 = (bf16[32,16,1024]{2,1,0:T(8,128)(2,1)}, bf16[32,16,1024]{2,1,0:T(8,128)(2,1)}, u32[]{:S(2)}, u32[]{:S(2)}) collective-permute-start(bf16[32,16,1024]{2,1,0:T(8,128)(2,1)} %slice_bitcast_fusion.3), channel_id=1, source_target_pairs={{0,1},{2,3},{4,5},{6,7},{8,9},{10,11},{12,13},{14,15},{16,17},{18,... | collective-permute-start | bytes 3145736 | tf_op jit(solution)/shard_map/ppermute | solution.py:26
  1171.7 260.7 %collective-permute-start.3 = (bf16[32,16,1024]{2,1,0:T(8,128)(2,1)}, bf16[32,16,1024]{2,1,0:T(8,128)(2,1)}, u32[]{:S(2)}, u32[]{:S(2)}) collective-permute-start(bf16[32,16,1024]{2,1,0:T(8,128)(2,1)} %slice_bitcast_fusion.6), channel_id=1, source_target_pairs={{0,1},{2,3},{4,5},{6,7},{8,9},{10,11},{12,13},{14,15},{16,17},{18,... | collective-permute-start | bytes 3145736 | tf_op jit(solution)/shard_map/ppermute | solution.py:26
  1318.2 121.6 %collective-permute-start.9 = (bf16[32,16,1024]{2,1,0:T(8,128)(2,1)}, bf16[32,16,1024]{2,1,0:T(8,128)(2,1)S(1)}, u32[]{:S(2)}, u32[]{:S(2)}) collective-permute-start(bf16[32,16,1024]{2,1,0:T(8,128)(2,1)} %slice_bitcast_fusion), channel_id=1, source_target_pairs={{0,1},{2,3},{4,5},{6,7},{8,9},{10,11},{12,13},{14,15},{16,17},{18,... | collective-permute-start | bytes 3145736 | tf_op jit(solution)/shard_map/ppermute | solution.py:26
  1644.3 330.6 %reduce-scatter.17.cloned.1.call-start = ((), (), s32[]{:S(2)}) async-start(), calls=%async_computation.9 | async-start | bytes 139264
  1645.4 330.4 %reduce-scatter.15.cloned.1.call-start = ((), (), s32[]{:S(2)}) async-start(), calls=%async_computation.8 | async-start | bytes 139264 | tf_op jit(solution)/shard_map/reduce_scatter | solution.py:339
  1649.0 335.5 %all-reduce.14.cloned.1.call-start = ((), (), s32[]{:S(2)}) async-start(), calls=%async_computation.11 | async-start | bytes 3145728
  1681.3 304.8 %reduce-scatter.13.cloned.1.call-start = ((), (), s32[]{:S(2)}) async-start(), calls=%async_computation.7 | async-start | bytes 1114112 | tf_op jit(solution)/shard_map/reduce_scatter | solution.py:338
  1692.1 338.9 %reduce-scatter.11.cloned.1.call-start = ((), (), s32[]{:S(2)}) async-start(), calls=%async_computation.6 | async-start | bytes 1114112 | tf_op jit(solution)/shard_map/reduce_scatter | solution.py:334
  1899.9 155.8 %copy-start.105 = (f32[2,48,256]{2,1,0:T(8,128)S(1)}, f32[2,48,256]{2,1,0:T(8,128)}, u32[]{:S(2)}) copy-start(f32[2,48,256]{2,1,0:T(8,128)} %param.32) | copy-start | bytes 294916
  1899.9 155.8 %copy-start.126 = (f32[2,48,256]{2,1,0:T(8,128)S(1)}, f32[2,48,256]{2,1,0:T(8,128)}, u32[]{:S(2)}) copy-start(f32[2,48,256]{2,1,0:T(8,128)} %param.48) | copy-start | bytes 294916
  1899.9 155.8 %copy-start.127 = (f32[2,48,256]{2,1,0:T(8,128)S(1)}, f32[2,48,256]{2,1,0:T(8,128)}, u32[]{:S(2)}) copy-start(f32[2,48,256]{2,1,0:T(8,128)} %param.40) | copy-start | bytes 294916
  1899.9 157.4 %copy-start.109 = (f32[128,128]{1,0:T(8,128)S(1)}, f32[128,128]{1,0:T(8,128)}, u32[]{:S(2)}) copy-start(f32[128,128]{1,0:T(8,128)} %param.37) | copy-start | bytes 196612
  1899.9 157.4 %copy-start.128 = (f32[128,128]{1,0:T(8,128)S(1)}, f32[128,128]{1,0:T(8,128)}, u32[]{:S(2)}) copy-start(f32[128,128]{1,0:T(8,128)} %param.53) | copy-start | bytes 196612
  1900.0 157.4 %copy-start.129 = (f32[128,128]{1,0:T(8,128)S(1)}, f32[128,128]{1,0:T(8,128)}, u32[]{:S(2)}) copy-start(f32[128,128]{1,0:T(8,128)} %param.45) | copy-start | bytes 196612
  1900.0 158.9 %copy-start.110 = (f32[4,16,256]{2,1,0:T(8,128)S(1)}, f32[4,16,256]{2,1,0:T(8,128)}, u32[]{:S(2)}) copy-start(f32[4,16,256]{2,1,0:T(8,128)} %param.33) | copy-start | bytes 196612
  1900.0 158.9 %copy-start.130 = (f32[4,16,256]{2,1,0:T(8,128)S(1)}, f32[4,16,256]{2,1,0:T(8,128)}, u32[]{:S(2)}) copy-start(f32[4,16,256]{2,1,0:T(8,128)} %param.49) | copy-start | bytes 196612
  1900.0 158.9 %copy-start.131 = (f32[4,16,256]{2,1,0:T(8,128)S(1)}, f32[4,16,256]{2,1,0:T(8,128)}, u32[]{:S(2)}) copy-start(f32[4,16,256]{2,1,0:T(8,128)} %param.41) | copy-start | bytes 196612
  1900.0 155.7 %all-reduce.16.cloned.1.call-start = ((), (), s32[]{:S(2)}) async-start(), calls=%async_computation.12 | async-start | bytes 458752 | tf_op jit(solution)/shard_map/psum | solution.py:343
  (165 other events, 3397.2 us)
Sparse Core Ops, SparseCore 0:
  596.9 127.1 all-reduce.11
Sparse Core Ops, SparseCore 1:
  1644.4 53.1 reduce-scatter.18
  1700.9 54.1 reduce-scatter.16
  1758.4 54.1 reduce-scatter.14
  1816.1 94.4 all-reduce.13
  1914.2 56.2 reduce-scatter.12
  1974.5 56.4 reduce-scatter.10
  2033.9 21.7 all-reduce.15
where the time goes:
time: 2090 us; the launch traced here: 2070 us
  local copies, waits for them, and re-layouts  740 us (35%)
  matrix products  495 us (24%)
  other arithmetic  371 us (18%)
  blocking collectives  341 us (16%)
  waiting for transfers between devices  66.8 us (3%)
  starting transfers between devices  29.1 us (1%)
  between operations  26.2 us (1%)
    reshape x8, local copies, waits for them, and re-layouts, judge_forward(): pre_one = mat_dot(patches, first_conv).reshape(count_rows, -1)  227 us
    dot_general x26, matrix products, dot_trail(): lax.dot_general(operand, other, (((1,), (1,)), ((), ())), preferred_eleme...  181 us
    dot_general x32, matrix products, mat_dot(): return jnp.dot(operand, weights, preferred_element_type=jnp.float32)  168 us
    dot_general x28, matrix products, dot_lead(): lax.dot_general(operand, other, (((0,), (0,)), ((), ())), preferred_eleme...  141 us
    reshape x6, local copies, waits for them, and re-layouts, judge_backward(): grad_small = grad_one.reshape(patches.shape[0], first_conv.shape[1])  133 us
    psum x1, blocking collectives, on_device(): lax.psum((jnp.sum(weight_mask), counts), ('dp', 'grp'))  107 us
    convert_element_type x4, other arithmetic, judge_backward(): ((own_part + moved.astype(jnp.float32)) * silu_slope(pre_one)).astype(jnp...  95.5 us
    unnamed x2, blocking collectives  88.3 us
  transfers between devices with their start and end apart: 18, of which 2 were waited for; matrix products, arithmetic and copies ran while one was open for 57% of the time, Pallas kernels for 0%

commit v1 on v0

v1 whole, which is shorter than its diff:
```python
import jax
import jax.numpy as jnp
import numpy as np
from jax import lax
from jax.experimental import pallas as pl
from jax.experimental.pallas import tpu as pltpu
from jax.sharding import PartitionSpec as P

CODES = 64000
STEP = 10
EPS_NORM = 1e-06
BETA_ONE = 0.9
BETA_TWO = 0.95
ADAM_EPS = 1e-08
DECAY = 0.1
RATE_MATRIX = 0.04
RATE_GAIN = 0.25
GEN_WEIGHT = 0.02
HALVES = (3.5, 3.5, 3.5, 2.0, 2.0, 2.0)
LEVELS = (8, 8, 8, 5, 5, 5)

F32 = jnp.float32
BF16 = jnp.bfloat16
VMEM_LIMIT = 60 * 2**20
MAX_LANES = 512


def nn(left, right):
    return jnp.dot(left, right, preferred_element_type=F32)


def nt(left, right):
    return lax.dot_general(left, right, (((1,), (1,)), ((), ())), preferred_element_type=F32)


def low(value):
    return value.astype(BF16)


def wide(columns, lanes):
    return jnp.concatenate([columns] * (lanes // 128), axis=1)


def fold(value):
    total = value[:, :128]
    for start in range(128, value.shape[1], 128):
        total = total + value[:, start : start + 128]
    return total


def silu_parts(half):
    turned = jnp.tanh(half)
    acted = half + half * turned
    return acted, (1.0 + turned) + (acted - acted * turned)


def norm_parts(stream):
    scaling = lax.rsqrt(jnp.mean(stream * stream, axis=0, keepdims=True) + EPS_NORM)
    return scaling, stream * scaling


def softplus(value):
    return jnp.maximum(value, 0.0) + jnp.log1p(jnp.exp(-jnp.abs(value)))


def block_forward(stream, gain, first_half_t, second_t):
    scaling, normal = norm_parts(stream)
    normed = low(normal * gain)
    acted, slope = silu_parts(nn(first_half_t, normed))
    acted = low(acted)
    return stream + nn(second_t, acted), (scaling, normal, normed, acted, slope)


def block_backward(grad_out, saved, gain, first, second_half, grad_first, grad_second, grad_gain):
    scaling, normal, normed, acted, slope = saved
    grad_low = low(grad_out)
    grad_second[...] += nt(acted, grad_low)
    grad_inside = low(nn(second_half, grad_low) * slope)
    grad_first[...] += nt(normed, grad_inside)
    grad_normed = nn(first, grad_inside)
    along = grad_normed * normal
    grad_gain[...] += fold(along)
    mean = jnp.mean(along * gain, axis=0, keepdims=True)
    return grad_out + scaling * (grad_normed * gain - normal * mean)


def judge_middle(stash_q, fresh_p, wlt_half, wl_half, head_half, head_rows, count_all, active, kind):
    lanes = fresh_p.shape[1]
    acted_two, slope_two = silu_parts(fresh_p[:128] + stash_q)
    acted_two = low(acted_two)
    acted_three, slope_three = silu_parts(nn(wlt_half, acted_two))
    acted_three = low(acted_three)
    score = nn(head_rows, acted_three)[:1]
    shaped = wide(head_half, lanes) * slope_three
    if kind == "real":
        grad_score = -jax.nn.sigmoid(1.0 - score) * (active / count_all)
        grad_three = low(grad_score * shaped)
        grad_two = (low(nn(wl_half, grad_three) * slope_two),)
        losses = (softplus(1.0 - score),)
    else:
        pull = jax.nn.sigmoid(1.0 + score)
        grad_score = pull * (active / count_all)
        grad_three = low(grad_score * shaped)
        grad_three_gen = low((-GEN_WEIGHT / count_all * active) * shaped)
        grad_two_gen = nn(wl_half, grad_three_gen) * slope_two
        grad_two = (low(grad_two_gen * (pull * (-1.0 / GEN_WEIGHT))), low(grad_two_gen))
        losses = (softplus(1.0 + score), -score)
    return acted_two, acted_three, grad_score, grad_three, grad_two, losses


def make_kernel(kind, band, lanes, chunks, count_all):
    frames_in = lanes // 16
    fake = kind == "fake"

    def kernel(*refs):
        refs = list(refs)

        def take(number):
            taken = refs[:number]
            del refs[:number]
            return taken

        places, reals = take(2)
        xa_ref, xb_ref, xbelow_ref, xabove_ref = take(4)
        bdt_ref, wm_ref, wl_ref, headw_ref, headr_ref = take(5)
        if fake:
            codes_ref, lane_ref, consts_ref, spots_ref = take(4)
            proj_ref, blocks_ref, fsq_ref, fsqt_ref, gains_ref, bd_ref = take(6)
            gproj_ref, gblocks_ref, gfsq_ref, ggains_ref = take(4)
        gwm_ref, gwl_ref, gw1_ref, ghead_ref, loss_ref = take(5)
        wmt_s, wmh_s, wlt_s, wlh_s, q_s = take(5)
        kinds = 2 if fake else 1
        g2_s = take(kinds)
        if fake:
            projt_s, blockt_s, blockh_s, gradlow_s = take(4)
            names = ("xt", "fake", "gl1", "act", "slope", "normal", "scaling", "normed", "acted", "bslope", "outlow", "values")
        else:
            names = ("xt", "act", "slope")
        stash_a = dict(zip(names, take(len(names))))
        stash_b = dict(zip(names, take(len(names))))
        chunk, step = pl.program_id(0), pl.program_id(1)
        last_step = band // 2
        row_start, has_below, has_above = places[0], places[1], places[2]
        inv_total = reals[0]
        has_above_f = has_above.astype(F32)

        @pl.when((chunk == 0) & (step == 0))
        def prepare():
            half = jnp.asarray(0.5, BF16)
            for part in range(4):
                rows = pl.ds(part * 256, 256)
                wmh_s[rows, :] = wm_ref[rows, :] * half
                wmt_s[:, rows] = (wm_ref[rows, :] * half).T
            wlt_s[...] = (wl_ref[...] * half).T
            wlh_s[...] = wl_ref[...] * half
            for ref in (gwm_ref, gwl_ref, gw1_ref, ghead_ref, loss_ref):
                ref[...] = jnp.zeros_like(ref)
            if fake:
                projt_s[0] = proj_ref[0].T
                projt_s[1] = proj_ref[1].T
                for number in range(4):
                    scale = jnp.asarray(0.5 if number % 2 == 0 else 1.0, BF16)
                    blockt_s[number] = (blocks_ref[number] * scale).T
                    if number % 2 == 1:
                        blockh_s[number // 2] = blocks_ref[number] * half
                for ref in (gproj_ref, gblocks_ref, gfsq_ref, ggains_ref):
                    ref[...] = jnp.zeros_like(ref)

        def front(row, x, stash, lite=False):
            xt = x.reshape(lanes, 768).T
            if not lite:
                stash["xt"][...] = xt
            if fake:
                consts = consts_ref[...]
                code = codes_ref[pl.ds(row + 1, 1), :]
                turn = jnp.floor((code + 0.5) * wide(consts[0:16], lanes))
                level = wide(consts[16:32], lanes)
                digit = turn - level * jnp.floor((turn + 0.5) * wide(consts[32:48], lanes))
                values = low((digit - wide(consts[48:64], lanes)) * wide(consts[64:80], lanes))
                gain = wide(gains_ref[1], lanes)
                start = nn(fsq_ref[1], values)
                output, saved = block_forward(start, gain, blockt_s[2], blockt_s[3])
                outlow = low(output)
                if not lite:
                    stash["values"][...] = values
                    stash["outlow"][...] = outlow
                    for name, item in zip(("scaling", "normal", "normed", "acted", "bslope"), saved):
                        stash[name][...] = item
                    lane = lax.broadcasted_iota(jnp.int32, (1, lanes), 1)
                    column = (lane % 16).astype(F32)
                    place = (row_start + row).astype(F32)
                    high = lane_ref[0:1, :] - 16.0 * place
                    broad = lane_ref[1:2, :] - 16.0 * column
                    valid = jnp.where(row >= 0, 1.0, 0.0)
                    weight = lane_ref[2:3, :] * valid
                    weight_share = weight * inv_total
                    l1_sum = jnp.zeros((1, lanes), F32)
            parts = []
            for group in range(4):
                rows = pl.ds(group * 192, 192)
                if fake:
                    recon = nn(proj_ref[1, rows, :], outlow)
                    inputs = low(recon)
                    if not lite:
                        stash["fake"][rows, :] = inputs
                        diff = recon - xt[group * 192 : group * 192 + 192].astype(F32)
                        square = diff * diff + 1.0
                        inverse = lax.rsqrt(square)
                        inside = (wide(spots_ref[0, rows, :], lanes) < high) & (
                            wide(spots_ref[1, rows, :], lanes) < broad
                        )
                        l1_sum = l1_sum + jnp.sum(jnp.where(inside, square * inverse, 0.0), axis=0, keepdims=True)
                        stash["gl1"][rows, :] = jnp.where(inside, diff * inverse, 0.0) * weight_share
                else:
                    inputs = xt[group * 192 : group * 192 + 192]
                acted, slope = silu_parts(nn(bdt_ref[...], inputs))
                acted = low(acted)
                wide_rows = pl.ds(group * 256, 256)
                if not lite:
                    stash["act"][wide_rows, :] = acted
                    stash["slope"][wide_rows, :] = slope
                parts.append(acted)
            joined = jnp.concatenate(parts, axis=0)
            if lite:
                q_s[...] = nn(wmt_s[128:256, :], joined)
                return
            fresh = nn(wmt_s[...], joined)
            active = jnp.where(row >= 0, 1.0, has_above_f)
            counted = jnp.where(row >= 0, 1.0, 0.0)
            acted_two, acted_three, grad_score, grad_three, grad_two, losses = judge_middle(
                q_s[...], fresh, wlt_s[...], wlh_s[...], headw_ref[...], headr_ref[...], count_all, active, kind
            )
            q_s[...] = fresh[128:]
            for number, item in enumerate(losses):
                loss_ref[number : number + 1, :] += item * counted
            if fake:
                loss_ref[2:3, :] += l1_sum * weight
            gwl_ref[...] += nt(acted_two * counted.astype(BF16), grad_three)
            ghead_ref[...] += fold(acted_three.astype(F32) * (grad_score * counted))
            for ref, item in zip(g2_s, grad_two):
                ref[128:256, :] = item

        def finish(stash):
            for group in range(4):
                rows, wide_rows = pl.ds(group * 192, 192), pl.ds(group * 256, 256)
                slope = stash["slope"][wide_rows, :]
                small = low(nn(wmh_s[wide_rows, :], g2_s[0][...]) * slope)
                inputs = stash["fake" if fake else "xt"][rows, :]
                gw1_ref[...] += nt(inputs, small)
                gwm_ref[wide_rows, :] += nt(stash["act"][wide_rows, :], g2_s[0][...])
                if fake:
                    small_gen = low(nn(wmh_s[wide_rows, :], g2_s[1][...]) * slope)
                    grad_recon = low(stash["gl1"][rows, :] + nn(bd_ref[...], small_gen))
                    gradlow_s[rows, :] = grad_recon
                    gproj_ref[1, rows, :] += nt(grad_recon, stash["outlow"][...])
            if fake:
                gain = wide(gains_ref[1], lanes)
                saved = tuple(stash[name][...] for name in ("scaling", "normal", "normed", "acted", "bslope"))
                grad_start = block_backward(
                    nn(projt_s[1], gradlow_s[...]), saved, gain, blocks_ref[2], blockh_s[1],
                    gblocks_ref.at[2], gblocks_ref.at[3], ggains_ref.at[1],
                )
                start_low = low(grad_start)
                gfsq_ref[1] += nt(start_low, stash["values"][...])
                grad_values = nn(fsqt_ref[1], start_low)
                gain = wide(gains_ref[0], lanes)
                stream = nn(projt_s[0], stash["xt"][...])
                middle, saved = block_forward(stream, gain, blockt_s[0], blockt_s[1])
                middle_low = low(middle)
                tangent = jnp.tanh(nn(fsqt_ref[0], middle_low))
                grad_latent = low(grad_values * (1.0 - tangent * tangent))
                gfsq_ref[0] += nt(middle_low, grad_latent)
                grad_stream = block_backward(
                    nn(fsq_ref[0], grad_latent), saved, gain, blocks_ref[0], blockh_s[0],
                    gblocks_ref.at[0], gblocks_ref.at[1], ggains_ref.at[0],
                )
                gproj_ref[0] += nt(stash["xt"][...], low(grad_stream))
            for ref in g2_s:
                ref[0:128, :] = ref[128:256, :]

        @pl.when((step == 0) & (has_below > 0))
        def below():
            front(jnp.int32(band), xbelow_ref[...], None, lite=True)

        @pl.when((step == 0) & (has_below == 0))
        def edge():
            q_s[...] = jnp.zeros_like(q_s)

        @pl.when(step == 0)
        def first():
            front(jnp.int32(band - 1), xa_ref[...], stash_a)
            for ref in g2_s:
                ref[0:128, :] = ref[128:256, :]

        @pl.when(step > 0)
        def main():
            front(band - 2 * step, xa_ref[...], stash_b)
            finish(stash_a)
            x = jnp.where(step == last_step, xabove_ref[...], xb_ref[...].reshape(frames_in, 16, 768))
            front(band - 2 * step - 1, x, stash_a)
            finish(stash_b)

    return kernel


def run_kernel(kind, pixels, halos, places, reals, judge, extra, weights, count_all):
    frames, band = pixels.shape[:2]
    lanes = min(MAX_LANES, frames * 16)
    chunks = frames * 16 // lanes
    frames_in = lanes // 16
    fake = kind == "fake"
    smem = pl.BlockSpec(memory_space=pltpu.SMEM)

    def whole(array):
        return pl.BlockSpec(array.shape, lambda c, s: (0,) * array.ndim)

    def row_spec(first):
        if first:
            return lambda c, s: (c, jnp.where(s == 0, band - 1, band - 2 * s), 0, 0)
        return lambda c, s: (c, jnp.maximum(band - 1 - 2 * s, 0), 0, 0)

    block = (frames_in, 1, 16, 768)
    halo_spec = pl.BlockSpec((frames_in, 16, 768), lambda c, s: (c, 0, 0))
    operands = [places, reals, pixels, pixels, *halos, *judge]
    specs = [smem, smem, pl.BlockSpec(block, row_spec(True)), pl.BlockSpec(block, row_spec(False)), halo_spec, halo_spec]
    specs += [whole(item) for item in judge]
    if fake:
        codes, lane_info, consts, spots = extra
        operands += [codes, lane_info, consts, spots, *weights]
        specs += [
            pl.BlockSpec((codes.shape[0], lanes), lambda c, s: (0, c)),
            pl.BlockSpec((lane_info.shape[0], lanes), lambda c, s: (0, c)),
            whole(consts),
            whole(spots),
        ]
        specs += [whole(item) for item in weights]
    outs = []
    if fake:
        outs += [(2, 768, 256), (4, 256, 256), (2, 256, 16), (2, 256, 128)]
    outs += [(1024, 256), (128, 256), (192, 256), (256, 128), (8, lanes)]
    outs = [jax.ShapeDtypeStruct(shape, F32) for shape in outs]
    scratch = [
        pltpu.VMEM((256, 1024), BF16),
        pltpu.VMEM((1024, 256), BF16),
        pltpu.VMEM((256, 128), BF16),
        pltpu.VMEM((128, 256), BF16),
        pltpu.VMEM((128, lanes), F32),
    ]
    scratch += [pltpu.VMEM((256, lanes), BF16)] * (2 if fake else 1)
    if fake:
        scratch += [
            pltpu.VMEM((2, 256, 768), BF16),
            pltpu.VMEM((4, 256, 256), BF16),
            pltpu.VMEM((2, 256, 256), BF16),
            pltpu.VMEM((768, lanes), BF16),
        ]
        stash = [
            ((768, lanes), BF16),
            ((768, lanes), BF16),
            ((768, lanes), F32),
            ((1024, lanes), BF16),
            ((1024, lanes), F32),
            ((256, lanes), F32),
            ((1, lanes), F32),
            ((256, lanes), BF16),
            ((256, lanes), BF16),
            ((256, lanes), F32),
            ((256, lanes), BF16),
            ((16, lanes), BF16),
        ]
    else:
        stash = [((768, lanes), BF16), ((1024, lanes), BF16), ((1024, lanes), F32)]
    scratch += [pltpu.VMEM(*item) for item in stash] * 2
    return pl.pallas_call(
        make_kernel(kind, band, lanes, chunks, count_all),
        grid=(chunks, band // 2 + 1),
        in_specs=specs,
        out_specs=[pl.BlockSpec(item.shape, lambda c, s, n=len(item.shape): (0,) * n) for item in outs],
        out_shape=outs,
        scratch_shapes=scratch,
        compiler_params=pltpu.CompilerParams(
            vmem_limit_bytes=VMEM_LIMIT, dimension_semantics=("arbitrary", "arbitrary")
        ),
        name="judge_" + kind,
    )(*operands)


def count_kernel(codes_ref, counts_ref):
    @pl.when(pl.program_id(0) == 0)
    def clear():
        counts_ref[...] = jnp.zeros_like(counts_ref)

    code = codes_ref[0]
    upper = jnp.floor(code * (1.0 / 256.0))
    lower = code - 256.0 * upper
    bins = lax.broadcasted_iota(jnp.int32, (256, code.shape[1]), 0).astype(F32)
    one, zero = jnp.asarray(1.0, F32), jnp.asarray(0.0, F32)
    counts_ref[...] += nt(low(jnp.where(bins == upper, one, zero)), low(jnp.where(bins == lower, one, zero)))


def count_codes(codes):
    parts = codes.size // 1024
    return pl.pallas_call(
        count_kernel,
        grid=(parts,),
        in_specs=[pl.BlockSpec((1, 1, 1024), lambda s: (s, 0, 0))],
        out_specs=pl.BlockSpec((256, 256), lambda s: (0, 0)),
        out_shape=jax.ShapeDtypeStruct((256, 256), F32),
        name="count",
    )(codes.astype(F32).reshape(parts, 1, 1024))


def passed_along(x, axis, by):
    size = lax.axis_size(axis)
    pairs = [(i, i + by) for i in range(size) if 0 <= i + by < size]
    return lax.ppermute(x, axis, pairs)


def frame_weights(bounds, clip_frames, first_frame):
    clip_ends = jnp.cumsum(clip_frames)
    frame_index = first_frame + jnp.arange(bounds.shape[0], dtype=jnp.int32)
    clip_of = jnp.sum((clip_ends[None, :] <= frame_index[:, None]).astype(jnp.int32), axis=1)
    picked = jnp.sum(
        jnp.where(
            clip_of[:, None] == jnp.arange(clip_frames.shape[0], dtype=jnp.int32)[None, :],
            clip_frames[None, :],
            0,
        ),
        axis=1,
    )
    return 1.0 / picked.astype(F32)


def adamw(master, moment, square, grad, rate, decay):
    new_moment = BETA_ONE * moment + (1.0 - BETA_ONE) * grad
    new_square = BETA_TWO * square + (1.0 - BETA_TWO) * grad * grad
    update = (
        new_moment
        / (1.0 - BETA_ONE**STEP)
        / (jnp.sqrt(new_square / (1.0 - BETA_TWO**STEP)) + ADAM_EPS)
    )
    return (new_moment, new_square, master - rate * (update + decay * master))


def constants():
    products = np.cumprod((1,) + LEVELS)[:6]
    rows = np.zeros((5, 16), np.float32)
    rows[1] = 1.0
    rows[2] = 1.0
    rows[0, :6] = 1.0 / products
    rows[1, :6] = LEVELS
    rows[2, :6] = 1.0 / np.array(LEVELS)
    rows[3, :6] = HALVES
    rows[4, :6] = 1.0 / np.array(HALVES)
    consts = np.broadcast_to(rows.reshape(80, 1), (80, 128)).astype(np.float32)
    places = np.arange(768)
    down = places // 48 // 4 * 4 + places % 48 // 12
    across = places // 48 % 4 * 4 + places % 48 % 12 // 3
    spots = np.broadcast_to(np.stack([down, across])[:, :, None], (2, 768, 128)).astype(np.float32)
    return jnp.asarray(consts), jnp.asarray(spots)


def on_device(pixels, frame_bounds, clip_frames, codes, *states):
    masters, moments, squares = states[:8], states[8:16], states[16:24]
    frames, band = pixels.shape[:2]
    grp, bands = lax.axis_index("grp"), lax.axis_size("grp")
    parts = lax.axis_size("dp")
    count_all = float(frames * parts * 256)
    halos = (passed_along(pixels[:, 0], "grp", -1), passed_along(pixels[:, band - 1], "grp", 1))
    code_halos = (passed_along(codes[:, 0], "grp", -1), passed_along(codes[:, band - 1], "grp", 1))
    weighting = frame_weights(frame_bounds, clip_frames, lax.axis_index("dp") * frames)
    own_total = jnp.sum(
        weighting * (3 * frame_bounds[:, 0] * frame_bounds[:, 1]).astype(F32)
    )
    total_weight = lax.psum(own_total, "dp")
    counts = lax.psum(count_codes(codes), ("dp", "grp"))

    shards = [low(weight) for weight in masters]
    axes = (1, 1, 1, 1, 1, 0, 1, 0)
    project, matrices, fsq_pair, gain_pair, first_conv, mid_conv, last_conv, head_map = (
        lax.all_gather(shard, "dp", axis=axis, tiled=True) for shard, axis in zip(shards, axes)
    )
    half = jnp.asarray(0.5, BF16)
    eye = jnp.eye(4, dtype=BF16)
    bd = jnp.kron(eye, first_conv)
    bdt = bd.T * half
    wm = jnp.concatenate([mid_conv[:1024], mid_conv[1024:]], axis=1)
    headw = jnp.broadcast_to(head_map.astype(F32)[:, None] * 0.5, (256, 128))
    headr = jnp.concatenate([head_map[None, :], jnp.zeros((15, 256), BF16)], axis=0)
    judge = (bdt, wm, last_conv, headw, headr)
    fsq = jnp.pad(fsq_pair, ((0, 0), (0, 0), (0, 10)))
    fsqt = fsq.transpose(0, 2, 1)
    gains = jnp.broadcast_to(gain_pair.astype(F32)[:, :, None], (2, 256, 128))
    weights = (project, matrices, fsq, fsqt, gains, bd)

    places = jnp.stack([grp * band, (grp < bands - 1).astype(jnp.int32), (grp > 0).astype(jnp.int32)]).astype(jnp.int32)
    reals = jnp.stack([1.0 / total_weight, total_weight])
    all_codes = jnp.concatenate([code_halos[1][:, None], codes, code_halos[0][:, None]], axis=1)
    code_rows = all_codes.transpose(1, 0, 2).reshape(band + 2, frames * 16).astype(F32)
    lane_info = jnp.repeat(
        jnp.stack([frame_bounds[:, 0].astype(F32), frame_bounds[:, 1].astype(F32), weighting] + [weighting] * 5), 16, axis=1
    )
    consts, spots = constants()
    extra = (code_rows, lane_info, consts, spots)

    fake_outs = run_kernel("fake", pixels, halos, places, reals, judge, extra, weights, count_all)
    real_outs = run_kernel("real", pixels, halos, places, reals, judge, None, None, count_all)
    gproj, gblocks, gfsq, ggains = fake_outs[:4]
    gwm, gwl, gw1, ghead = (left + right for left, right in zip(fake_outs[4:8], real_outs[:4]))
    first_grad = sum(gw1[48 * n : 48 * n + 48, 64 * n : 64 * n + 64] for n in range(4))
    grads = (
        gproj,
        gblocks,
        gfsq[:, :, :6],
        jnp.sum(ggains, axis=-1),
        first_grad,
        jnp.concatenate([gwm[:, :128], gwm[:, 128:]], axis=0),
        gwl,
        jnp.sum(ghead, axis=-1),
    )
    losses = jnp.stack(
        [jnp.sum(fake_outs[8][2]), jnp.sum(fake_outs[8][1]), jnp.sum(fake_outs[8][0]) + jnp.sum(real_outs[4][0])]
    )
    pieces = []
    for grad, axis in zip(grads, axes):
        shape = grad.shape
        split = grad.reshape(shape[:axis] + (parts, shape[axis] // parts) + shape[axis + 1 :])
        pieces.append(jnp.moveaxis(split, axis, 0).reshape(parts, -1))
    sizes = [piece.shape[1] for piece in pieces]
    packed = jnp.concatenate(pieces, axis=1)
    padding = -packed.shape[1] % 1024
    packed = jnp.pad(packed, ((0, 0), (0, padding)))
    summed = lax.psum_scatter(packed, "dp", scatter_dimension=0, tiled=True)
    summed = lax.psum(summed, "grp").reshape(-1)
    totals, place = [], 0
    for master, size in zip(masters, sizes):
        totals.append(summed[place : place + size].reshape(master.shape))
        place += size
    losses = lax.psum(losses, ("dp", "grp"))
    results = [
        adamw(
            masters[number],
            moments[number],
            squares[number],
            totals[number],
            RATE_GAIN if number == 3 else RATE_MATRIX,
            0.0 if number == 3 else DECAY,
        )
        for number in range(8)
    ]
    shares_all = counts / jnp.sum(counts)
    perplexity = jnp.exp(-jnp.sum(jax.scipy.special.xlogy(shares_all, shares_all)))
    loss_terms = jnp.stack([losses[0], total_weight])
    adversarial_sums = jnp.stack([losses[1], losses[2]])
    return (
        *(result[0] for result in results),
        *(result[1] for result in results),
        *(result[2] for result in results),
        loss_terms,
        adversarial_sums,
        perplexity,
    )


def solution(mesh):
    states = (
        P(None, "dp", None),
        P(None, "dp", None),
        P(None, "dp", None),
        P(None, "dp"),
        P(None, "dp"),
        P("dp", None),
        P(None, "dp"),
        P("dp"),
    )
    return jax.shard_map(
        on_device,
        mesh=mesh,
        in_specs=(P("dp", "grp", None, None), P("dp", None), P(), P("dp", "grp", None)) + states * 3,
        out_specs=states * 3 + (P(), P(), P()),
        check_vma=False,
    )
```

time: 2090 us -> 689 us (0.33)
  local copies, waits for them, and re-layouts: 740 us -> 58.9 us
  matrix products: 495 us -> 0 us
  other arithmetic: 371 us -> 33 us
  Pallas kernels: 0 us -> 218 us
  blocking collectives: 341 us -> 237 us
  waiting for transfers between devices: 66.8 us -> 101 us
    dot_general x90 -> x0, matrix products: 495 us -> none  [the longest x26 181 us: dot_trail(): lax.dot_general(operand, other, (((1,), (1,)), ((), ())), preferred_eleme...]
    reshape x18, local copies, waits for them, and re-layouts: 462 us -> 3.36 us  [the longest x5 0.84 us: on_device(): pieces.append(jnp.moveaxis(split, axis, 0).reshape(parts, -1))]
    pallas_call x0 -> x3, Pallas kernels: none -> 218 us  [the longest x2 212 us: run_kernel(): pl.pallas_call(make_kernel(kind, band, lanes, chunks, count_all), grid=(c...]
    convert_element_type x22 -> x11, other arithmetic: 215 us -> 5.19 us  [the longest x6 2.07 us: low(): return value.astype(BF16)]
    slice x21 -> x8, local copies, waits for them, and re-layouts: 129 us -> 5.58 us  [the longest x5 4.68 us: on_device(): totals.append(summed[place:place + size].reshape(master.shape))]
    unnamed x11 -> x4, waiting for transfers between devices: 0.16 us -> 101 us
    concatenate x10 -> x2, other arithmetic: 74 us -> 2.84 us  [the longest x1 1.8 us: on_device(): wm = jnp.concatenate([mid_conv[:1024], mid_conv[1024:]], axis=1)]
    unnamed x2 -> x1, blocking collectives: 88.3 us -> 32.7 us
  transfers between devices with their start and end apart: 18 -> 7, of which waited for: 2 -> 1; matrix products, arithmetic and copies ran while one was open for 57% -> 11% of each run, Pallas kernels for 0% -> 32%
where the time goes in v1:
time: 689 us; the launch traced here: 680 us
  blocking collectives  237 us (34%)
  Pallas kernels  218 us (32%)
  waiting for transfers between devices  101 us (15%)
  local copies, waits for them, and re-layouts  58.9 us (9%)
  other arithmetic  33 us (5%)
  between operations  19.2 us (3%)
  starting transfers between devices  13.7 us (2%)
    pallas_call x2, Pallas kernels, run_kernel(): pl.pallas_call(make_kernel(kind, band, lanes, chunks, count_all), grid=(c...  212 us
    all_gather x7, blocking collectives, on_device(): lax.all_gather(shard, 'dp', axis=axis, tiled=True)  135 us
    unnamed x4, waiting for transfers between devices  101 us
    psum x1, blocking collectives, on_device(): losses = lax.psum(losses, ('dp', 'grp'))  39.5 us
    unnamed x1, blocking collectives  32.7 us
    psum x1, blocking collectives, on_device(): total_weight = lax.psum(own_total, 'dp')  30.1 us
    unnamed x113, local copies, waits for them, and re-layouts  23.6 us
  transfers between devices with their start and end apart: 7, of which 1 were waited for; matrix products, arithmetic and copies ran while one was open for 11% of the time, Pallas kernels for 32%

profile of v1, /device:TPU:0, one launch (start us, length us, event | category | flops | bytes accessed | tf_op | source)
XLA Modules:
  0.0 680.3 jit_solution(12350592527492910678)
XLA Ops:
  8.6 5.6 collective-permute-start.2
  17.4 5.3 count.1
  22.8 3.8 slice_bitcast_fusion
  26.5 5.2 collective-permute-start.1
  35.1 32.7 %all-reduce.3 = bf16[256]{0:T(256)(128)(2,1)S(1)} all-reduce(bf16[256]{0:T(256)(128)(2,1)S(1)} %dynamic-update-slice), channel_id=1, replica_groups=mesh['dp'=16,'grp'=2] {'dp'}, use_global_device_ids=true, to_apply=%add.3 | all-reduce | flops 256 | bytes 1024
  69.9 30.1 %psum.28 = f32[]{:T(128)} all-reduce(f32[]{:T(128)} %get-tuple-element.219), channel_id=1, replica_groups=mesh['dp'=16,'grp'=2] {'dp'}, use_global_device_ids=true, to_apply=%region_5.6 | all-reduce | flops 1 | bytes 8 | tf_op jit(solution)/shard_map/psum | solution.py:475
  100.7 17.1 %all-gather = bf16[16,4,48]{2,1,0:T(4,128)(2,1)S(1)} all-gather(bf16[1,4,48]{2,1,0:T(4,128)(2,1)S(1)} %convert_bitcast_fusion), channel_id=1, replica_groups=mesh['dp'=16,'grp'=2] {'dp'}, dimensions={0}, use_global_device_ids=true | all-gather | bytes 6528 | tf_op jit(solution)/shard_map/all_gather | solution.py:481
  118.0 19.4 %all_gather.30 = bf16[2,256,6]{2,0,1:T(2,128)(2,1)S(1)} all-gather(bf16[2,16,6]{2,0,1:T(2,128)(2,1)S(1)} %copy.283), channel_id=1, replica_groups=mesh['dp'=16,'grp'=2] {'dp'}, dimensions={1}, use_global_device_ids=true | all-gather | bytes 6528 | tf_op jit(solution)/shard_map/all_gather | solution.py:481
  138.1 18.9 %all_gather.25 = bf16[2048,128]{1,0:T(8,128)(2,1)S(1)} all-gather(bf16[128,128]{1,0:T(8,128)(2,1)S(1)} %convert_element_type.105), channel_id=1, replica_groups=mesh['dp'=16,'grp'=2] {'dp'}, dimensions={0}, use_global_device_ids=true | all-gather | bytes 557056 | tf_op jit(solution)/shard_map/all_gather | solution.py:481
  165.1 18.9 %all-gather.1 = bf16[16,16,2]{1,2,0:T(2,128)(2,1)S(1)} all-gather(bf16[1,16,2]{1,2,0:T(2,128)(2,1)} %convert_bitcast_fusion.1), channel_id=1, replica_groups=mesh['dp'=16,'grp'=2] {'dp'}, dimensions={0}, use_global_device_ids=true | all-gather | bytes 1088 | tf_op jit(solution)/shard_map/all_gather | solution.py:481
  184.0 1.8 pad_maximum_fusion.1.refs_7_
  186.6 1.6 multiply_bitcast_fusion.refs_6_
  188.1 20.5 %all_gather.29.refs_16_ = bf16[4,256,256]{2,1,0:T(8,128)(2,1)} all-gather(bf16[4,16,256]{2,1,0:T(8,128)(2,1)} %convert_element_type.117), channel_id=1, replica_groups=mesh['dp'=16,'grp'=2] {'dp'}, dimensions={1}, use_global_device_ids=true | all-gather | bytes 557056 | tf_op jit(solution)/shard_map/all_gather | solution.py:481
  208.6 22.4 %all_gather.28.refs_15_ = bf16[2,768,256]{2,1,0:T(8,128)(2,1)} all-gather(bf16[2,48,256]{2,1,0:T(8,128)(2,1)S(1)} %convert_element_type.116), channel_id=1, replica_groups=mesh['dp'=16,'grp'=2] {'dp'}, dimensions={1}, use_global_device_ids=true | all-gather | bytes 835584 | tf_op jit(solution)/shard_map/all_gather | solution.py:481
  231.0 17.9 %all_gather.26 = bf16[128,256]{0,1:T(8,128)(2,1)S(1)} all-gather(bf16[128,16]{0,1:T(8,128)(2,1)} %convert_element_type.106), channel_id=1, replica_groups=mesh['dp'=16,'grp'=2] {'dp'}, dimensions={1}, use_global_device_ids=true | all-gather | bytes 69632 | tf_op jit(solution)/shard_map/all_gather | solution.py:481
  254.3 1.5 fusion.3
  257.7 1.7 broadcast_in_dim.48.refs_9_
  260.2 161.5 %judge_fake.1 = (f32[2,768,256]{2,1,0:T(8,128)}, f32[4,256,256]{2,1,0:T(8,128)}, f32[2,256,16]{2,1,0:T(8,128)}, f32[2,256,128]{2,1,0:T(8,128)}, f32[1024,256]{1,...) custom-call(s32[3]{0:T(128)} %pad_add_fusion.refs_0_, ...), custom_call_target="tpu_custom_call" | custom-call | tf_op jit(solution)/shard_map/judge_fake/pallas_call | solution.py:374
  421.8 1.6 copy.288
  424.4 1.6 copy.317
  426.1 50.8 %judge_real.1 = (f32[1024,256]{1,0:T(8,128)}, f32[128,256]{1,0:T(8,128)}, f32[192,256]{1,0:T(8,128)}, f32[256,128]{1,0:T(8,128)}, f32[8,512]{1,0:T(8,128)}) custom-call(s32[3]{0:T(128)} %pad_add_fusion.refs_0_, f32[2]{0:T(128)} %pad_maximum_fusion.2.refs_1_, bf16[64,8,16,768]{3,2,1,0:T(8,128)(2,1)} %refs_3_.3, bf16[64,8,16,768]{3,2,1,0:T(8,128)(2,1)} %refs_3_.3, ...), custom_call_target="tpu_custom_call" | custom-call | tf_op jit(solution)/shard_map/judge_real/pallas_call | solution.py:374
  480.4 1.5 reshape_reshape.3
  491.2 1.5 dynamic-update-slice.5
  492.7 4.9 dynamic-update-slice.6
  497.6 1.8 dynamic-update-slice.7
  499.4 1.6 dynamic-update-slice.8
  500.9 4.2 pad.10
  506.1 1.6 reduce_sum.108
  507.7 2.3 fusion.1
  510.7 100.6 %all-reduce.13.cloned.1.call-done = f32[16,60416]{1,0:T(8,128)} async-done(((f32[16,60416]{1,0:T(8,128)}), f32[16,60416]{1,0:T(8,128)}) %all-reduce.13.cloned.1.call-update) | async-done | bytes 3866640
  611.3 3.1 constant_dynamic-slice_fusion
  618.6 39.5 %psum.30 = f32[3]{0:T(128)S(1)} all-reduce(f32[3]{0:T(128)S(1)} %pad_maximum_fusion.3), channel_id=1, replica_groups=mesh['dp'=16,'grp'=2] {'dp','grp'}, use_global_device_ids=true, to_apply=%region_14.15 | all-reduce | flops 3 | bytes 24 | tf_op jit(solution)/shard_map/psum | solution.py:539
  (214 shorter events, 58.9 us)
Async XLA Ops:
  7.2 498.9 %all-reduce.11.cloned.1.call-start = ((), (), s32[]{:S(2)}) async-start(), calls=%async_computation.1 | async-start | bytes 524288 | tf_op jit(solution)/shard_map/psum | solution.py:476
  8.6 245.8 %collective-permute-start.2 = (s32[64,16]{0,1:T(8,128)}, s32[64,16]{0,1:T(8,128)}, u32[]{:S(2)}, u32[]{:S(2)}) collective-permute-start(s32[64,16]{0,1:T(8,128)} %get-tuple-element.229), channel_id=1, source_target_pairs={{0,1},{2,3},{4,5},{6,7},{8,9},{10,11},{12,13},{14,15},{16,17},{18,... | collective-permute-start | bytes 12296 | tf_op jit(solution)/shard_map/ppermute | solution.py:416
  14.2 240.2 %collective-permute-start.3 = (s32[64,16]{0,1:T(8,128)}, s32[64,16]{0,1:T(8,128)}, u32[]{:S(2)}, u32[]{:S(2)}) collective-permute-start(s32[64,16]{0,1:T(8,128)} %get-tuple-element.230), channel_id=1, source_target_pairs={{1,0},{3,2},{5,4},{7,6},{9,8},{11,10},{13,12},{15,14},{17,16},{19,... | collective-permute-start | bytes 12296 | tf_op jit(solution)/shard_map/ppermute | solution.py:416
  16.5 101.5 %copy-start.9 = (f32[128,128]{1,0:T(8,128)S(1)}, f32[128,128]{1,0:T(8,128)}, u32[]{:S(2)}) copy-start(f32[128,128]{1,0:T(8,128)} %param.39) | copy-start | bytes 196612
  22.7 138.4 %copy-start.22 = (f32[128,16]{0,1:T(8,128)S(1)}, f32[128,16]{0,1:T(8,128)}, u32[]{:S(2)}) copy-start(f32[128,16]{0,1:T(8,128)} %param.40) | copy-start | bytes 24580
  22.7 140.5 %copy-start.6 = (f32[2,48,256]{2,1,0:T(8,128)S(1)}, f32[2,48,256]{2,1,0:T(8,128)}, u32[]{:S(2)}) copy-start(f32[2,48,256]{2,1,0:T(8,128)} %param.34) | copy-start | bytes 294916
  22.7 588.6 %all-reduce.13.cloned.1.call-start = ((), (), s32[]{:S(2)}) async-start(), calls=%async_computation.2 | async-start | bytes 7733248
  26.5 231.2 %collective-permute-start.1 = (bf16[64,16,768]{2,1,0:T(8,128)(2,1)}, bf16[64,16,768]{2,1,0:T(8,128)(2,1)S(1)}, u32[]{:S(2)}, u32[]{:S(2)}) collective-permute-start(bf16[64,16,768]{2,1,0:T(8,128)(2,1)} %get-tuple-element.221), channel_id=1, source_target_pairs={{0,1},{2,3},{4,5},{6,7},{8,9},{10,11},{12,13},{14,15},{16,17},{18,... | collective-permute-start | bytes 4718600 | tf_op jit(solution)/shard_map/ppermute | solution.py:416
  31.8 225.9 %collective-permute-start = (bf16[64,16,768]{2,1,0:T(8,128)(2,1)}, bf16[64,16,768]{2,1,0:T(8,128)(2,1)S(1)}, u32[]{:S(2)}, u32[]{:S(2)}) collective-permute-start(bf16[64,16,768]{2,1,0:T(8,128)(2,1)} %get-tuple-element.222), channel_id=1, source_target_pairs={{1,0},{3,2},{5,4},{7,6},{9,8},{11,10},{13,12},{15,14},{17,16},{19,... | collective-permute-start | bytes 4718600 | tf_op jit(solution)/shard_map/ppermute | solution.py:416
  164.3 90.0 %copy-start.5 = (bf16[192,256]{1,0:T(8,128)(2,1)}, bf16[192,256]{1,0:T(8,128)(2,1)S(1)}, u32[]{:S(2)}) copy-start(bf16[192,256]{1,0:T(8,128)(2,1)S(1)} %mul.331.refs_20_) | copy-start | bytes 294916
  505.2 162.0 %copy-start.38 = (f32[2,16]{1,0:T(2,128)S(1)}, f32[2,16]{1,0:T(2,128)}, u32[]{:S(2)}) copy-start(f32[2,16]{1,0:T(2,128)} %param.37) | copy-start | bytes 388
  505.2 162.0 %copy-start.39 = (f32[2,16]{1,0:T(2,128)S(1)}, f32[2,16]{1,0:T(2,128)}, u32[]{:S(2)}) copy-start(f32[2,16]{1,0:T(2,128)} %param.53) | copy-start | bytes 388
  505.2 162.0 %copy-start.40 = (f32[2,16]{1,0:T(2,128)S(1)}, f32[2,16]{1,0:T(2,128)}, u32[]{:S(2)}) copy-start(f32[2,16]{1,0:T(2,128)} %param.45) | copy-start | bytes 388
  505.2 162.6 %copy-start.29 = (f32[48,4]{0,1:T(4,128)S(1)}, f32[48,4]{0,1:T(4,128)}, u32[]{:S(2)}) copy-start(f32[48,4]{0,1:T(4,128)} %param.38) | copy-start | bytes 2308
  505.2 162.6 %copy-start.34 = (f32[48,4]{0,1:T(4,128)S(1)}, f32[48,4]{0,1:T(4,128)}, u32[]{:S(2)}) copy-start(f32[48,4]{0,1:T(4,128)} %param.54) | copy-start | bytes 2308
  505.2 162.6 %copy-start.35 = (f32[48,4]{0,1:T(4,128)S(1)}, f32[48,4]{0,1:T(4,128)}, u32[]{:S(2)}) copy-start(f32[48,4]{0,1:T(4,128)} %param.46) | copy-start | bytes 2308
  505.2 163.2 %copy-start.23 = (f32[128,16]{0,1:T(8,128)S(1)}, f32[128,16]{0,1:T(8,128)}, u32[]{:S(2)}) copy-start(f32[128,16]{0,1:T(8,128)} %param.40) | copy-start | bytes 24580
  505.2 163.2 %copy-start.26 = (f32[128,16]{0,1:T(8,128)S(1)}, f32[128,16]{0,1:T(8,128)}, u32[]{:S(2)}) copy-start(f32[128,16]{0,1:T(8,128)} %param.56) | copy-start | bytes 24580
  505.2 163.2 %copy-start.27 = (f32[128,16]{0,1:T(8,128)S(1)}, f32[128,16]{0,1:T(8,128)}, u32[]{:S(2)}) copy-start(f32[128,16]{0,1:T(8,128)} %param.48) | copy-start | bytes 24580
  505.3 163.8 %copy-start.8 = (f32[4,16,256]{2,1,0:T(8,128)S(1)}, f32[4,16,256]{2,1,0:T(8,128)}, u32[]{:S(2)}) copy-start(f32[4,16,256]{2,1,0:T(8,128)} %param.35) | copy-start | bytes 196612
  505.3 163.8 %copy-start.18 = (f32[4,16,256]{2,1,0:T(8,128)S(1)}, f32[4,16,256]{2,1,0:T(8,128)}, u32[]{:S(2)}) copy-start(f32[4,16,256]{2,1,0:T(8,128)} %param.51) | copy-start | bytes 196612
  505.3 163.8 %copy-start.19 = (f32[4,16,256]{2,1,0:T(8,128)S(1)}, f32[4,16,256]{2,1,0:T(8,128)}, u32[]{:S(2)}) copy-start(f32[4,16,256]{2,1,0:T(8,128)} %param.43) | copy-start | bytes 196612
  505.3 164.5 %copy-start.10 = (f32[128,128]{1,0:T(8,128)S(1)}, f32[128,128]{1,0:T(8,128)}, u32[]{:S(2)}) copy-start(f32[128,128]{1,0:T(8,128)} %param.39) | copy-start | bytes 196612
  505.3 164.5 %copy-start.20 = (f32[128,128]{1,0:T(8,128)S(1)}, f32[128,128]{1,0:T(8,128)}, u32[]{:S(2)}) copy-start(f32[128,128]{1,0:T(8,128)} %param.55) | copy-start | bytes 196612
  505.3 164.5 %copy-start.21 = (f32[128,128]{1,0:T(8,128)S(1)}, f32[128,128]{1,0:T(8,128)}, u32[]{:S(2)}) copy-start(f32[128,128]{1,0:T(8,128)} %param.47) | copy-start | bytes 196612
  505.3 165.1 %copy-start.7 = (f32[2,48,256]{2,1,0:T(8,128)S(1)}, f32[2,48,256]{2,1,0:T(8,128)}, u32[]{:S(2)}) copy-start(f32[2,48,256]{2,1,0:T(8,128)} %param.34) | copy-start | bytes 294916
  505.3 165.1 %copy-start.15 = (f32[2,48,256]{2,1,0:T(8,128)S(1)}, f32[2,48,256]{2,1,0:T(8,128)}, u32[]{:S(2)}) copy-start(f32[2,48,256]{2,1,0:T(8,128)} %param.50) | copy-start | bytes 294916
  505.4 165.1 %copy-start.16 = (f32[2,48,256]{2,1,0:T(8,128)S(1)}, f32[2,48,256]{2,1,0:T(8,128)}, u32[]{:S(2)}) copy-start(f32[2,48,256]{2,1,0:T(8,128)} %param.42) | copy-start | bytes 294916
  505.4 165.9 %copy-start.42 = (f32[16]{0:T(128)S(1)}, f32[16]{0:T(128)}, u32[]{:S(2)}) copy-start(f32[16]{0:T(128)} %param.41) | copy-start | bytes 196
  505.4 165.9 %copy-start.43 = (f32[16]{0:T(128)S(1)}, f32[16]{0:T(128)}, u32[]{:S(2)}) copy-start(f32[16]{0:T(128)} %param.57) | copy-start | bytes 196
  505.4 165.8 %copy-start.44 = (f32[16]{0:T(128)S(1)}, f32[16]{0:T(128)}, u32[]{:S(2)}) copy-start(f32[16]{0:T(128)} %param.49) | copy-start | bytes 196
  505.4 154.4 %all-reduce.9.cloned.1.call-start = ((), (), s32[]{:S(2)}) async-start(), calls=%async_computation | async-start | bytes 483328 | tf_op jit(solution)/shard_map/psum | solution.py:534
  (21 other events, 532.1 us)
Sparse Core Ops, SparseCore 0:
  22.8 128.1 all-reduce.10
  505.5 105.7 all-reduce.12
  614.5 22.3 all-reduce.8

commit v2 on v1

v2 whole, which is shorter than its diff:
```python
import jax
import jax.numpy as jnp
import numpy as np
from jax import lax
from jax.experimental import pallas as pl
from jax.experimental.pallas import tpu as pltpu
from jax.sharding import PartitionSpec as P

STEP = 10
EPS_NORM = 1e-06
BETA_ONE = 0.9
BETA_TWO = 0.95
ADAM_EPS = 1e-08
DECAY = 0.1
RATE_MATRIX = 0.04
RATE_GAIN = 0.25
GEN_WEIGHT = 0.02
HALVES = (3.5, 3.5, 3.5, 2.0, 2.0, 2.0)
LEVELS = (8, 8, 8, 5, 5, 5)

F32 = jnp.float32
BF16 = jnp.bfloat16
VMEM_LIMIT = 60 * 2**20
FAKE_LANES = 512
REAL_LANES = 1024
SLABS = 16
VALUES = (0, 8, 4, 12, 2, 10, 6, 14)
AUTO_ROWS = 160
SLAB_ROWS = 240
AXES = (1, 1, 1, 1, 1, 0, 1, 0)
HIGHEST = lax.Precision.HIGHEST


def nn(left, right):
    return jnp.dot(left, right, preferred_element_type=F32)


def nt(left, right):
    return lax.dot_general(left, right, (((1,), (1,)), ((), ())), preferred_element_type=F32)


def low(value):
    return value.astype(BF16)


def wide(columns, lanes):
    return jnp.concatenate([columns] * (lanes // 128), axis=1)


def fold(value):
    total = value[:, :128]
    for start in range(128, value.shape[1], 128):
        total = total + value[:, start : start + 128]
    return total


def silu_parts(half):
    turned = jnp.tanh(half)
    upper = 1.0 + turned
    acted = half * upper
    return acted, upper + acted * (1.0 - turned)


def norm_parts(stream):
    scaling = lax.rsqrt(jnp.mean(stream * stream, axis=0, keepdims=True) + EPS_NORM)
    return scaling, stream * scaling


def softplus(value):
    return jnp.maximum(value, 0.0) + jnp.log1p(jnp.exp(-jnp.abs(value)))


def cost(flops, moved):
    return pl.CostEstimate(flops=int(flops), bytes_accessed=int(moved), transcendentals=0)


def aligned(index, size):
    return pl.ds(pl.multiple_of(index * size, size), size)


def interleave(*pieces):
    pieces = list(pieces)
    while pieces:
        for piece in list(pieces):
            try:
                next(piece)
            except StopIteration:
                pieces.remove(piece)


def slab_owners(me, slabs):
    for core, array in enumerate(slabs):
        for place, value in enumerate(VALUES):
            yield me ^ value ^ core, array.at[place]


def unpack_judge(me, slabs, pair_s, misc_s, first_row):
    for owner, slab in slab_owners(me, slabs):
        rows = pl.ds(pl.multiple_of(lax.rem(owner, 8) * 128, 128), 64)
        more = pl.ds(pl.multiple_of(lax.rem(owner, 8) * 128 + 64, 64), 64)
        side = owner // 8
        pair_s[side, rows, :] = slab[first_row : first_row + 64, 0:128]
        pair_s[side, more, :] = slab[first_row : first_row + 64, 128:256]
        misc_s[aligned(owner, 16), :] = slab[first_row + 64 : first_row + 80, :]


def slab_targets(me):
    for core in range(2):
        for place, value in enumerate(VALUES):
            yield me ^ value ^ core, core, place


def scalar_rows(scalars, split):
    row = lax.broadcasted_iota(jnp.int32, (16, 128), 0)
    if not split:
        return jnp.where(row == 0, scalars, 0.0)
    upper = low(scalars).astype(F32)
    rest = scalars - upper
    middle = low(rest).astype(F32)
    return jnp.where(row == 0, upper, jnp.where(row == 1, middle, jnp.where(row == 2, rest - middle, 0.0)))


def prepare_judge(pair_s, misc_s, judge):
    wmt_s, wmh_s, wlt_s, wlh_s, headw_s, headr_s, bdt_s, bd_s = judge
    half = jnp.asarray(0.5, BF16)
    for side in range(2):
        columns = pl.ds(side * 128, 128)
        for part in range(4):
            rows = pl.ds(part * 256, 256)
            block = pair_s[side, rows, :] * half
            wmh_s[rows, columns] = block
            wmt_s[columns, rows] = block.T
    last_t = misc_s[:, 0:128]
    wlt_s[...] = last_t * half
    wlh_s[...] = last_t.T * half
    turned = misc_s[:, 128:256].T
    headr_s[...] = turned[32:48, :]
    headw_s[...] = jnp.broadcast_to(misc_s[:, 128:256].astype(F32)[:, 32:33] * 0.5, headw_s.shape)
    row = lax.broadcasted_iota(jnp.int32, (256, 256), 0) % 64
    column = lax.broadcasted_iota(jnp.int32, (256, 256), 1)
    pick = low(jnp.where(column == row // 4 * 16 + row % 4, 1.0, 0.0))
    picked = low(nn(pick, misc_s[...]))
    lane = lax.broadcasted_iota(jnp.int32, (256, 192), 0)
    place = lax.broadcasted_iota(jnp.int32, (256, 192), 1)
    spread = low(jnp.where(lane == 176 + place % 48, 1.0, 0.0))
    diagonal = (lane // 64) == (place // 48)
    band_t = jnp.where(diagonal, nn(picked, spread), 0.0)
    bdt_s[...] = low(band_t * 0.5)
    if bd_s is not None:
        bd_s[...] = low(band_t).T


def judge_scratch(fake):
    shapes = [((256, 1024), BF16), ((1024, 256), BF16), ((256, 128), BF16), ((128, 256), BF16)]
    shapes += [((256, 128), F32), ((16, 256), BF16), ((256, 192), BF16)]
    if fake:
        shapes += [((192, 256), BF16)]
    return shapes


def judge_middle(fresh, q_s, judge, count_all, active, counted, kind, gwl_ref, ghead_ref, loss_ref, new_g2, extra_loss=None):
    _, _, wlt_s, wlh_s, headw_s, headr_s = judge[:6]
    lanes = fresh.shape[1]
    acted_two, slope_two = silu_parts(fresh[:128] + q_s[...])
    q_s[...] = fresh[128:]
    acted_two = low(acted_two)
    yield
    acted_three, slope_three = silu_parts(nn(wlt_s[...], acted_two))
    acted_three = low(acted_three)
    yield
    score = nn(headr_s[...], acted_three)[:1]
    shaped = wide(headw_s[...], lanes) * slope_three
    if kind == "real":
        grad_score = -jax.nn.sigmoid(1.0 - score) * (active / count_all)
        grad_three = low(grad_score * shaped)
        loss_ref[0:1, :] += softplus(1.0 - score) * counted
        yield
        new_g2[0][...] = low(nn(wlh_s[...], grad_three) * slope_two)
    else:
        pull = jax.nn.sigmoid(1.0 + score)
        grad_score = pull * (active / count_all)
        grad_three = low(grad_score * shaped)
        grad_three_gen = low((-GEN_WEIGHT / count_all * active) * shaped)
        loss_ref[0:1, :] += softplus(1.0 + score) * counted
        loss_ref[1:2, :] -= score * counted
        yield
        grad_two_gen = nn(wlh_s[...], grad_three_gen) * slope_two
        new_g2[0][...] = low(grad_two_gen * (pull * (-1.0 / GEN_WEIGHT)))
        new_g2[1][...] = low(grad_two_gen)
    yield
    gwl_ref[...] += nt(acted_two * counted.astype(BF16), grad_three)
    ghead_ref[...] += fold(acted_three.astype(F32) * (grad_score * counted))
    yield


def real_kernel(band, lanes, chunks, count_all):
    rows_n = band + 1
    total = chunks * rows_n

    def kernel(*refs):
        refs = list(refs)

        def take(number):
            taken = refs[:number]
            del refs[:number]
            return taken

        (places,) = take(1)
        slabs = take(2)
        xf, xe, xbelow, xabove = take(4)
        start_refs = take(4)
        (fake_loss,) = take(1)
        send_ref, keep_ref = take(2)
        judge = take(7) + [None]
        pair_s, misc_s = take(2)
        gwm_ref, gwl_ref, gw1_ref, ghead_ref = take(4)
        q_s, g2, g2_new, act_s, slope_s, small = take(6)
        first_s, lastt_s, loss_ref = take(3)
        wmt_s, wmh_s, bdt_s = judge[0], judge[1], judge[6]
        stage = pl.program_id(0)
        has_below, has_above, me = places[1], places[2].astype(F32), places[3]
        step = lax.rem(stage, rows_n)
        row = band - 1 - step
        slot = lax.rem(stage, 2)
        back_ok = (stage >= 2) & (lax.rem(stage - 2, rows_n) != band)
        front_ok = stage < total
        act, slope = act_s.at[slot], slope_s.at[slot]
        halo = row < 0
        active = jnp.where(halo, has_above, 1.0)
        counted = jnp.where(halo, 0.0, 1.0)

        @pl.when(stage == 0)
        def prepare():
            unpack_judge(me, slabs, pair_s, misc_s, 0)
            prepare_judge(pair_s, misc_s, judge)
            for ref, start in zip((gwm_ref, gwl_ref, gw1_ref, ghead_ref), start_refs):
                ref[...] = start[...]
            loss_ref[...] = jnp.zeros_like(loss_ref)

        @pl.when(front_ok & (step == 0) & (has_below > 0))
        def below():
            joined = jnp.zeros((128, lanes), F32)
            for group in range(4):
                acted, _ = silu_parts(nn(bdt_s[...], xbelow[192 * group : 192 * group + 192, :]))
                joined = joined + nn(wmt_s[128:256, 256 * group : 256 * group + 256], low(acted))
            q_s[...] = joined

        @pl.when(front_ok & (step == 0) & (has_below == 0))
        def edge():
            q_s[...] = jnp.zeros_like(q_s)

        def back_small():
            for group in range(4):
                rows = slice(256 * group, 256 * group + 256)
                for start in range(0, lanes, 256):
                    part = slice(start, start + 256)
                    small[rows, part] = low(nn(wmh_s[rows, :], g2[:, part]) * slope[rows, part])
                yield

        def back_middle():
            for group in range(4):
                rows = slice(256 * group, 256 * group + 256)
                gwm_ref[rows, :] += nt(act[rows, :], g2[...])
                yield

        def back_first():
            for group in range(4):
                gw1_ref[...] += nt(xe[0, 192 * group : 192 * group + 192, :], small[256 * group : 256 * group + 256, :])
                yield

        def front_first():
            for group in range(4):
                for start in range(0, lanes, 256):
                    part = slice(start, start + 256)
                    rows = slice(192 * group, 192 * group + 192)
                    x = jnp.where(halo, xabove[rows, part], xf[0, rows, part])
                    acted, slope_new = silu_parts(nn(bdt_s[...], x))
                    act[256 * group : 256 * group + 256, part] = low(acted)
                    slope[256 * group : 256 * group + 256, part] = slope_new
                yield

        def front_middle():
            fresh = nn(wmt_s[...], act[...])
            yield
            yield from judge_middle(
                fresh, q_s, judge, count_all, active, counted, "real", gwl_ref, ghead_ref, loss_ref, (g2_new,)
            )

        def shift():
            g2[0:128, :] = g2[128:256, :]
            g2[128:256, :] = g2_new[...]

        @pl.when(front_ok & back_ok)
        def both():
            interleave(back_small())
            interleave(back_middle(), front_first())
            interleave(front_middle(), back_first())
            shift()

        @pl.when(front_ok & jnp.logical_not(back_ok))
        def front_only():
            interleave(front_first())
            interleave(front_middle())
            shift()

        @pl.when(jnp.logical_not(front_ok) & back_ok)
        def back_only():
            interleave(back_small())
            interleave(back_first(), back_middle())

        @pl.when(stage == total)
        def write():
            turned = gw1_ref[...].T
            lane = lax.broadcasted_iota(jnp.int32, (64, 192), 1)
            summed = jnp.zeros((64, 192), F32)
            for block in range(4):
                summed = summed + jnp.where(lane // 48 == block, turned[64 * block : 64 * block + 64, :], 0.0)
            place = lax.broadcasted_iota(jnp.int32, (192, 128), 0) % 48
            folding = jnp.where(place == lax.broadcasted_iota(jnp.int32, (192, 128), 1), 1.0, 0.0)
            first = jnp.dot(summed, folding, precision=HIGHEST, preferred_element_type=F32)
            for owner in range(SLABS):
                first_s[16 * owner : 16 * owner + 16, :] = jnp.zeros((16, 128), F32)
                first_s[16 * owner : 16 * owner + 4, :] = first[4 * owner : 4 * owner + 4, :]
            lastt_s[...] = gwl_ref[...].T
            scalars = jnp.zeros((1, 128), F32)
            sums = (jnp.sum(fake_loss[2:3, :]), jnp.sum(fake_loss[1:2, :]), jnp.sum(fake_loss[0:1, :]) + jnp.sum(loss_ref[0:1, :]))
            for number, item in enumerate(sums):
                scalars = jnp.where(lax.broadcasted_iota(jnp.int32, (1, 128), 1) == number, item, scalars)
            for owner, core, chip in slab_targets(me):
                side, rows = owner // 8, lax.rem(owner, 8) * 128
                upper = pl.ds(pl.multiple_of(rows, 64), 64)
                lower = pl.ds(pl.multiple_of(rows + 64, 64), 64)
                own = aligned(owner, 16)
                left = jnp.where(side == 0, gwm_ref[upper, 0:128], gwm_ref[upper, 128:256])
                right = jnp.where(side == 0, gwm_ref[lower, 0:128], gwm_ref[lower, 128:256])
                target = (keep_ref, send_ref)[core]
                target[chip, 0:64, 0:128] = left
                target[chip, 0:64, 128:256] = right
                target[chip, 64:80, 0:128] = ghead_ref[own, :]
                target[chip, 64:80, 128:256] = lastt_s[own, :]
                target[chip, 80:96, 0:128] = first_s[own, :]
                target[chip, 80:96, 128:256] = scalar_rows(scalars, False)

    return kernel


def run_real(xt, halos, places, slabs, starts, count_all):
    band, _, positions = xt.shape
    lanes = min(REAL_LANES, positions)
    chunks = positions // lanes
    rows_n = band + 1
    total = chunks * rows_n

    def front_row(t):
        t = jnp.minimum(t, total - 1)
        return (jnp.maximum(band - 1 - lax.rem(t, rows_n), 0), 0, t // rows_n)

    def back_row(t):
        t = jnp.maximum(t - 2, 0)
        return (jnp.maximum(band - 1 - lax.rem(t, rows_n), 0), 0, t // rows_n)

    def halo_row(t):
        return (0, jnp.minimum(t, total - 1) // rows_n)

    specs = [pl.BlockSpec(memory_space=pltpu.SMEM)]
    specs += [pl.BlockSpec((SLABS // 2, 80, 256), lambda t: (0, 2, 0))] * 2
    specs += [pl.BlockSpec((1, 768, lanes), front_row), pl.BlockSpec((1, 768, lanes), back_row)]
    specs += [pl.BlockSpec((768, lanes), halo_row)] * 2
    specs += [pl.BlockSpec(item.shape, lambda t: (0, 0)) for item in starts]
    outs = [
        jax.ShapeDtypeStruct((SLABS // 2, 96, 256), F32),
        jax.ShapeDtypeStruct((SLABS // 2, 96, 256), F32),
    ]
    scratch = judge_scratch(False) + [((2, 1024, 128), BF16), ((256, 256), BF16)]
    scratch += [((1024, 256), F32), ((128, 256), F32), ((192, 256), F32), ((256, 128), F32)]
    scratch += [((128, lanes), F32), ((256, lanes), BF16), ((128, lanes), BF16)]
    scratch += [((2, 1024, lanes), BF16), ((2, 1024, lanes), F32), ((1024, lanes), BF16)]
    scratch += [((256, 128), F32), ((256, 128), F32), ((8, lanes), F32)]
    return pl.pallas_call(
        real_kernel(band, lanes, chunks, count_all),
        grid=(total + 1,),
        in_specs=specs,
        out_specs=[pl.BlockSpec(item.shape, lambda t, n=len(item.shape): (0,) * n) for item in outs],
        out_shape=outs,
        scratch_shapes=[pltpu.VMEM(*item) for item in scratch],
        compiler_params=pltpu.CompilerParams(vmem_limit_bytes=VMEM_LIMIT),
        cost_estimate=cost(5.4e6 * band * positions, 3072 * band * positions),
        name="judge_real",
    )(places, *slabs, xt, xt, *halos, *starts)


def block_forward(stream, gain, first_half_t, second_t):
    scaling, normal = norm_parts(stream)
    normed = low(normal * gain)
    acted, slope = silu_parts(nn(first_half_t, normed))
    acted = low(acted)
    return stream + nn(second_t, acted), (scaling, normal, normed, acted, slope)


def block_backward(grad_out, saved, gain, first, second_half, grad_first, grad_second, grad_gain):
    scaling, normal, normed, acted, slope = saved
    grad_low = low(grad_out)
    grad_second[...] += nt(acted, grad_low)
    grad_inside = low(nn(second_half, grad_low) * slope)
    grad_first[...] += nt(normed, grad_inside)
    grad_normed = nn(first, grad_inside)
    along = grad_normed * normal
    grad_gain[...] += fold(along)
    mean = jnp.mean(along * gain, axis=0, keepdims=True)
    return grad_out + scaling * (grad_normed * gain - normal * mean)


def fake_kernel(band, lanes, chunks, count_all):
    names = ("fake", "gl1", "act", "slope", "normal", "scaling", "normed", "acted", "bslope", "outlow", "values")

    def kernel(*refs):
        refs = list(refs)

        def take(number):
            taken = refs[:number]
            del refs[:number]
            return taken

        (places,) = take(1)
        slabs = take(2)
        xc_ref, xa_ref, xb_ref, codes_ref, lane_ref, consts_ref, spots_ref = take(7)
        send_ref, keep_ref, gwm_ref, gwl_ref, gw1_ref, ghead_ref, loss_ref = take(7)
        judge = take(8)
        pair_s, misc_s = take(2)
        proj_s, projt_s, block_s, blockt_s, blockh_s, fsq_s, fsqt_s, gains_s, total_s = take(9)
        gproj_ref, gblocks_ref, gfsq_ref, ggains_ref = take(4)
        q_s, g2_disc, g2_gen, new_disc, new_gen, small_s, smallgen_s, gradlow_s = take(8)
        stash_a = dict(zip(names, take(len(names))))
        stash_b = dict(zip(names, take(len(names))))
        wmt_s, wmh_s, bdt_s, bd_s = judge[0], judge[1], judge[6], judge[7]
        chunk, step = pl.program_id(0), pl.program_id(1)
        last_step = band // 2
        row_start, has_below, me = places[0], places[1], places[3]
        has_above = places[2].astype(F32)

        @pl.when((chunk == 0) & (step == 0))
        def prepare():
            unpack_judge(me, slabs, pair_s, misc_s, AUTO_ROWS)
            prepare_judge(pair_s, misc_s, judge)
            for owner, slab in slab_owners(me, slabs):
                rows, some = aligned(owner, 48), aligned(owner, 16)
                proj_s[0, rows, :] = slab[0:48, :]
                proj_s[1, rows, :] = slab[48:96, :]
                for index in range(4):
                    block_s[index, some, :] = slab[96 + 16 * index : 112 + 16 * index, :]
            projt_s[0] = proj_s[0].T
            projt_s[1] = proj_s[1].T
            for index in range(4):
                scale = jnp.asarray(0.5 if index % 2 == 0 else 1.0, BF16)
                blockt_s[index] = (block_s[index] * scale).T
                if index % 2 == 1:
                    blockh_s[index // 2] = block_s[index] * jnp.asarray(0.5, BF16)
            tail = misc_s[:, 128:256]
            turned = tail.T
            fsqt_s[0] = turned[0:16, :]
            fsqt_s[1] = turned[16:32, :]
            for index in range(2):
                fsq_s[index] = fsqt_s[index].T
                gains_s[index] = jnp.broadcast_to(tail.astype(F32)[:, 33 + index : 34 + index], (256, 128))
            lane = lax.broadcasted_iota(jnp.int32, (256, 128), 1)
            held = (lane >= 96) & (lane < 99)
            total_s[...] = jnp.broadcast_to(jnp.sum(jnp.where(held, tail.astype(F32), 0.0)), (8, 128))
            for ref in (gwm_ref, gwl_ref, gw1_ref, ghead_ref, loss_ref, gproj_ref, gblocks_ref, gfsq_ref, ggains_ref):
                ref[...] = jnp.zeros_like(ref)

        def latent_values(row):
            consts = consts_ref[...]
            code = codes_ref[pl.ds(row + 1, 1), :]
            turn = jnp.floor((code + 0.5) * wide(consts[0:16], lanes))
            level = wide(consts[16:32], lanes)
            digit = turn - level * jnp.floor((turn + 0.5) * wide(consts[32:48], lanes))
            return low((digit - wide(consts[48:64], lanes)) * wide(consts[64:80], lanes))

        def front(row, x_ref, stash):
            values = latent_values(row)
            stash["values"][...] = values
            gain = wide(gains_s[1], lanes)
            output, saved = block_forward(nn(fsq_s[1], values), gain, blockt_s[2], blockt_s[3])
            outlow = low(output)
            stash["outlow"][...] = outlow
            for name, item in zip(("scaling", "normal", "normed", "acted", "bslope"), saved):
                stash[name][...] = item
            lane = lax.broadcasted_iota(jnp.int32, (1, lanes), 1)
            column = (lane % 16).astype(F32)
            place = (row_start + row).astype(F32)
            high = lane_ref[0:1, :] - 16.0 * place
            broad = lane_ref[1:2, :] - 16.0 * column
            counted = jnp.where(row >= 0, 1.0, 0.0)
            active = jnp.where(row >= 0, 1.0, has_above)
            weight = lane_ref[2:3, :] * counted
            weight_share = weight / wide(total_s[0:1, :], lanes)
            l1_sum = jnp.zeros((1, lanes), F32)
            for group in range(4):
                rows = pl.ds(group * 192, 192)
                recon = nn(proj_s[1, rows, :], outlow)
                stash["fake"][rows, :] = low(recon)
                diff = recon - x_ref[0, rows, :].astype(F32)
                square = diff * diff + 1.0
                inverse = lax.rsqrt(square)
                inside = (wide(spots_ref[0, rows, :], lanes) < high) & (wide(spots_ref[1, rows, :], lanes) < broad)
                l1_sum = l1_sum + jnp.sum(jnp.where(inside, square * inverse, 0.0), axis=0, keepdims=True)
                stash["gl1"][rows, :] = jnp.where(inside, diff * inverse, 0.0) * weight_share
            loss_ref[2:3, :] += l1_sum * weight
            for group in range(4):
                rows, wide_rows = pl.ds(group * 192, 192), pl.ds(group * 256, 256)
                acted, slope = silu_parts(nn(bdt_s[...], stash["fake"][rows, :]))
                stash["act"][wide_rows, :] = low(acted)
                stash["slope"][wide_rows, :] = slope
            fresh = nn(wmt_s[...], stash["act"][...])
            for _ in judge_middle(
                fresh, q_s, judge, count_all, active, counted, "fake", gwl_ref, ghead_ref, loss_ref, (new_disc, new_gen)
            ):
                pass
            g2_disc[128:256, :] = new_disc[...]
            g2_gen[128:256, :] = new_gen[...]

        def below():
            values = latent_values(jnp.int32(band))
            output, _ = block_forward(nn(fsq_s[1], values), wide(gains_s[1], lanes), blockt_s[2], blockt_s[3])
            outlow = low(output)
            joined = jnp.zeros((128, lanes), F32)
            for group in range(4):
                recon = low(nn(proj_s[1, pl.ds(group * 192, 192), :], outlow))
                acted, _ = silu_parts(nn(bdt_s[...], recon))
                joined = joined + nn(wmt_s[128:256, 256 * group : 256 * group + 256], low(acted))
            q_s[...] = joined

        def finish(x_ref, stash):
            for group in range(4):
                wide_rows = pl.ds(group * 256, 256)
                slope = stash["slope"][wide_rows, :]
                smallgen_s[wide_rows, :] = low(nn(wmh_s[wide_rows, :], g2_gen[...]) * slope)
                small_s[wide_rows, :] = low(nn(wmh_s[wide_rows, :], g2_disc[...]) * slope)
            for group in range(4):
                rows, wide_rows = pl.ds(group * 192, 192), pl.ds(group * 256, 256)
                gradlow_s[rows, :] = low(stash["gl1"][rows, :] + nn(bd_s[...], smallgen_s[wide_rows, :]))
            gain = wide(gains_s[1], lanes)
            saved = tuple(stash[name][...] for name in ("scaling", "normal", "normed", "acted", "bslope"))
            grad_output = nn(projt_s[1], gradlow_s[...])
            for group in range(4):
                rows, wide_rows = pl.ds(group * 192, 192), pl.ds(group * 256, 256)
                gw1_ref[...] += nt(stash["fake"][rows, :], small_s[wide_rows, :])
                gwm_ref[wide_rows, :] += nt(stash["act"][wide_rows, :], g2_disc[...])
                gproj_ref[1, rows, :] += nt(gradlow_s[rows, :], stash["outlow"][...])
            grad_start = block_backward(
                grad_output, saved, gain, block_s[2], blockh_s[1],
                gblocks_ref.at[2], gblocks_ref.at[3], ggains_ref.at[1],
            )
            start_low = low(grad_start)
            gfsq_ref[1] += nt(start_low, stash["values"][...])
            grad_values = nn(fsqt_s[1], start_low)
            gain = wide(gains_s[0], lanes)
            stream = nn(projt_s[0], x_ref[0])
            middle, saved = block_forward(stream, gain, blockt_s[0], blockt_s[1])
            middle_low = low(middle)
            tangent = jnp.tanh(nn(fsqt_s[0], middle_low))
            grad_latent = low(grad_values * (1.0 - tangent * tangent))
            gfsq_ref[0] += nt(middle_low, grad_latent)
            grad_stream = block_backward(
                nn(fsq_s[0], grad_latent), saved, gain, block_s[0], blockh_s[0],
                gblocks_ref.at[0], gblocks_ref.at[1], ggains_ref.at[0],
            )
            gproj_ref[0] += nt(x_ref[0], low(grad_stream))
            for ref in (g2_disc, g2_gen):
                ref[0:128, :] = ref[128:256, :]

        @pl.when((step == 0) & (has_below > 0))
        def halo():
            below()

        @pl.when((step == 0) & (has_below == 0))
        def edge():
            q_s[...] = jnp.zeros_like(q_s)

        @pl.when(step == 0)
        def first():
            front(jnp.int32(band - 1), xa_ref, stash_a)
            for ref in (g2_disc, g2_gen):
                ref[0:128, :] = ref[128:256, :]

        @pl.when(step > 0)
        def main():
            front(band - 2 * step, xa_ref, stash_b)
            finish(xc_ref, stash_a)
            front(band - 2 * step - 1, xb_ref, stash_a)
            finish(xa_ref, stash_b)

        @pl.when((chunk == chunks - 1) & (step == last_step))
        def write():
            loss_ref[3:4, 0:128] = total_s[0:1, :]
            for owner, core, chip in slab_targets(me):
                rows, own = aligned(owner, 48), aligned(owner, 16)
                target = (keep_ref, send_ref)[core]
                target[chip, 0:48, :] = gproj_ref[0, rows, :]
                target[chip, 48:96, :] = gproj_ref[1, rows, :]
                for index in range(4):
                    target[chip, 96 + 16 * index : 112 + 16 * index, :] = gblocks_ref[index, own, :]
                target[chip, 160:192, :] = jnp.zeros((32, 256), F32)
                target[chip, 160:176, 0:16] = gfsq_ref[0, own, :]
                target[chip, 160:176, 128:144] = gfsq_ref[1, own, :]
                target[chip, 176:192, 0:128] = ggains_ref[0, own, :]
                target[chip, 176:192, 128:256] = ggains_ref[1, own, :]

    return kernel


def run_fake(xt, places, slabs, extra, count_all):
    band, _, positions = xt.shape
    lanes = min(FAKE_LANES, positions)
    chunks = positions // lanes
    codes, lane_info, consts, spots = extra

    def whole(array):
        return pl.BlockSpec(array.shape, lambda c, s: (0,) * array.ndim)

    def row_spec(shift):
        def index(c, s):
            row = jnp.where(s == 0, band - 1, band - 2 * s + shift)
            return (jnp.maximum(row, 0), 0, c)

        return pl.BlockSpec((1, 768, lanes), index)

    specs = [pl.BlockSpec(memory_space=pltpu.SMEM)]
    specs += [whole(item) for item in slabs]
    specs += [row_spec(1), row_spec(0), row_spec(-1)]
    specs += [
        pl.BlockSpec((codes.shape[0], lanes), lambda c, s: (0, c)),
        pl.BlockSpec((lane_info.shape[0], lanes), lambda c, s: (0, c)),
        whole(consts),
        whole(spots),
    ]
    outs = [
        jax.ShapeDtypeStruct((SLABS // 2, 192, 256), F32),
        jax.ShapeDtypeStruct((SLABS // 2, 192, 256), F32),
        *(jax.ShapeDtypeStruct(shape, F32) for shape in [(1024, 256), (128, 256), (192, 256), (256, 128), (8, lanes)]),
    ]
    scratch = judge_scratch(True) + [((2, 1024, 128), BF16), ((256, 256), BF16)]
    scratch += [((2, 768, 256), BF16), ((2, 256, 768), BF16), ((4, 256, 256), BF16), ((4, 256, 256), BF16)]
    scratch += [((2, 256, 256), BF16), ((2, 256, 16), BF16), ((2, 16, 256), BF16), ((2, 256, 128), F32), ((8, 128), F32)]
    scratch += [((2, 768, 256), F32), ((4, 256, 256), F32), ((2, 256, 16), F32), ((2, 256, 128), F32)]
    scratch += [((128, lanes), F32)] + [((256, lanes), BF16)] * 2 + [((128, lanes), BF16)] * 2
    scratch += [((1024, lanes), BF16)] * 2 + [((768, lanes), BF16)]
    scratch += [
        ((768, lanes), BF16),
        ((768, lanes), F32),
        ((1024, lanes), BF16),
        ((1024, lanes), F32),
        ((256, lanes), F32),
        ((1, lanes), F32),
        ((256, lanes), BF16),
        ((256, lanes), BF16),
        ((256, lanes), F32),
        ((256, lanes), BF16),
        ((16, lanes), BF16),
    ] * 2
    return pl.pallas_call(
        fake_kernel(band, lanes, chunks, count_all),
        grid=(chunks, band // 2 + 1),
        in_specs=specs,
        out_specs=[pl.BlockSpec(item.shape, lambda c, s, n=len(item.shape): (0,) * n) for item in outs],
        out_shape=outs,
        scratch_shapes=[pltpu.VMEM(*item) for item in scratch],
        compiler_params=pltpu.CompilerParams(vmem_limit_bytes=VMEM_LIMIT),
        cost_estimate=cost(1.6e7 * band * positions, 3072 * band * positions),
        name="judge_fake",
    )(places, *slabs, xt, xt, xt, codes, lane_info, consts, spots)


def turn_kernel(pixels_ref, turned_ref):
    frames = pixels_ref.shape[0]
    turned_ref[0] = pixels_ref[...].reshape(frames * 16, 768).T


def turn_pixels(pixels):
    frames, band = pixels.shape[:2]
    part = min(frames, 32)
    return pl.pallas_call(
        turn_kernel,
        grid=(band, frames // part),
        in_specs=[pl.BlockSpec((part, 1, 16, 768), lambda r, c: (c, r, 0, 0))],
        out_specs=pl.BlockSpec((1, 768, part * 16), lambda r, c: (r, 0, c)),
        out_shape=jax.ShapeDtypeStruct((band, 768, frames * 16), BF16),
        compiler_params=pltpu.CompilerParams(vmem_limit_bytes=VMEM_LIMIT),
        cost_estimate=cost(0, 4 * pixels.size),
        name="turn",
    )(pixels)


def count_kernel(codes_ref, counts_ref):
    @pl.when(pl.program_id(0) == 0)
    def clear():
        counts_ref[...] = jnp.zeros_like(counts_ref)

    code = codes_ref[0]
    upper = jnp.floor(code * (1.0 / 256.0))
    lower = code - 256.0 * upper
    bins = lax.broadcasted_iota(jnp.int32, (256, code.shape[1]), 0).astype(F32)
    one, zero = jnp.asarray(1.0, F32), jnp.asarray(0.0, F32)
    counts_ref[...] += nt(low(jnp.where(bins == upper, one, zero)), low(jnp.where(bins == lower, one, zero)))


def count_codes(codes):
    parts, lanes = codes.shape
    return pl.pallas_call(
        count_kernel,
        grid=(parts,),
        in_specs=[pl.BlockSpec((1, 1, lanes), lambda s: (s, 0, 0))],
        out_specs=pl.BlockSpec((256, 256), lambda s: (0, 0)),
        out_shape=jax.ShapeDtypeStruct((256, 256), F32),
        cost_estimate=cost(5e5 * codes.size, 4 * codes.size),
        name="count",
    )(codes[:, None, :])


def frame_kernel(place_ref, clips_ref, bounds_ref, project, matrices, fsq_pair, gain_pair, first_conv, mid_conv, last_conv, head_map, lane_ref, slab_ref, turned_s):
    lanes = lane_ref.shape[1]
    clips = clips_ref[...]
    number = clips.shape[0]
    ahead = lax.broadcasted_iota(jnp.int32, (number, number), 1) < lax.broadcasted_iota(jnp.int32, (number, number), 0)
    starts = nn(low(jnp.where(ahead, 1.0, 0.0)), low(clips))
    frame = (place_ref[0] + lax.broadcasted_iota(jnp.int32, (1, lanes), 1) // 16).astype(F32)
    first, size = wide(starts, lanes), wide(clips, lanes)
    mine = (first <= frame) & (frame < first + size)
    weight = 1.0 / jnp.sum(jnp.where(mine, size, 0.0), axis=0, keepdims=True)
    height, width = bounds_ref[0:1, :], bounds_ref[1:2, :]
    lane_ref[0:1, :] = height
    lane_ref[1:2, :] = width
    lane_ref[2:3, :] = weight
    lane_ref[3:8, :] = jnp.zeros((5, lanes), F32)
    total = jnp.sum(height * width * weight * (3.0 / 16.0), axis=1, keepdims=True)
    for index in range(2):
        slab_ref[48 * index : 48 * index + 48, :] = low(project[index])
    for index in range(4):
        slab_ref[96 + 16 * index : 112 + 16 * index, :] = low(matrices[index])
    slab_ref[160:224, 0:128] = low(mid_conv[0:64, :])
    slab_ref[160:224, 128:256] = low(mid_conv[64:128, :])
    slab_ref[224:240, 0:128] = low(last_conv[...])
    turned_s[...] = jnp.zeros_like(turned_s)
    for index in range(2):
        turned_s[16 * index : 16 * index + 6, :] = fsq_pair[index]
    turned_s[32:33, :] = head_map[...]
    turned_s[33:35, :] = gain_pair[...]
    turned_s[48:96, 0:4] = first_conv[...].T
    upper = low(total).astype(F32)
    rest = total - upper
    middle = low(rest).astype(F32)
    for index, item in enumerate((upper, middle, rest - middle)):
        turned_s[96 + index : 97 + index, 0:1] = item
    slab_ref[224:240, 128:256] = low(turned_s[...].T)


def frame_lanes(first, clip_frames, frame_bounds, masters):
    lanes = frame_bounds.shape[0] * 16
    clips = jnp.broadcast_to(clip_frames.astype(F32)[:, None], (clip_frames.shape[0], 128))
    bounds = jnp.repeat(frame_bounds.T.astype(F32), 16, axis=1)
    operands = list(masters)
    operands[2] = operands[2].transpose(0, 2, 1)
    operands[4] = operands[4].T
    operands[6] = operands[6].T
    operands[7] = operands[7][None, :]
    return pl.pallas_call(
        frame_kernel,
        in_specs=[pl.BlockSpec(memory_space=pltpu.SMEM)] + [pl.BlockSpec(memory_space=pltpu.VMEM)] * 10,
        out_specs=[pl.BlockSpec(memory_space=pltpu.VMEM)] * 2,
        out_shape=[jax.ShapeDtypeStruct((8, lanes), F32), jax.ShapeDtypeStruct((SLAB_ROWS, 256), BF16)],
        scratch_shapes=[pltpu.VMEM((128, 16), F32)],
        name="frames",
    )(first.reshape(1), clips, bounds, *operands)


def passed_along(x, axis, by):
    size = lax.axis_size(axis)
    pairs = [(i, i + by) for i in range(size) if 0 <= i + by < size]
    return lax.ppermute(x, axis, pairs)


def swap(x, axis, bits):
    return lax.ppermute(x, axis, [(i, i ^ bits) for i in range(lax.axis_size(axis))])


def sum_all(x, axis):
    bits, size = 1, lax.axis_size(axis)
    while bits < size:
        x = x + swap(x, axis, bits)
        bits *= 2
    return x


def gather_slabs(slab, beside):
    gathered = slab[None]
    for bits, item in zip((8, 4, 2), beside):
        got = swap(gathered, "dp", bits)
        if item is not None:
            got, _ = lax.optimization_barrier((got, item))
        gathered = jnp.concatenate([gathered, got], axis=0)
    return gathered, swap(gathered, "dp", 1)


def hop_kernel(plans, *refs):
    refs = list(refs)
    inputs, outputs = refs[: 2 * len(plans)], refs[2 * len(plans) :]
    for number, (count, scalars, sent) in enumerate(plans):
        keep_ref, got_ref = inputs[2 * number : 2 * number + 2]
        half = count // 2
        for slab in range(count):
            place, cast, out_ref = slab, F32, outputs[0]
            if half and slab >= half:
                place, cast, out_ref = slab - half, sent, outputs[1]
            out_ref[place] = (keep_ref[slab] + got_ref[slab].astype(F32)).astype(cast)
            if scalars:
                got = got_ref[slab, 80:96, 128:256].astype(F32)
                exact = keep_ref[slab, 80:81, 128:256] + ((got[0:1] + got[1:2]) + got[2:3])
                out_ref[place, 80:96, 128:256] = scalar_rows(exact, cast == BF16).astype(cast)
        outputs = outputs[2 if half else 1 :]


def hop(*sums):
    plans, operands, outs = [], [], []
    for keep, got, scalars, sent in sums:
        count, rows = keep.shape[0], keep.shape[1]
        plans.append((count, scalars, sent))
        operands += [keep, got]
        outs.append(jax.ShapeDtypeStruct((max(count // 2, 1), rows, 256), F32))
        if count > 1:
            outs.append(jax.ShapeDtypeStruct((count // 2, rows, 256), sent))
    vmem = pl.BlockSpec(memory_space=pltpu.VMEM)
    return pl.pallas_call(
        lambda *refs: hop_kernel(plans, *refs),
        in_specs=[vmem] * len(operands),
        out_specs=[vmem] * len(outs),
        out_shape=outs,
        name="hop",
    )(*operands)


def reduce_both(auto_keep, auto_got, judge_send, judge_keep):
    judge_got = swap(judge_send, "dp", 1)
    auto_got, judge_got = lax.optimization_barrier((auto_got, judge_got))
    auto_keep, auto_send, judge_keep, judge_send = hop(
        (auto_keep, auto_got, False, BF16), (judge_keep, judge_got, True, BF16)
    )
    auto_got, judge_got = lax.optimization_barrier((swap(auto_send, "dp", 4), swap(judge_send, "dp", 2)))
    auto_keep, auto_send, judge_keep, judge_send = hop(
        (auto_keep, auto_got, False, F32), (judge_keep, judge_got, True, BF16)
    )
    auto_got, judge_got = lax.optimization_barrier((swap(auto_send, "dp", 8), swap(judge_send, "dp", 4)))
    auto_keep, judge_keep, judge_send = hop((auto_keep, auto_got, False, F32), (judge_keep, judge_got, True, F32))
    auto_got, judge_got = lax.optimization_barrier((swap(auto_keep, "grp", 1), swap(judge_send, "dp", 8)))
    (judge_keep,) = hop((judge_keep, judge_got, True, F32))
    judge_got = swap(judge_keep, "grp", 1)
    return auto_keep[0] + auto_got[0], judge_keep[0] + judge_got[0]


def unpack_auto(total):
    project = total[:96].reshape(2, 48, 256)
    matrices = total[96:160].reshape(4, 16, 256)
    fsq_pair = jnp.stack([total[160:176, 0:6], total[160:176, 128:134]])
    gain_pair = jnp.stack([jnp.sum(total[176:192, 0:128], axis=1), jnp.sum(total[176:192, 128:256], axis=1)])
    return project, matrices, fsq_pair, gain_pair


def unpack_judge_grads(total):
    mid = jnp.concatenate([total[:64, :128], total[:64, 128:]], axis=0)
    head = jnp.sum(total[64:80, 0:128], axis=1)
    last = total[64:80, 128:256].T
    first = total[80:84, 0:48].T
    return first, mid, last, head


def whole_slabs(first, clip_frames, frame_bounds, masters):
    gathered = [lax.all_gather(item, "dp", axis=axis, tiled=True) for item, axis in zip(masters, AXES)]

    def share(array, axis, number):
        size = array.shape[axis] // SLABS
        return lax.slice_in_dim(array, number * size, number * size + size, axis=axis)

    slabs = []
    for number in range(SLABS):
        shares = [share(item, axis, number) for item, axis in zip(gathered, AXES)]
        lane_info, slab = frame_lanes(first, clip_frames, frame_bounds, shares)
        slabs.append(slab)
    held = slabs[0][224, 224:227].astype(F32)
    total = lax.psum(held[0] + held[1] + held[2], "dp")
    upper = low(total)
    middle = low(total - upper.astype(F32))
    lower = low(total - upper.astype(F32) - middle.astype(F32))
    parts = jnp.stack([upper, middle, lower])
    slabs = [slab.at[224, 224:227].set(parts if number == 0 else 0) for number, slab in enumerate(slabs)]
    return lane_info, tuple(jnp.stack([slabs[value ^ core] for value in VALUES]) for core in range(2))


def whole_grads(auto, judge):
    def ordered(send, keep):
        pieces = [None] * SLABS
        for place, value in enumerate(VALUES):
            pieces[value] = keep[place]
            pieces[value ^ 1] = send[place].astype(F32)
        return pieces

    shares = [
        unpack_auto(left) + unpack_judge_grads(right) for left, right in zip(ordered(*auto), ordered(*judge))
    ]
    totals = []
    for index, axis in enumerate(AXES):
        whole = jnp.concatenate([share[index] for share in shares], axis=axis)
        totals.append(lax.psum_scatter(whole, "dp", scatter_dimension=axis, tiled=True))
    scalars = judge[1][0, 80, 128:131]
    totals.append(lax.psum(scalars, "dp"))
    return lax.psum(tuple(totals), "grp")


def adamw(master, moment, square, grad, rate, decay):
    new_moment = BETA_ONE * moment + (1.0 - BETA_ONE) * grad
    new_square = BETA_TWO * square + (1.0 - BETA_TWO) * grad * grad
    update = (
        new_moment
        / (1.0 - BETA_ONE**STEP)
        / (jnp.sqrt(new_square / (1.0 - BETA_TWO**STEP)) + ADAM_EPS)
    )
    return (new_moment, new_square, master - rate * (update + decay * master))


def constants():
    products = np.cumprod((1,) + LEVELS)[:6]
    rows = np.zeros((5, 16), np.float32)
    rows[1] = 1.0
    rows[2] = 1.0
    rows[0, :6] = 1.0 / products
    rows[1, :6] = LEVELS
    rows[2, :6] = 1.0 / np.array(LEVELS)
    rows[3, :6] = HALVES
    rows[4, :6] = 1.0 / np.array(HALVES)
    consts = np.broadcast_to(rows.reshape(80, 1), (80, 128)).astype(np.float32)
    places = np.arange(768)
    down = places // 48 // 4 * 4 + places % 48 // 12
    across = places // 48 % 4 * 4 + places % 48 % 12 // 3
    spots = np.broadcast_to(np.stack([down, across])[:, :, None], (2, 768, 128)).astype(np.float32)
    return jnp.asarray(consts), jnp.asarray(spots)


def on_device(pixels, frame_bounds, clip_frames, codes, *states):
    masters, moments, squares = states[:8], states[8:16], states[16:24]
    frames, band = pixels.shape[:2]
    grp, bands = lax.axis_index("grp"), lax.axis_size("grp")
    me, parts = lax.axis_index("dp"), lax.axis_size("dp")
    shared = parts == SLABS
    positions = frames * 16
    count_all = float(frames * parts * 256)

    code_halos = (passed_along(codes[:, 0], "grp", -1), passed_along(codes[:, band - 1], "grp", 1))
    code_rows = codes.transpose(1, 0, 2).reshape(band, positions).astype(F32)
    counts = count_codes(code_rows)
    xt = turn_pixels(pixels)
    if shared:
        lane_info, slab = frame_lanes(me * frames, clip_frames, frame_bounds, masters)
        slabs = gather_slabs(slab, (counts, None, xt))
    else:
        lane_info, slabs = whole_slabs(me * frames, clip_frames, frame_bounds, masters)
    counts = lax.psum(counts, ("dp", "grp"))
    halos = (passed_along(xt[0], "grp", -1), passed_along(xt[band - 1], "grp", 1))

    places = jnp.stack(
        [grp * band, (grp < bands - 1).astype(jnp.int32), (grp > 0).astype(jnp.int32), me if shared else jnp.int32(0)]
    ).astype(jnp.int32)
    above, under = (item.reshape(1, positions).astype(F32) for item in (code_halos[1], code_halos[0]))
    all_codes = jnp.concatenate([above, code_rows, under], axis=0)
    extra = (all_codes, lane_info, *constants())

    fake_outs = run_fake(xt, places, slabs, extra, count_all)
    halos, counts, fake_outs = lax.optimization_barrier((halos, counts, fake_outs))
    auto, starts = fake_outs[:2], fake_outs[2:7]
    if shared:
        auto_send, auto_keep = auto
        auto_keep, auto_send = hop((auto_keep, swap(auto_send, "dp", 1), False, BF16))
        got = swap(auto_send, "dp", 2)
    judge = run_real(xt, halos, places, slabs, starts, count_all)
    if shared:
        got, judge = lax.optimization_barrier((got, judge))
        auto_total, judge_total = reduce_both(auto_keep, got, *judge)
        totals = (*unpack_auto(auto_total), *unpack_judge_grads(judge_total))
        losses = judge_total[80, 128:131]
    else:
        *totals, losses = whole_grads(auto, judge)

    shares = counts * (1.0 / count_all)
    perplexity = jnp.exp(-jnp.sum(jax.scipy.special.xlogy(shares, shares)))
    results = [
        adamw(
            masters[number],
            moments[number],
            squares[number],
            totals[number],
            RATE_GAIN if number == 3 else RATE_MATRIX,
            0.0 if number == 3 else DECAY,
        )
        for number in range(8)
    ]
    return (
        *(result[0] for result in results),
        *(result[1] for result in results),
        *(result[2] for result in results),
        jnp.stack([losses[0], fake_outs[6][3, 0]]),
        losses[1:3],
        perplexity,
    )


def solution(mesh):
    states = (
        P(None, "dp", None),
        P(None, "dp", None),
        P(None, "dp", None),
        P(None, "dp"),
        P(None, "dp"),
        P("dp", None),
        P(None, "dp"),
        P("dp"),
    )
    return jax.shard_map(
        on_device,
        mesh=mesh,
        in_specs=(P("dp", "grp", None, None), P("dp", None), P(), P("dp", "grp", None)) + states * 3,
        out_specs=states * 3 + (P(), P(), P()),
        check_vma=False,
    )
```

time: 689 us -> 319 us (0.46); the launches traced: 680 us -> 318 us
  blocking collectives: 237 us -> 0 us
  waiting for transfers between devices: 101 us -> 31.2 us
  local copies, waits for them, and re-layouts: 58.9 us -> 14.9 us
  other arithmetic: 33 us -> 13.8 us
  starting transfers between devices: 13.7 us -> 27 us
    all_gather x7 -> x0, blocking collectives: 135 us -> none  [on_device(): lax.all_gather(shard, 'dp', axis=axis, tiled=True)]
    unnamed x4 -> x1, waiting for transfers between devices: 101 us -> 0.02 us
    psum x2 -> x0, blocking collectives: 69.6 us -> none  [the longest x1 39.5 us: on_device(): losses = lax.psum(losses, ('dp', 'grp'))]
    unnamed x1 -> x0, blocking collectives: 32.7 us -> none
    ppermute x0 -> x14, waiting for transfers between devices: none -> 31.2 us  [swap(): lax.ppermute(x, axis, [(i, i ^ bits) for i in range(lax.axis_size(axis))])]
    unnamed x113 -> x72, local copies, waits for them, and re-layouts: 23.6 us -> 6.6 us
    ppermute x0 -> x14, starting transfers between devices: none -> 15.3 us  [swap(): lax.ppermute(x, axis, [(i, i ^ bits) for i in range(lax.axis_size(axis))])]
    reduce_sum x8 -> x3, other arithmetic: 8.13 us -> 0.9 us  [the longest x1 0.67 us: on_device(): perplexity = jnp.exp(-jnp.sum(jax.scipy.special.xlogy(shares, shares)))]
  transfers between devices with their start and end apart: 7 -> 19, of which waited for: 1 -> 8; matrix products, arithmetic and copies ran while one was open for 11% -> 4% of each run, Pallas kernels for 32% -> 63%
where the time goes in v2:
time: 319 us; the launch traced here: 318 us
  Pallas kernels  215 us (67%)
  waiting for transfers between devices  31.2 us (10%)
  starting transfers between devices  27 us (8%)
  between operations  16.3 us (5%)
  local copies, waits for them, and re-layouts  14.9 us (5%)
  other arithmetic  13.8 us (4%)
    pallas_call x1, Pallas kernels, run_fake(): pl.pallas_call(fake_kernel(band, lanes, chunks, count_all), grid=(chunks,...  136 us
    pallas_call x1, Pallas kernels, run_real(): pl.pallas_call(real_kernel(band, lanes, chunks, count_all), grid=(total +...  44 us
    ppermute x14, waiting for transfers between devices, swap(): lax.ppermute(x, axis, [(i, i ^ bits) for i in range(lax.axis_size(axis))])  31.2 us
    pallas_call x1, Pallas kernels, turn_pixels(): pl.pallas_call(turn_kernel, grid=(band, frames // part), in_specs=[pl.Blo...  15.9 us
    ppermute x14, starting transfers between devices, swap(): lax.ppermute(x, axis, [(i, i ^ bits) for i in range(lax.axis_size(axis))])  15.3 us
    ppermute x4, starting transfers between devices, passed_along(): return lax.ppermute(x, axis, pairs)  11.7 us
    pallas_call x5, Pallas kernels, hop(): pl.pallas_call(lambda *refs: hop_kernel(plans, *refs), in_specs=[vmem] *...  11.5 us
    unnamed x72, local copies, waits for them, and re-layouts  6.6 us
  transfers between devices with their start and end apart: 19, of which 8 were waited for; matrix products, arithmetic and copies ran while one was open for 4% of the time, Pallas kernels for 63%

profile of v2, /device:TPU:0, one launch (start us, length us, event | category | flops | bytes accessed | tf_op | source)
XLA Modules:
  0.0 318.2 jit_solution(14297567338832871568)
XLA Ops:
  8.6 1.3 copy.103
  11.4 2.2 frames.1
  13.7 4.0 %collective-permute-start.2 = (bf16[1,240,256]{2,1,0:T(8,128)(2,1)}, bf16[1,240,256]{2,1,0:T(8,128)(2,1)S(1)}, u32[]{:S(2)}, u32[]{:S(2)}) collective-permute-start(bf16[1,240,256]{2,1,0:T(8,128)(2,1)} %bitcast.53), channel_id=1, source_target_pairs={{0,16},{2,18},{4,20},{6,22},{8,24},{10,26},{12,28},{14,30},{16,0},... | collective-permute-start | bytes 368648 | tf_op jit(solution)/shard_map/ppermute | solution.py:783
  19.5 5.3 %count.1 = f32[256,256]{1,0:T(8,128)} custom-call(f32[8,1,1024]{2,1,0:T(1,128)} %convert_element_type.70.codes_ref), custom_call_target="tpu_custom_call" | custom-call | flops 4096000000 | bytes 32768 | tf_op jit(solution)/shard_map/count/pallas_call | solution.py:709
  24.8 1.6 collective-permute-start.3
  26.4 5.8 %collective-permute-done.3 = bf16[2,240,256]{2,1,0:T(8,128)(2,1)S(1)} collective-permute-done((bf16[2,240,256]{2,1,0:T(8,128)(2,1)S(1)}, bf16[2,240,256]{2,1,0:T(8,128)(2,1)S(1)}, u32[]{:S(2)}, u32[]{:S(2)}) %collective-permute-start.3) | collective-permute-done | bytes 245792 | tf_op jit(solution)/shard_map/ppermute | solution.py:783
  32.3 1.6 collective-permute-start.4
  33.9 15.9 %turn.1.refs_3_.refs_4_.refs_5_ = bf16[8,768,1024]{2,1,0:T(8,128)(2,1)} custom-call(bf16[64,8,16,768]{3,2,1,0:T(8,128)(2,1)} %pixels_ref.1), custom_call_target="tpu_custom_call" | custom-call | bytes 25165824 | tf_op jit(solution)/shard_map/turn/pallas_call | solution.py:682
  51.6 3.4 %collective-permute-start.6 = (s32[64,16]{0,1:T(8,128)S(1)}, s32[64,16]{0,1:T(8,128)S(1)}, u32[]{:S(2)}, u32[]{:S(2)}) collective-permute-start(s32[64,16]{0,1:T(8,128)S(1)} %get-tuple-element.207), channel_id=1, source_target_pairs={{0,1},{2,3},{4,5},{6,7},{8,9},{10,11},{12,13},{14,15},{16,17},{18,... | collective-permute-start | bytes 12296 | tf_op jit(solution)/shard_map/ppermute | solution.py:779
  55.0 1.3 collective-permute-start.7
  56.3 2.2 slice_bitcast_fusion
  58.5 5.7 %collective-permute-start.1 = (bf16[768,1024]{1,0:T(8,128)(2,1)S(1)}, bf16[768,1024]{1,0:T(8,128)(2,1)}, u32[]{:S(2)}, u32[]{:S(2)}) collective-permute-start(bf16[768,1024]{1,0:T(8,128)(2,1)S(1)} %get-tuple-element.201), channel_id=1, source_target_pairs={{0,1},{2,3},{4,5},{6,7},{8,9},{10,11},{12,13},{14,15},{16,17},{18,... | collective-permute-start | bytes 4718600 | tf_op jit(solution)/shard_map/ppermute | solution.py:779
  64.2 1.3 collective-permute-start
  67.3 135.9 %judge_fake.1 = (f32[8,192,256]{2,1,0:T(8,128)}, f32[8,192,256]{2,1,0:T(8,128)}, f32[1024,256]{1,0:T(8,128)}, f32[128,256]{1,0:T(8,128)}, f32[192,256]{1,0:T(8,1...) custom-call(s32[4]{0:T(128)} %pad_add_fusion.refs_0_, bf16[8,240,256]{2,1,0:T(8,128)(2,1)} %pad_maximum_fusion.refs_1_, ...), custom_call_target="tpu_custom_call" | custom-call | flops 131072000000 | bytes 25165824 | tf_op jit(solution)/shard_map/judge_fake/pallas_call | solution.py:661
  203.4 3.6 %collective-permute-done.8.refs_1_ = f32[8,192,256]{2,1,0:T(8,128)S(1)} collective-permute-done((f32[8,192,256]{2,1,0:T(8,128)}, f32[8,192,256]{2,1,0:T(8,128)S(1)}, u32[]{:S(2)}, u32[]{:S(2)}) %collective-permute-start.8) | collective-permute-done | bytes 1572896 | tf_op jit(solution)/shard_map/ppermute | solution.py:783
  208.2 3.0 hop.5
  211.7 44.0 %judge_real.1 = (f32[8,96,256]{2,1,0:T(8,128)}, f32[8,96,256]{2,1,0:T(8,128)}) custom-call(s32[4]{0:T(128)} %pad_add_fusion.refs_0_, bf16[8,240,256]{2,1,0:T(8,128)(2,1)} %pad_maximum_fusion.refs_1_, bf16[8,240,256]{2,1,0:T(8,128)(2,1)} %collective-permute-done.5.refs_2_, bf16[8,768,1024]{2,1,0:T(8,128)(2,1)} %turn.1.refs_3_.refs_4_.refs_5_, ...), custom_call_target="tpu_custom_call" | custom-call | flops 44236800000 | bytes 25165824 | tf_op jit(solution)/shard_map/judge_real/pallas_call | solution.py:379
  255.8 2.5 collective-permute-done.10.refs_3_
  259.2 2.8 hop.6
  262.0 1.6 collective-permute-start.11
  263.5 1.5 collective-permute-start.12
  265.0 4.1 %collective-permute-done.11.refs_1_ = bf16[2,192,256]{2,1,0:T(8,128)(2,1)S(1)} collective-permute-done((bf16[2,192,256]{2,1,0:T(8,128)(2,1)}, bf16[2,192,256]{2,1,0:T(8,128)(2,1)S(1)}, u32[]{:S(2)}, u32[]{:S(2)}) %collective-permute-start.11) | collective-permute-done | bytes 196640 | tf_op jit(solution)/shard_map/ppermute | solution.py:783
  269.1 1.3 collective-permute-done.12.refs_3_
  271.1 2.1 hop.7
  273.3 2.2 collective-permute-start.13
  275.8 5.4 %collective-permute-done.14.refs_3_ = bf16[2,96,256]{2,1,0:T(8,128)(2,1)S(1)} collective-permute-done((bf16[2,96,256]{2,1,0:T(8,128)(2,1)}, bf16[2,96,256]{2,1,0:T(8,128)(2,1)S(1)}, u32[]{:S(2)}, u32[]{:S(2)}) %collective-permute-start.14) | collective-permute-done | bytes 98336 | tf_op jit(solution)/shard_map/ppermute | solution.py:783
  281.2 3.2 %collective-permute-done.13.refs_1_ = f32[1,192,256]{2,1,0:T(8,128)S(1)} collective-permute-done((f32[1,192,256]{2,1,0:T(8,128)}, f32[1,192,256]{2,1,0:T(8,128)S(1)}, u32[]{:S(2)}, u32[]{:S(2)}) %collective-permute-start.13) | collective-permute-done | bytes 196640 | tf_op jit(solution)/shard_map/ppermute | solution.py:783
  285.2 2.0 hop.8
  289.9 5.2 %collective-permute-done.16.refs_1_ = f32[1,96,256]{2,1,0:T(8,128)S(1)} collective-permute-done((f32[1,96,256]{2,1,0:T(8,128)}, f32[1,96,256]{2,1,0:T(8,128)S(1)}, u32[]{:S(2)}, u32[]{:S(2)}) %collective-permute-start.16) | collective-permute-done | bytes 98336 | tf_op jit(solution)/shard_map/ppermute | solution.py:783
  296.4 1.6 hop.9
  298.0 1.7 collective-permute-start.17
  305.8 1.9 pad_maximum_fusion.7
  (134 shorter events, 24.5 us)
Async XLA Ops:
  7.2 196.1 %all-reduce.2.cloned.1.call-start = ((), (), s32[]{:S(2)}) async-start(), calls=%async_computation | async-start | bytes 524288 | tf_op jit(solution)/shard_map/psum | solution.py:964
  13.7 11.1 %collective-permute-start.2 = (bf16[1,240,256]{2,1,0:T(8,128)(2,1)}, bf16[1,240,256]{2,1,0:T(8,128)(2,1)S(1)}, u32[]{:S(2)}, u32[]{:S(2)}) collective-permute-start(bf16[1,240,256]{2,1,0:T(8,128)(2,1)} %bitcast.53), channel_id=1, source_target_pairs={{0,16},{2,18},{4,20},{6,22},{8,24},{10,26},{12,28},{14,30},{16,0},... | collective-permute-start | bytes 368648 | tf_op jit(solution)/shard_map/ppermute | solution.py:783
  24.8 7.5 %collective-permute-start.3 = (bf16[2,240,256]{2,1,0:T(8,128)(2,1)S(1)}, bf16[2,240,256]{2,1,0:T(8,128)(2,1)S(1)}, u32[]{:S(2)}, u32[]{:S(2)}) collective-permute-start(bf16[2,240,256]{2,1,0:T(8,128)(2,1)S(1)} %pad_maximum_fusion.2), channel_id=1, source_target_pairs={{0,8},{2,10},{4,12},{6,14},{8,0},{10,2},{12,4},{14,6},{16,24},{18,... | collective-permute-start | bytes 737288 | tf_op jit(solution)/shard_map/ppermute | solution.py:783
  32.3 17.5 %collective-permute-start.4 = (bf16[4,240,256]{2,1,0:T(8,128)(2,1)S(1)}, bf16[4,240,256]{2,1,0:T(8,128)(2,1)S(1)}, u32[]{:S(2)}, u32[]{:S(2)}) collective-permute-start(bf16[4,240,256]{2,1,0:T(8,128)(2,1)S(1)} %pad_maximum_fusion.1), channel_id=1, source_target_pairs={{0,4},{2,6},{4,0},{6,2},{8,12},{10,14},{12,8},{14,10},{16,20},{18,... | collective-permute-start | bytes 1474568 | tf_op jit(solution)/shard_map/ppermute | solution.py:783
  50.9 16.5 %collective-permute-start.5 = (bf16[8,240,256]{2,1,0:T(8,128)(2,1)}, bf16[8,240,256]{2,1,0:T(8,128)(2,1)}, u32[]{:S(2)}, u32[]{:S(2)}) collective-permute-start(bf16[8,240,256]{2,1,0:T(8,128)(2,1)} %pad_maximum_fusion.refs_1_), channel_id=1, source_target_pairs={{0,2},{2,0},{4,6},{6,4},{8,10},{10,8},{12,14},{14,12},{16,18},{18,... | collective-permute-start | bytes 2949128 | tf_op jit(solution)/shard_map/ppermute | solution.py:783
  51.6 14.9 %collective-permute-start.6 = (s32[64,16]{0,1:T(8,128)S(1)}, s32[64,16]{0,1:T(8,128)S(1)}, u32[]{:S(2)}, u32[]{:S(2)}) collective-permute-start(s32[64,16]{0,1:T(8,128)S(1)} %get-tuple-element.207), channel_id=1, source_target_pairs={{0,1},{2,3},{4,5},{6,7},{8,9},{10,11},{12,13},{14,15},{16,17},{18,... | collective-permute-start | bytes 12296 | tf_op jit(solution)/shard_map/ppermute | solution.py:779
  55.0 11.3 %collective-permute-start.7 = (s32[64,16]{0,1:T(8,128)S(1)}, s32[64,16]{0,1:T(8,128)S(1)}, u32[]{:S(2)}, u32[]{:S(2)}) collective-permute-start(s32[64,16]{0,1:T(8,128)S(1)} %get-tuple-element.208), channel_id=1, source_target_pairs={{1,0},{3,2},{5,4},{7,6},{9,8},{11,10},{13,12},{15,14},{17,16},{19,... | collective-permute-start | bytes 12296 | tf_op jit(solution)/shard_map/ppermute | solution.py:779
  58.5 144.8 %collective-permute-start.1 = (bf16[768,1024]{1,0:T(8,128)(2,1)S(1)}, bf16[768,1024]{1,0:T(8,128)(2,1)}, u32[]{:S(2)}, u32[]{:S(2)}) collective-permute-start(bf16[768,1024]{1,0:T(8,128)(2,1)S(1)} %get-tuple-element.201), channel_id=1, source_target_pairs={{0,1},{2,3},{4,5},{6,7},{8,9},{10,11},{12,13},{14,15},{16,17},{18,... | collective-permute-start | bytes 4718600 | tf_op jit(solution)/shard_map/ppermute | solution.py:779
  64.2 139.1 %collective-permute-start = (bf16[768,1024]{1,0:T(8,128)(2,1)S(1)}, bf16[768,1024]{1,0:T(8,128)(2,1)}, u32[]{:S(2)}, u32[]{:S(2)}) collective-permute-start(bf16[768,1024]{1,0:T(8,128)(2,1)S(1)} %get-tuple-element.202), channel_id=1, source_target_pairs={{1,0},{3,2},{5,4},{7,6},{9,8},{11,10},{13,12},{15,14},{17,16},{19,... | collective-permute-start | bytes 4718600 | tf_op jit(solution)/shard_map/ppermute | solution.py:779
  203.3 3.7 %collective-permute-start.8 = (f32[8,192,256]{2,1,0:T(8,128)}, f32[8,192,256]{2,1,0:T(8,128)S(1)}, u32[]{:S(2)}, u32[]{:S(2)}) collective-permute-start(f32[8,192,256]{2,1,0:T(8,128)} %get-tuple-element.86), channel_id=1, source_target_pairs={{0,2},{2,0},{4,6},{6,4},{8,10},{10,8},{12,14},{14,12},{16,18},{18,... | collective-permute-start | bytes 4718600 | tf_op jit(solution)/shard_map/ppermute | solution.py:783
  211.2 44.5 %collective-permute-start.9 = (bf16[4,192,256]{2,1,0:T(8,128)(2,1)}, bf16[4,192,256]{2,1,0:T(8,128)(2,1)S(1)}, u32[]{:S(2)}, u32[]{:S(2)}) collective-permute-start(bf16[4,192,256]{2,1,0:T(8,128)(2,1)} %get-tuple-element.88), channel_id=1, source_target_pairs={{0,4},{2,6},{4,0},{6,2},{8,12},{10,14},{12,8},{14,10},{16,20},{18,... | collective-permute-start | bytes 1179656 | tf_op jit(solution)/shard_map/ppermute | solution.py:783
  255.7 2.6 collective-permute-start.10
  262.0 26.4 %copy-start.5 = (f32[256,256]{1,0:T(8,128)S(1)}, f32[256,256]{1,0:T(8,128)}, u32[]{:S(2)}) copy-start(f32[256,256]{1,0:T(8,128)} %all-reduce.2.cloned.1.call-done) | copy-start | bytes 786436
  262.0 7.2 %collective-permute-start.11 = (bf16[2,192,256]{2,1,0:T(8,128)(2,1)}, bf16[2,192,256]{2,1,0:T(8,128)(2,1)S(1)}, u32[]{:S(2)}, u32[]{:S(2)}) collective-permute-start(bf16[2,192,256]{2,1,0:T(8,128)(2,1)} %get-tuple-element.104), channel_id=1, source_target_pairs={{0,8},{2,10},{4,12},{6,14},{8,0},{10,2},{12,4},{14,6},{16,24},{18,... | collective-permute-start | bytes 589832 | tf_op jit(solution)/shard_map/ppermute | solution.py:783
  263.5 6.9 %collective-permute-start.12 = (bf16[4,96,256]{2,1,0:T(8,128)(2,1)}, bf16[4,96,256]{2,1,0:T(8,128)(2,1)S(1)}, u32[]{:S(2)}, u32[]{:S(2)}) collective-permute-start(bf16[4,96,256]{2,1,0:T(8,128)(2,1)} %get-tuple-element.105), channel_id=1, source_target_pairs={{0,4},{2,6},{4,0},{6,2},{8,12},{10,14},{12,8},{14,10},{16,20},{18,... | collective-permute-start | bytes 589832 | tf_op jit(solution)/shard_map/ppermute | solution.py:783
  271.1 28.7 %copy-start.6 = (f32[4,16,256]{2,1,0:T(8,128)S(1)}, f32[4,16,256]{2,1,0:T(8,128)}, u32[]{:S(2)}) copy-start(f32[4,16,256]{2,1,0:T(8,128)} %matrices.1) | copy-start | bytes 196612
  271.1 28.7 %copy-start.15 = (f32[4,16,256]{2,1,0:T(8,128)S(1)}, f32[4,16,256]{2,1,0:T(8,128)}, u32[]{:S(2)}) copy-start(f32[4,16,256]{2,1,0:T(8,128)} %param.51) | copy-start | bytes 196612
  271.1 28.7 %copy-start.16 = (f32[4,16,256]{2,1,0:T(8,128)S(1)}, f32[4,16,256]{2,1,0:T(8,128)}, u32[]{:S(2)}) copy-start(f32[4,16,256]{2,1,0:T(8,128)} %param.43) | copy-start | bytes 196612
  273.3 27.2 %copy-start.3 = (f32[2,48,256]{2,1,0:T(8,128)S(1)}, f32[2,48,256]{2,1,0:T(8,128)}, u32[]{:S(2)}) copy-start(f32[2,48,256]{2,1,0:T(8,128)} %project.1) | copy-start | bytes 294916
  273.3 27.2 %copy-start.12 = (f32[2,48,256]{2,1,0:T(8,128)S(1)}, f32[2,48,256]{2,1,0:T(8,128)}, u32[]{:S(2)}) copy-start(f32[2,48,256]{2,1,0:T(8,128)} %param.50) | copy-start | bytes 294916
  273.3 27.2 %copy-start.13 = (f32[2,48,256]{2,1,0:T(8,128)S(1)}, f32[2,48,256]{2,1,0:T(8,128)}, u32[]{:S(2)}) copy-start(f32[2,48,256]{2,1,0:T(8,128)} %param.42) | copy-start | bytes 294916
  273.3 11.2 %collective-permute-start.13 = (f32[1,192,256]{2,1,0:T(8,128)}, f32[1,192,256]{2,1,0:T(8,128)S(1)}, u32[]{:S(2)}, u32[]{:S(2)}) collective-permute-start(f32[1,192,256]{2,1,0:T(8,128)} %get-tuple-element.110), channel_id=1, source_target_pairs={{0,16},{2,18},{4,20},{6,22},{8,24},{10,26},{12,28},{14,30},{16,0},... | collective-permute-start | bytes 589832 | tf_op jit(solution)/shard_map/ppermute | solution.py:783
  275.4 5.8 %collective-permute-start.14 = (bf16[2,96,256]{2,1,0:T(8,128)(2,1)}, bf16[2,96,256]{2,1,0:T(8,128)(2,1)S(1)}, u32[]{:S(2)}, u32[]{:S(2)}) collective-permute-start(bf16[2,96,256]{2,1,0:T(8,128)(2,1)} %get-tuple-element.111), channel_id=1, source_target_pairs={{0,8},{2,10},{4,12},{6,14},{8,0},{10,2},{12,4},{14,6},{16,24},{18,... | collective-permute-start | bytes 294920 | tf_op jit(solution)/shard_map/ppermute | solution.py:783
  287.2 8.0 %collective-permute-start.15 = (f32[1,192,256]{2,1,0:T(8,128)}, f32[1,192,256]{2,1,0:T(8,128)S(1)}, u32[]{:S(2)}, u32[]{:S(2)}) collective-permute-start(f32[1,192,256]{2,1,0:T(8,128)} %get-tuple-element.115), channel_id=1, source_target_pairs={{0,1},{1,0},{2,3},{3,2},{4,5},{5,4},{6,7},{7,6},{8,9},{9,8},{10,11... | collective-permute-start | bytes 589832 | tf_op jit(solution)/shard_map/ppermute | solution.py:783
  288.4 6.8 %collective-permute-start.16 = (f32[1,96,256]{2,1,0:T(8,128)}, f32[1,96,256]{2,1,0:T(8,128)S(1)}, u32[]{:S(2)}, u32[]{:S(2)}) collective-permute-start(f32[1,96,256]{2,1,0:T(8,128)} %get-tuple-element.116), channel_id=1, source_target_pairs={{0,16},{2,18},{4,20},{6,22},{8,24},{10,26},{12,28},{14,30},{16,0},... | collective-permute-start | bytes 294920 | tf_op jit(solution)/shard_map/ppermute | solution.py:783
  289.1 19.9 %copy-start.27 = (f32[16]{0:T(128)S(1)}, f32[16]{0:T(128)}, u32[]{:S(2)}) copy-start(f32[16]{0:T(128)} %param.41) | copy-start | bytes 196
  289.1 19.9 %copy-start.32 = (f32[16]{0:T(128)S(1)}, f32[16]{0:T(128)}, u32[]{:S(2)}) copy-start(f32[16]{0:T(128)} %param.57) | copy-start | bytes 196
  289.1 19.9 %copy-start.33 = (f32[16]{0:T(128)S(1)}, f32[16]{0:T(128)}, u32[]{:S(2)}) copy-start(f32[16]{0:T(128)} %param.49) | copy-start | bytes 196
  289.1 20.4 %copy-start.7 = (f32[128,128]{1,0:T(8,128)S(1)}, f32[128,128]{1,0:T(8,128)}, u32[]{:S(2)}) copy-start(f32[128,128]{1,0:T(8,128)} %mid_conv.1) | copy-start | bytes 196612
  289.1 20.4 %copy-start.17 = (f32[128,128]{1,0:T(8,128)S(1)}, f32[128,128]{1,0:T(8,128)}, u32[]{:S(2)}) copy-start(f32[128,128]{1,0:T(8,128)} %param.55) | copy-start | bytes 196612
  289.1 20.4 %copy-start.18 = (f32[128,128]{1,0:T(8,128)S(1)}, f32[128,128]{1,0:T(8,128)}, u32[]{:S(2)}) copy-start(f32[128,128]{1,0:T(8,128)} %param.47) | copy-start | bytes 196612
  298.0 5.7 %collective-permute-start.17 = (f32[1,96,256]{2,1,0:T(8,128)}, f32[1,96,256]{2,1,0:T(8,128)S(1)}, u32[]{:S(2)}, u32[]{:S(2)}) collective-permute-start(f32[1,96,256]{2,1,0:T(8,128)} %hop.9), channel_id=1, source_target_pairs={{0,1},{1,0},{2,3},{3,2},{4,5},{5,4},{6,7},{7,6},{8,9},{9,8},{10,11... | collective-permute-start | bytes 294920 | tf_op jit(solution)/shard_map/ppermute | solution.py:783
  (21 other events, 229.6 us)
Sparse Core Ops, SparseCore 0:
  67.5 127.2 all-reduce.1

commit v3 on v2

--- a/solution.py
+++ b/solution.py
@@ -23,8 +23,10 @@
 VMEM_LIMIT = 60 * 2**20
 FAKE_LANES = 512
 REAL_LANES = 1024
+REAL_PART = 256
 SLABS = 16
 VALUES = (0, 8, 4, 12, 2, 10, 6, 14)
+WINDOWS = (0, 128, 384, 512)
 AUTO_ROWS = 160
 SLAB_ROWS = 240
 AXES = (1, 1, 1, 1, 1, 0, 1, 0)
@@ -78,14 +80,16 @@
     return pl.ds(pl.multiple_of(index * size, size), size)
 
 
-def interleave(*pieces):
-    pieces = list(pieces)
-    while pieces:
-        for piece in list(pieces):
-            try:
-                next(piece)
-            except StopIteration:
-                pieces.remove(piece)
+def interleave(*streams):
+    places = []
+    for index, (stream, count, *span) in enumerate(streams):
+        start, stop = span or (0.0, 1.0)
+        places += [(start + (stop - start) * (piece + 0.5) / count, index) for piece in range(count)]
+    for _, index in sorted(places):
+        next(streams[index][0], None)
+    for stream, *_ in streams:
+        for _ in stream:
+            pass
 
 
 def slab_owners(me, slabs):
@@ -110,18 +114,8 @@
             yield me ^ value ^ core, core, place
 
 
-def scalar_rows(scalars, split):
-    row = lax.broadcasted_iota(jnp.int32, (16, 128), 0)
-    if not split:
-        return jnp.where(row == 0, scalars, 0.0)
-    upper = low(scalars).astype(F32)
-    rest = scalars - upper
-    middle = low(rest).astype(F32)
-    return jnp.where(row == 0, upper, jnp.where(row == 1, middle, jnp.where(row == 2, rest - middle, 0.0)))
-
-
 def prepare_judge(pair_s, misc_s, judge):
-    wmt_s, wmh_s, wlt_s, wlh_s, headw_s, headr_s, bdt_s, bd_s = judge
+    wmt_s, wmh_s, wlt_s, wlh_s, headw_s, headr_s, bdt_s, bd_s, windows_s = judge
     half = jnp.asarray(0.5, BF16)
     for side in range(2):
         columns = pl.ds(side * 128, 128)
@@ -145,50 +139,64 @@
     spread = low(jnp.where(lane == 176 + place % 48, 1.0, 0.0))
     diagonal = (lane // 64) == (place // 48)
     band_t = jnp.where(diagonal, nn(picked, spread), 0.0)
-    bdt_s[...] = low(band_t * 0.5)
-    if bd_s is not None:
+    if bdt_s is not None:
+        bdt_s[...] = low(band_t * 0.5)
         bd_s[...] = low(band_t).T
+    if windows_s is not None:
+        windows_s[...] = jnp.zeros_like(windows_s)
+        windows_s[0, :, 0:192] = low(band_t * 0.5)
+        lane = lax.broadcasted_iota(jnp.int32, (256, 256), 0)
+        place = lax.broadcasted_iota(jnp.int32, (256, 256), 1)
+        spread = low(jnp.where((lane == 176 + (place + 32) % 48) & (place >= 64), 1.0, 0.0))
+        diagonal = (lane // 64) == (place - 64) // 48
+        windows_s[1] = low(jnp.where(diagonal & (place >= 64), nn(picked, spread), 0.0) * 0.5)
 
 
 def judge_scratch(fake):
     shapes = [((256, 1024), BF16), ((1024, 256), BF16), ((256, 128), BF16), ((128, 256), BF16)]
-    shapes += [((256, 128), F32), ((16, 256), BF16), ((256, 192), BF16)]
+    shapes += [((256, 128), F32), ((16, 256), BF16)]
     if fake:
-        shapes += [((192, 256), BF16)]
+        shapes += [((256, 192), BF16), ((192, 256), BF16)]
+    else:
+        shapes += [((2, 256, 256), BF16)]
     return shapes
 
 
-def judge_middle(fresh, q_s, judge, count_all, active, counted, kind, gwl_ref, ghead_ref, loss_ref, new_g2, extra_loss=None):
-    _, _, wlt_s, wlh_s, headw_s, headr_s = judge[:6]
-    lanes = fresh.shape[1]
-    acted_two, slope_two = silu_parts(fresh[:128] + q_s[...])
-    q_s[...] = fresh[128:]
+def judge_middle(part, act, q_s, judge, count_all, active, counted, kind, held, ghead_ref, loss_ref, new_g2):
+    wmt_s, _, wlt_s, wlh_s, headw_s, headr_s = judge[:6]
+    two_s, three_s = held
+    fresh = nn(wmt_s[...], act[:, part])
+    yield
+    acted_two, slope_two = silu_parts(fresh[:128] + q_s[:, part])
+    q_s[:, part] = fresh[128:]
     acted_two = low(acted_two)
+    two_s[:, part] = acted_two * counted.astype(BF16)
     yield
     acted_three, slope_three = silu_parts(nn(wlt_s[...], acted_two))
     acted_three = low(acted_three)
     yield
     score = nn(headr_s[...], acted_three)[:1]
-    shaped = wide(headw_s[...], lanes) * slope_three
+    shaped = wide(headw_s[...], score.shape[1]) * slope_three
+    yield
     if kind == "real":
         grad_score = -jax.nn.sigmoid(1.0 - score) * (active / count_all)
         grad_three = low(grad_score * shaped)
-        loss_ref[0:1, :] += softplus(1.0 - score) * counted
+        three_s[:, part] = grad_three
+        loss_ref[0:1, part] += softplus(1.0 - score) * counted
         yield
-        new_g2[0][...] = low(nn(wlh_s[...], grad_three) * slope_two)
+        new_g2[0][:, part] = low(nn(wlh_s[...], grad_three) * slope_two)
     else:
         pull = jax.nn.sigmoid(1.0 + score)
         grad_score = pull * (active / count_all)
-        grad_three = low(grad_score * shaped)
+        three_s[:, part] = low(grad_score * shaped)
         grad_three_gen = low((-GEN_WEIGHT / count_all * active) * shaped)
-        loss_ref[0:1, :] += softplus(1.0 + score) * counted
-        loss_ref[1:2, :] -= score * counted
+        loss_ref[0:1, part] += softplus(1.0 + score) * counted
+        loss_ref[1:2, part] -= score * counted
         yield
         grad_two_gen = nn(wlh_s[...], grad_three_gen) * slope_two
-        new_g2[0][...] = low(grad_two_gen * (pull * (-1.0 / GEN_WEIGHT)))
-        new_g2[1][...] = low(grad_two_gen)
+        new_g2[0][:, part] = low(grad_two_gen * (pull * (-1.0 / GEN_WEIGHT)))
+        new_g2[1][:, part] = low(grad_two_gen)
     yield
-    gwl_ref[...] += nt(acted_two * counted.astype(BF16), grad_three)
     ghead_ref[...] += fold(acted_three.astype(F32) * (grad_score * counted))
     yield
 
@@ -211,12 +219,13 @@
         start_refs = take(4)
         (fake_loss,) = take(1)
         send_ref, keep_ref = take(2)
-        judge = take(7) + [None]
+        judge = take(6) + [None, None] + take(1)
         pair_s, misc_s = take(2)
-        gwm_ref, gwl_ref, gw1_ref, ghead_ref = take(4)
+        gwm_ref, gwl_ref, gw1_ref, gwin_ref, ghead_ref = take(5)
         q_s, g2, g2_new, act_s, slope_s, small = take(6)
         first_s, lastt_s, loss_ref = take(3)
-        wmt_s, wmh_s, bdt_s = judge[0], judge[1], judge[6]
+        held = take(2)
+        wmt_s, wmh_s, windows_s = judge[0], judge[1], judge[8]
         stage = pl.program_id(0)
         has_below, has_above, me = places[1], places[2].astype(F32), places[3]
         step = lax.rem(stage, rows_n)
@@ -236,12 +245,14 @@
             for ref, start in zip((gwm_ref, gwl_ref, gw1_ref, ghead_ref), start_refs):
                 ref[...] = start[...]
             loss_ref[...] = jnp.zeros_like(loss_ref)
+            gwin_ref[...] = jnp.zeros_like(gwin_ref)
 
         @pl.when(front_ok & (step == 0) & (has_below > 0))
         def below():
             joined = jnp.zeros((128, lanes), F32)
             for group in range(4):
-                acted, _ = silu_parts(nn(bdt_s[...], xbelow[192 * group : 192 * group + 192, :]))
+                x = xbelow[:, :, WINDOWS[group] : WINDOWS[group] + 256].reshape(lanes, 256)
+                acted, _ = silu_parts(nt(windows_s[group % 2], x))
                 joined = joined + nn(wmt_s[128:256, 256 * group : 256 * group + 256], low(acted))
             q_s[...] = joined
 
@@ -255,7 +266,7 @@
                 for start in range(0, lanes, 256):
                     part = slice(start, start + 256)
                     small[rows, part] = low(nn(wmh_s[rows, :], g2[:, part]) * slope[rows, part])
-                yield
+                    yield
 
         def back_middle():
             for group in range(4):
@@ -265,48 +276,58 @@
 
         def back_first():
             for group in range(4):
-                gw1_ref[...] += nt(xe[0, 192 * group : 192 * group + 192, :], small[256 * group : 256 * group + 256, :])
+                x = xe[:, 0, :, WINDOWS[group] : WINDOWS[group] + 256].reshape(lanes, 256)
+                gwin_ref[group % 2] += nn(small[256 * group : 256 * group + 256, :], x)
                 yield
 
         def front_first():
             for group in range(4):
                 for start in range(0, lanes, 256):
                     part = slice(start, start + 256)
-                    rows = slice(192 * group, 192 * group + 192)
-                    x = jnp.where(halo, xabove[rows, part], xf[0, rows, part])
-                    acted, slope_new = silu_parts(nn(bdt_s[...], x))
+                    some, window = slice(start // 16, start // 16 + 16), slice(WINDOWS[group], WINDOWS[group] + 256)
+                    x = jnp.where(halo, xabove[some, :, window], xf[some, 0, :, window]).reshape(256, 256)
+                    acted, slope_new = silu_parts(nt(windows_s[group % 2], x))
                     act[256 * group : 256 * group + 256, part] = low(acted)
                     slope[256 * group : 256 * group + 256, part] = slope_new
-                yield
-
-        def front_middle():
-            fresh = nn(wmt_s[...], act[...])
-            yield
-            yield from judge_middle(
-                fresh, q_s, judge, count_all, active, counted, "real", gwl_ref, ghead_ref, loss_ref, (g2_new,)
+                    yield
+
+        def front_middle(part):
+            return judge_middle(
+                part, act, q_s, judge, count_all, active, counted, "real", held, ghead_ref, loss_ref, (g2_new,)
             )
+
+        def front_last():
+            gwl_ref[...] += nt(held[0][...], held[1][...])
+            yield
 
         def shift():
             g2[0:128, :] = g2[128:256, :]
             g2[128:256, :] = g2_new[...]
 
+        parts = [slice(start, start + REAL_PART) for start in range(0, lanes, REAL_PART)]
+
         @pl.when(front_ok & back_ok)
         def both():
-            interleave(back_small())
-            interleave(back_middle(), front_first())
-            interleave(front_middle(), back_first())
+            interleave(
+                (back_small(), lanes // 64, 0.0, 0.8),
+                (back_middle(), 4, 0.0, 0.8),
+                (front_first(), lanes // 64, 0.2, 1.0),
+            )
+            interleave(*((front_middle(part), 7) for part in parts), (back_first(), 4))
+            interleave((front_last(), 1))
             shift()
 
         @pl.when(front_ok & jnp.logical_not(back_ok))
         def front_only():
-            interleave(front_first())
-            interleave(front_middle())
+            interleave((front_first(), 1))
+            interleave(*((front_middle(part), 7) for part in parts))
+            interleave((front_last(), 1))
             shift()
 
         @pl.when(jnp.logical_not(front_ok) & back_ok)
         def back_only():
-            interleave(back_small())
-            interleave(back_first(), back_middle())
+            interleave((back_small(), 1))
+            interleave((back_first(), 4), (back_middle(), 4))
 
         @pl.when(stage == total)
         def write():
@@ -318,6 +339,16 @@
             place = lax.broadcasted_iota(jnp.int32, (192, 128), 0) % 48
             folding = jnp.where(place == lax.broadcasted_iota(jnp.int32, (192, 128), 1), 1.0, 0.0)
             first = jnp.dot(summed, folding, precision=HIGHEST, preferred_element_type=F32)
+            lane = lax.broadcasted_iota(jnp.int32, (64, 256), 1)
+            place = lax.broadcasted_iota(jnp.int32, (256, 128), 0)
+            for odd in range(2):
+                summed = jnp.zeros((64, 256), F32)
+                for block in range(4):
+                    start = 64 * odd + 48 * block
+                    inside = (lane >= start) & (lane < start + 48)
+                    summed = summed + jnp.where(inside, gwin_ref[odd, 64 * block : 64 * block + 64, :], 0.0)
+                folding = jnp.where((place + 32 * odd) % 48 == lax.broadcasted_iota(jnp.int32, (256, 128), 1), 1.0, 0.0)
+                first = first + jnp.dot(summed, folding, precision=HIGHEST, preferred_element_type=F32)
             for owner in range(SLABS):
                 first_s[16 * owner : 16 * owner + 16, :] = jnp.zeros((16, 128), F32)
                 first_s[16 * owner : 16 * owner + 4, :] = first[4 * owner : 4 * owner + 4, :]
@@ -339,43 +370,35 @@
                 target[chip, 64:80, 0:128] = ghead_ref[own, :]
                 target[chip, 64:80, 128:256] = lastt_s[own, :]
                 target[chip, 80:96, 0:128] = first_s[own, :]
-                target[chip, 80:96, 128:256] = scalar_rows(scalars, False)
+                target[chip, 80:96, 128:256] = jnp.where(lax.broadcasted_iota(jnp.int32, (16, 128), 0) < 3, scalars, 0.0)
 
     return kernel
 
 
-def run_real(xt, halos, places, slabs, starts, count_all):
-    band, _, positions = xt.shape
+def run_real(pixels, halos, places, slabs, starts, count_all):
+    frames, band = pixels.shape[:2]
+    positions = frames * 16
     lanes = min(REAL_LANES, positions)
     chunks = positions // lanes
     rows_n = band + 1
     total = chunks * rows_n
 
-    def front_row(t):
-        t = jnp.minimum(t, total - 1)
-        return (jnp.maximum(band - 1 - lax.rem(t, rows_n), 0), 0, t // rows_n)
-
-    def back_row(t):
-        t = jnp.maximum(t - 2, 0)
-        return (jnp.maximum(band - 1 - lax.rem(t, rows_n), 0), 0, t // rows_n)
-
-    def halo_row(t):
-        return (0, jnp.minimum(t, total - 1) // rows_n)
-
+    halo_spec = pl.BlockSpec((lanes // 16, 16, 768), lambda t: (jnp.minimum(t, total - 1) // rows_n, 0, 0))
     specs = [pl.BlockSpec(memory_space=pltpu.SMEM)]
     specs += [pl.BlockSpec((SLABS // 2, 80, 256), lambda t: (0, 2, 0))] * 2
-    specs += [pl.BlockSpec((1, 768, lanes), front_row), pl.BlockSpec((1, 768, lanes), back_row)]
-    specs += [pl.BlockSpec((768, lanes), halo_row)] * 2
+    specs += stage_rows(band, lanes, chunks)
+    specs += [halo_spec] * 2
     specs += [pl.BlockSpec(item.shape, lambda t: (0, 0)) for item in starts]
     outs = [
         jax.ShapeDtypeStruct((SLABS // 2, 96, 256), F32),
         jax.ShapeDtypeStruct((SLABS // 2, 96, 256), F32),
     ]
     scratch = judge_scratch(False) + [((2, 1024, 128), BF16), ((256, 256), BF16)]
-    scratch += [((1024, 256), F32), ((128, 256), F32), ((192, 256), F32), ((256, 128), F32)]
+    scratch += [((1024, 256), F32), ((128, 256), F32), ((192, 256), F32), ((2, 256, 256), F32), ((256, 128), F32)]
     scratch += [((128, lanes), F32), ((256, lanes), BF16), ((128, lanes), BF16)]
     scratch += [((2, 1024, lanes), BF16), ((2, 1024, lanes), F32), ((1024, lanes), BF16)]
     scratch += [((256, 128), F32), ((256, 128), F32), ((8, lanes), F32)]
+    scratch += [((128, lanes), BF16), ((256, lanes), BF16)]
     return pl.pallas_call(
         real_kernel(band, lanes, chunks, count_all),
         grid=(total + 1,),
@@ -386,32 +409,23 @@
         compiler_params=pltpu.CompilerParams(vmem_limit_bytes=VMEM_LIMIT),
         cost_estimate=cost(5.4e6 * band * positions, 3072 * band * positions),
         name="judge_real",
-    )(places, *slabs, xt, xt, *halos, *starts)
-
-
-def block_forward(stream, gain, first_half_t, second_t):
+    )(places, *slabs, pixels, pixels, *halos, *starts)
+
+
+def block_steps(stream, gain, first_half_t, second_t):
     scaling, normal = norm_parts(stream)
     normed = low(normal * gain)
-    acted, slope = silu_parts(nn(first_half_t, normed))
+    yield None
+    acted, slope = silu_parts(nn(first_half_t[...], normed))
     acted = low(acted)
-    return stream + nn(second_t, acted), (scaling, normal, normed, acted, slope)
-
-
-def block_backward(grad_out, saved, gain, first, second_half, grad_first, grad_second, grad_gain):
-    scaling, normal, normed, acted, slope = saved
-    grad_low = low(grad_out)
-    grad_second[...] += nt(acted, grad_low)
-    grad_inside = low(nn(second_half, grad_low) * slope)
-    grad_first[...] += nt(normed, grad_inside)
-    grad_normed = nn(first, grad_inside)
-    along = grad_normed * normal
-    grad_gain[...] += fold(along)
-    mean = jnp.mean(along * gain, axis=0, keepdims=True)
-    return grad_out + scaling * (grad_normed * gain - normal * mean)
+    yield None
+    yield stream + nn(second_t[...], acted), (scaling, normal, normed, acted, slope)
 
 
 def fake_kernel(band, lanes, chunks, count_all):
-    names = ("fake", "gl1", "act", "slope", "normal", "scaling", "normed", "acted", "bslope", "outlow", "values")
+    rows_n = band + 1
+    total = chunks * rows_n
+    halves = [slice(start, start + 256) for start in range(0, lanes, 256)]
 
     def kernel(*refs):
         refs = list(refs)
@@ -423,22 +437,34 @@
 
         (places,) = take(1)
         slabs = take(2)
-        xc_ref, xa_ref, xb_ref, codes_ref, lane_ref, consts_ref, spots_ref = take(7)
+        xf_ref, xe_ref, codes_ref, lane_ref, consts_ref, spots_ref = take(6)
         send_ref, keep_ref, gwm_ref, gwl_ref, gw1_ref, ghead_ref, loss_ref = take(7)
-        judge = take(8)
+        judge = take(8) + [None]
         pair_s, misc_s = take(2)
         proj_s, projt_s, block_s, blockt_s, blockh_s, fsq_s, fsqt_s, gains_s, total_s = take(9)
-        gproj_ref, gblocks_ref, gfsq_ref, ggains_ref = take(4)
-        q_s, g2_disc, g2_gen, new_disc, new_gen, small_s, smallgen_s, gradlow_s = take(8)
-        stash_a = dict(zip(names, take(len(names))))
-        stash_b = dict(zip(names, take(len(names))))
+        gproj_ref, gprojt_ref, gblocks_ref, gfsq_ref, gfsqt_ref, ggains_ref = take(6)
+        q_s, g2_disc, g2_gen, new_disc, new_gen, small_s, smallgen_s, gradlow_s, xt_s = take(9)
+        fake_s, gl1_s, act_s, slope_s = take(4)
+        saved_s = take(5)
+        outlow_s, values_s = take(2)
+        encoded_s = take(7)
+        outer_s, inner_s, start_s, latent_s, stream_s = take(5)
+        held = take(2)
         wmt_s, wmh_s, bdt_s, bd_s = judge[0], judge[1], judge[6], judge[7]
-        chunk, step = pl.program_id(0), pl.program_id(1)
-        last_step = band // 2
+        stage = pl.program_id(0)
         row_start, has_below, me = places[0], places[1], places[3]
         has_above = places[2].astype(F32)
-
-        @pl.when((chunk == 0) & (step == 0))
+        step = lax.rem(stage, rows_n)
+        row = band - 1 - step
+        slot, slot_three, back_three = lax.rem(stage, 2), lax.rem(stage, 3), lax.rem(stage + 1, 3)
+        back_ok = (stage >= 2) & (lax.rem(stage - 2, rows_n) != band)
+        front_ok = stage < total
+        gl1, act, slope = gl1_s.at[slot], act_s.at[slot], slope_s.at[slot]
+        fake, fake_back = fake_s.at[slot_three], fake_s.at[back_three]
+        counted = jnp.where(row >= 0, 1.0, 0.0)
+        active = jnp.where(row >= 0, 1.0, has_above)
+
+        @pl.when(stage == 0)
         def prepare():
             unpack_judge(me, slabs, pair_s, misc_s, AUTO_ROWS)
             prepare_judge(pair_s, misc_s, judge)
@@ -465,7 +491,7 @@
             lane = lax.broadcasted_iota(jnp.int32, (256, 128), 1)
             held = (lane >= 96) & (lane < 99)
             total_s[...] = jnp.broadcast_to(jnp.sum(jnp.where(held, tail.astype(F32), 0.0)), (8, 128))
-            for ref in (gwm_ref, gwl_ref, gw1_ref, ghead_ref, loss_ref, gproj_ref, gblocks_ref, gfsq_ref, ggains_ref):
+            for ref in (gwm_ref, gwl_ref, gw1_ref, ghead_ref, loss_ref, gproj_ref, gprojt_ref, gblocks_ref, gfsqt_ref, ggains_ref):
                 ref[...] = jnp.zeros_like(ref)
 
         def latent_values(row):
@@ -476,123 +502,247 @@
             digit = turn - level * jnp.floor((turn + 0.5) * wide(consts[32:48], lanes))
             return low((digit - wide(consts[48:64], lanes)) * wide(consts[64:80], lanes))
 
-        def front(row, x_ref, stash):
-            values = latent_values(row)
-            stash["values"][...] = values
-            gain = wide(gains_s[1], lanes)
-            output, saved = block_forward(nn(fsq_s[1], values), gain, blockt_s[2], blockt_s[3])
-            outlow = low(output)
-            stash["outlow"][...] = outlow
-            for name, item in zip(("scaling", "normal", "normed", "acted", "bslope"), saved):
-                stash[name][...] = item
+        @pl.when(front_ok & (step == 0) & (has_below > 0))
+        def below():
+            values = latent_values(jnp.int32(band))
+            outputs = list(block_steps(nn(fsq_s[1], values), wide(gains_s[1], lanes), blockt_s.at[2], blockt_s.at[3]))
+            outlow = low(outputs[-1][0])
+            joined = jnp.zeros((128, lanes), F32)
+            for group in range(4):
+                recon = low(nn(proj_s[1, pl.ds(group * 192, 192), :], outlow))
+                acted, _ = silu_parts(nn(bdt_s[...], recon))
+                joined = joined + nn(wmt_s[128:256, 256 * group : 256 * group + 256], low(acted))
+            q_s[...] = joined
+
+        @pl.when(front_ok & (step == 0) & (has_below == 0))
+        def edge():
+            q_s[...] = jnp.zeros_like(q_s)
+
+        def front_block(part):
+            values = values_s[slot_three, :, part]
+            width = values.shape[1]
+            stream = nn(fsq_s[1], values)
+            yield
+            result = None
+            for result in block_steps(stream, wide(gains_s[1], width), blockt_s.at[2], blockt_s.at[3]):
+                yield
+            output, saved = result
+            outlow_s[slot_three, :, part] = low(output)
+            for ref, item in zip(saved_s, saved):
+                ref[slot_three, :, part] = item
+            yield
+
+        def front_turn():
+            for part in halves:
+                some = slice(part.start // 16, part.stop // 16)
+                for column in range(0, 768, 256):
+                    xt_s[column : column + 256, part] = xf_ref[some, 0, :, column : column + 256].reshape(256, 256).T
+                    yield
+
+        def front_recon():
             lane = lax.broadcasted_iota(jnp.int32, (1, lanes), 1)
             column = (lane % 16).astype(F32)
             place = (row_start + row).astype(F32)
             high = lane_ref[0:1, :] - 16.0 * place
             broad = lane_ref[1:2, :] - 16.0 * column
-            counted = jnp.where(row >= 0, 1.0, 0.0)
-            active = jnp.where(row >= 0, 1.0, has_above)
             weight = lane_ref[2:3, :] * counted
             weight_share = weight / wide(total_s[0:1, :], lanes)
-            l1_sum = jnp.zeros((1, lanes), F32)
-            for group in range(4):
-                rows = pl.ds(group * 192, 192)
-                recon = nn(proj_s[1, rows, :], outlow)
-                stash["fake"][rows, :] = low(recon)
-                diff = recon - x_ref[0, rows, :].astype(F32)
-                square = diff * diff + 1.0
-                inverse = lax.rsqrt(square)
-                inside = (wide(spots_ref[0, rows, :], lanes) < high) & (wide(spots_ref[1, rows, :], lanes) < broad)
-                l1_sum = l1_sum + jnp.sum(jnp.where(inside, square * inverse, 0.0), axis=0, keepdims=True)
-                stash["gl1"][rows, :] = jnp.where(inside, diff * inverse, 0.0) * weight_share
-            loss_ref[2:3, :] += l1_sum * weight
-            for group in range(4):
-                rows, wide_rows = pl.ds(group * 192, 192), pl.ds(group * 256, 256)
-                acted, slope = silu_parts(nn(bdt_s[...], stash["fake"][rows, :]))
-                stash["act"][wide_rows, :] = low(acted)
-                stash["slope"][wide_rows, :] = slope
-            fresh = nn(wmt_s[...], stash["act"][...])
-            for _ in judge_middle(
-                fresh, q_s, judge, count_all, active, counted, "fake", gwl_ref, ghead_ref, loss_ref, (new_disc, new_gen)
+            sums = [jnp.zeros((1, 256), F32) for _ in halves]
+            for group in range(4):
+                rows = slice(group * 192, group * 192 + 192)
+                for index, part in enumerate(halves):
+                    recon = nn(proj_s[1, rows, :], outlow_s[slot_three, :, part])
+                    fake[rows, part] = low(recon)
+                    diff = recon - xt_s[rows, part].astype(F32)
+                    square = diff * diff + 1.0
+                    inside = (wide(spots_ref[0, rows, :], 256) < high[:, part]) & (
+                        wide(spots_ref[1, rows, :], 256) < broad[:, part]
+                    )
+                    share = lax.rsqrt(square) * jnp.where(inside, weight_share[:, part], 0.0)
+                    gl1[rows, part] = diff * share
+                    sums[index] = sums[index] + jnp.sum(square * share, axis=0, keepdims=True)
+                    yield
+            loss_ref[2:3, :] += jnp.concatenate(sums, axis=1) * wide(total_s[0:1, :], lanes)
+
+        def front_first():
+            for group in range(4):
+                for part in halves:
+                    acted, slope_new = silu_parts(nn(bdt_s[...], fake[192 * group : 192 * group + 192, part]))
+                    act[256 * group : 256 * group + 256, part] = low(acted)
+                    slope[256 * group : 256 * group + 256, part] = slope_new
+                    yield
+
+        def front_middle(part):
+            return judge_middle(
+                part, act, q_s, judge, count_all, active, counted, "fake", held, ghead_ref, loss_ref, (new_disc, new_gen)
+            )
+
+        def front_last():
+            gwl_ref[...] += nt(held[0][...], held[1][...])
+            yield
+
+        def back_gen():
+            for group in range(4):
+                rows = slice(256 * group, 256 * group + 256)
+                for part in halves:
+                    smallgen_s[rows, part] = low(nn(wmh_s[rows, :], g2_gen[:, part]) * slope[rows, part])
+                    yield
+
+        def back_disc():
+            for group in range(4):
+                rows = slice(256 * group, 256 * group + 256)
+                for part in halves:
+                    small_s[rows, part] = low(nn(wmh_s[rows, :], g2_disc[:, part]) * slope[rows, part])
+                    yield
+
+        def back_recon():
+            for group in range(4):
+                rows = slice(group * 192, group * 192 + 192)
+                gradlow_s[rows, :] = low(gl1[rows, :] + nn(bd_s[...], smallgen_s[256 * group : 256 * group + 256, :]))
+                yield
+
+        def back_first():
+            for group in range(4):
+                rows = slice(group * 192, group * 192 + 192)
+                gw1_ref[...] += nt(fake_back[rows, :], small_s[256 * group : 256 * group + 256, :])
+                yield
+
+        def back_middle():
+            for group in range(4):
+                rows = slice(256 * group, 256 * group + 256)
+                gwm_ref[rows, :] += nt(act[rows, :], g2_disc[...])
+                yield
+
+        def back_project():
+            for group in range(4):
+                rows = slice(group * 192, group * 192 + 192)
+                gproj_ref[1, rows, :] += nt(gradlow_s[rows, :], outlow_s[back_three])
+                yield
+
+        def back_encode(part):
+            some = slice(part.start // 16, part.stop // 16)
+            stream = nt(projt_s[0], xe_ref[some].reshape(part.stop - part.start, 768))
+            yield
+            result = None
+            for result in block_steps(
+                stream, wide(gains_s[0], part.stop - part.start), blockt_s.at[0], blockt_s.at[1]
             ):
-                pass
-            g2_disc[128:256, :] = new_disc[...]
-            g2_gen[128:256, :] = new_gen[...]
-
-        def below():
-            values = latent_values(jnp.int32(band))
-            output, _ = block_forward(nn(fsq_s[1], values), wide(gains_s[1], lanes), blockt_s[2], blockt_s[3])
-            outlow = low(output)
-            joined = jnp.zeros((128, lanes), F32)
-            for group in range(4):
-                recon = low(nn(proj_s[1, pl.ds(group * 192, 192), :], outlow))
-                acted, _ = silu_parts(nn(bdt_s[...], recon))
-                joined = joined + nn(wmt_s[128:256, 256 * group : 256 * group + 256], low(acted))
-            q_s[...] = joined
-
-        def finish(x_ref, stash):
-            for group in range(4):
-                wide_rows = pl.ds(group * 256, 256)
-                slope = stash["slope"][wide_rows, :]
-                smallgen_s[wide_rows, :] = low(nn(wmh_s[wide_rows, :], g2_gen[...]) * slope)
-                small_s[wide_rows, :] = low(nn(wmh_s[wide_rows, :], g2_disc[...]) * slope)
-            for group in range(4):
-                rows, wide_rows = pl.ds(group * 192, 192), pl.ds(group * 256, 256)
-                gradlow_s[rows, :] = low(stash["gl1"][rows, :] + nn(bd_s[...], smallgen_s[wide_rows, :]))
-            gain = wide(gains_s[1], lanes)
-            saved = tuple(stash[name][...] for name in ("scaling", "normal", "normed", "acted", "bslope"))
-            grad_output = nn(projt_s[1], gradlow_s[...])
-            for group in range(4):
-                rows, wide_rows = pl.ds(group * 192, 192), pl.ds(group * 256, 256)
-                gw1_ref[...] += nt(stash["fake"][rows, :], small_s[wide_rows, :])
-                gwm_ref[wide_rows, :] += nt(stash["act"][wide_rows, :], g2_disc[...])
-                gproj_ref[1, rows, :] += nt(gradlow_s[rows, :], stash["outlow"][...])
-            grad_start = block_backward(
-                grad_output, saved, gain, block_s[2], blockh_s[1],
-                gblocks_ref.at[2], gblocks_ref.at[3], ggains_ref.at[1],
+                yield
+            middle, saved = result
+            middle_low = low(middle)
+            for ref, item in zip(encoded_s, (*saved, middle_low, nn(fsqt_s[0], middle_low))):
+                ref[:, part] = item
+            yield
+
+        def back_block(grad_out, saved, index, part):
+            scaling, normal, slope_in = saved
+            gain = wide(gains_s[index], part.stop - part.start)
+            outer = low(grad_out)
+            outer_s[index, :, part] = outer
+            grad_acted = nn(blockh_s[index], outer)
+            yield None
+            inner = low(grad_acted * slope_in)
+            inner_s[index, :, part] = inner
+            grad_normed = nn(block_s[2 * index], inner)
+            yield None
+            along = grad_normed * normal
+            ggains_ref[index] += fold(along)
+            mean = jnp.mean(along * gain, axis=0, keepdims=True)
+            yield grad_out + scaling * (grad_normed * gain - normal * mean)
+
+        def back_chain(part):
+            grad_out = nn(projt_s[1], gradlow_s[:, part])
+            yield
+            saved = tuple(saved_s[n][back_three, :, part] for n in (0, 1, 4))
+            grad_start = None
+            for grad_start in back_block(grad_out, saved, 1, part):
+                yield
+            start_low = low(grad_start)
+            start_s[:, part] = start_low
+            grad_values = nn(fsqt_s[1], start_low)
+            yield
+            tangent = jnp.tanh(encoded_s[6][:, part])
+            grad_latent = low(grad_values * (1.0 - tangent * tangent))
+            latent_s[:, part] = grad_latent
+            grad_middle = nn(fsq_s[0], grad_latent)
+            yield
+            saved = tuple(encoded_s[n][:, part] for n in (0, 1, 4))
+            grad_stream = None
+            for grad_stream in back_block(grad_middle, saved, 0, part):
+                yield
+            stream_s[:, part] = low(grad_stream)
+            yield
+
+        def back_weights():
+            gblocks_ref[3] += nt(saved_s[3][back_three], outer_s[1])
+            yield
+            gblocks_ref[2] += nt(saved_s[2][back_three], inner_s[1])
+            yield
+            gfsqt_ref[1] += nt(values_s[back_three], start_s[...])
+            gfsqt_ref[0] += nt(latent_s[...], encoded_s[5][...])
+            yield
+            gblocks_ref[1] += nt(encoded_s[3][...], outer_s[0])
+            yield
+            gblocks_ref[0] += nt(encoded_s[2][...], inner_s[0])
+            yield
+            for start in range(0, 768, 256):
+                x = xe_ref[:, 0, :, start : start + 256].reshape(lanes, 256)
+                gprojt_ref[:, start : start + 256] += nn(stream_s[...], x)
+                yield
+
+        def shift():
+            for ref, new in ((g2_disc, new_disc), (g2_gen, new_gen)):
+                ref[0:128, :] = ref[128:256, :]
+                ref[128:256, :] = new[...]
+
+        @pl.when(front_ok & back_ok)
+        def both():
+            values_s[slot_three] = latent_values(row)
+            interleave(
+                (back_gen(), 4 * len(halves)),
+                *((front_block(part), 5) for part in halves),
+                *((back_encode(part), 5) for part in halves),
+                (front_turn(), 6),
             )
-            start_low = low(grad_start)
-            gfsq_ref[1] += nt(start_low, stash["values"][...])
-            grad_values = nn(fsqt_s[1], start_low)
-            gain = wide(gains_s[0], lanes)
-            stream = nn(projt_s[0], x_ref[0])
-            middle, saved = block_forward(stream, gain, blockt_s[0], blockt_s[1])
-            middle_low = low(middle)
-            tangent = jnp.tanh(nn(fsqt_s[0], middle_low))
-            grad_latent = low(grad_values * (1.0 - tangent * tangent))
-            gfsq_ref[0] += nt(middle_low, grad_latent)
-            grad_stream = block_backward(
-                nn(fsq_s[0], grad_latent), saved, gain, block_s[0], blockh_s[0],
-                gblocks_ref.at[0], gblocks_ref.at[1], ggains_ref.at[0],
+            interleave(
+                (back_recon(), 4, 0.0, 0.8), (back_disc(), 4 * len(halves)), (front_recon(), 4 * len(halves), 0.2, 1.0)
             )
-            gproj_ref[0] += nt(x_ref[0], low(grad_stream))
-            for ref in (g2_disc, g2_gen):
-                ref[0:128, :] = ref[128:256, :]
-
-        @pl.when((step == 0) & (has_below > 0))
-        def halo():
-            below()
-
-        @pl.when((step == 0) & (has_below == 0))
-        def edge():
-            q_s[...] = jnp.zeros_like(q_s)
-
-        @pl.when(step == 0)
-        def first():
-            front(jnp.int32(band - 1), xa_ref, stash_a)
-            for ref in (g2_disc, g2_gen):
-                ref[0:128, :] = ref[128:256, :]
-
-        @pl.when(step > 0)
-        def main():
-            front(band - 2 * step, xa_ref, stash_b)
-            finish(xc_ref, stash_a)
-            front(band - 2 * step - 1, xb_ref, stash_a)
-            finish(xa_ref, stash_b)
-
-        @pl.when((chunk == chunks - 1) & (step == last_step))
+            interleave(
+                *((back_chain(part), 10) for part in halves),
+                (back_middle(), 4, 0.0, 0.8),
+                (front_first(), 4 * len(halves), 0.2, 1.0),
+                (back_first(), 4),
+                (back_project(), 4),
+            )
+            interleave(*((front_middle(part), 7) for part in halves), (back_weights(), 8))
+            interleave((front_last(), 1))
+            shift()
+
+        @pl.when(front_ok & jnp.logical_not(back_ok))
+        def front_only():
+            values_s[slot_three] = latent_values(row)
+            interleave(*((front_block(part), 5) for part in halves), (front_turn(), 6))
+            interleave((front_recon(), 1))
+            interleave((front_first(), 1))
+            interleave(*((front_middle(part), 7) for part in halves))
+            interleave((front_last(), 1))
+            shift()
+
+        @pl.when(jnp.logical_not(front_ok) & back_ok)
+        def back_only():
+            interleave((back_gen(), 4 * len(halves)), *((back_encode(part), 5) for part in halves))
+            interleave((back_recon(), 4), (back_disc(), 4 * len(halves)))
+            interleave(
+                *((back_chain(part), 10) for part in halves), (back_middle(), 4), (back_first(), 4), (back_project(), 4)
+            )
+            interleave((back_weights(), 1))
+
+        @pl.when(stage == total)
         def write():
             loss_ref[3:4, 0:128] = total_s[0:1, :]
+            gproj_ref[0] = gprojt_ref[...].T
+            for index in range(2):
+                gfsq_ref[index] = gfsqt_ref[index].T
             for owner, core, chip in slab_targets(me):
                 rows, own = aligned(owner, 48), aligned(owner, 16)
                 target = (keep_ref, send_ref)[core]
@@ -609,31 +759,40 @@
     return kernel
 
 
-def run_fake(xt, places, slabs, extra, count_all):
-    band, _, positions = xt.shape
+def stage_rows(band, lanes, chunks):
+    rows_n = band + 1
+    total = chunks * rows_n
+
+    def front(t):
+        t = jnp.minimum(t, total - 1)
+        return (t // rows_n, jnp.maximum(band - 1 - lax.rem(t, rows_n), 0), 0, 0)
+
+    def back(t):
+        t = jnp.maximum(t - 2, 0)
+        return (t // rows_n, jnp.maximum(band - 1 - lax.rem(t, rows_n), 0), 0, 0)
+
+    block = (lanes // 16, 1, 16, 768)
+    return pl.BlockSpec(block, front), pl.BlockSpec(block, back)
+
+
+def run_fake(pixels, places, slabs, extra, count_all):
+    frames, band = pixels.shape[:2]
+    positions = frames * 16
     lanes = min(FAKE_LANES, positions)
     chunks = positions // lanes
+    total = chunks * (band + 1)
     codes, lane_info, consts, spots = extra
 
     def whole(array):
-        return pl.BlockSpec(array.shape, lambda c, s: (0,) * array.ndim)
-
-    def row_spec(shift):
-        def index(c, s):
-            row = jnp.where(s == 0, band - 1, band - 2 * s + shift)
-            return (jnp.maximum(row, 0), 0, c)
-
-        return pl.BlockSpec((1, 768, lanes), index)
+        return pl.BlockSpec(array.shape, lambda t: (0,) * array.ndim)
+
+    def chunk_spec(array):
+        return pl.BlockSpec((array.shape[0], lanes), lambda t: (0, jnp.minimum(t, total - 1) // (band + 1)))
 
     specs = [pl.BlockSpec(memory_space=pltpu.SMEM)]
     specs += [whole(item) for item in slabs]
-    specs += [row_spec(1), row_spec(0), row_spec(-1)]
-    specs += [
-        pl.BlockSpec((codes.shape[0], lanes), lambda c, s: (0, c)),
-        pl.BlockSpec((lane_info.shape[0], lanes), lambda c, s: (0, c)),
-        whole(consts),
-        whole(spots),
-    ]
+    specs += stage_rows(band, lanes, chunks)
+    specs += [chunk_spec(codes), chunk_spec(lane_info), whole(consts), whole(spots)]
     outs = [
         jax.ShapeDtypeStruct((SLABS // 2, 192, 256), F32),
         jax.ShapeDtypeStruct((SLABS // 2, 192, 256), F32),
@@ -642,53 +801,27 @@
     scratch = judge_scratch(True) + [((2, 1024, 128), BF16), ((256, 256), BF16)]
     scratch += [((2, 768, 256), BF16), ((2, 256, 768), BF16), ((4, 256, 256), BF16), ((4, 256, 256), BF16)]
     scratch += [((2, 256, 256), BF16), ((2, 256, 16), BF16), ((2, 16, 256), BF16), ((2, 256, 128), F32), ((8, 128), F32)]
-    scratch += [((2, 768, 256), F32), ((4, 256, 256), F32), ((2, 256, 16), F32), ((2, 256, 128), F32)]
+    scratch += [((2, 768, 256), F32), ((256, 768), F32), ((4, 256, 256), F32), ((2, 256, 16), F32), ((2, 16, 256), F32), ((2, 256, 128), F32)]
     scratch += [((128, lanes), F32)] + [((256, lanes), BF16)] * 2 + [((128, lanes), BF16)] * 2
-    scratch += [((1024, lanes), BF16)] * 2 + [((768, lanes), BF16)]
-    scratch += [
-        ((768, lanes), BF16),
-        ((768, lanes), F32),
-        ((1024, lanes), BF16),
-        ((1024, lanes), F32),
-        ((256, lanes), F32),
-        ((1, lanes), F32),
-        ((256, lanes), BF16),
-        ((256, lanes), BF16),
-        ((256, lanes), F32),
-        ((256, lanes), BF16),
-        ((16, lanes), BF16),
-    ] * 2
+    scratch += [((1024, lanes), BF16)] * 2 + [((768, lanes), BF16)] * 2
+    scratch += [((3, 768, lanes), BF16), ((2, 768, lanes), F32), ((2, 1024, lanes), BF16), ((2, 1024, lanes), F32)]
+    scratch += [((3, 1, lanes), F32), ((3, 256, lanes), F32), ((3, 256, lanes), BF16), ((3, 256, lanes), BF16)]
+    scratch += [((3, 256, lanes), F32), ((3, 256, lanes), BF16), ((3, 16, lanes), BF16)]
+    scratch += [((1, lanes), F32), ((256, lanes), F32), ((256, lanes), BF16), ((256, lanes), BF16)]
+    scratch += [((256, lanes), F32), ((256, lanes), BF16), ((16, lanes), F32)]
+    scratch += [((2, 256, lanes), BF16)] * 2 + [((256, lanes), BF16), ((16, lanes), BF16), ((256, lanes), BF16)]
+    scratch += [((128, lanes), BF16), ((256, lanes), BF16)]
     return pl.pallas_call(
         fake_kernel(band, lanes, chunks, count_all),
-        grid=(chunks, band // 2 + 1),
+        grid=(total + 1,),
         in_specs=specs,
-        out_specs=[pl.BlockSpec(item.shape, lambda c, s, n=len(item.shape): (0,) * n) for item in outs],
+        out_specs=[pl.BlockSpec(item.shape, lambda t, n=len(item.shape): (0,) * n) for item in outs],
         out_shape=outs,
         scratch_shapes=[pltpu.VMEM(*item) for item in scratch],
         compiler_params=pltpu.CompilerParams(vmem_limit_bytes=VMEM_LIMIT),
         cost_estimate=cost(1.6e7 * band * positions, 3072 * band * positions),
         name="judge_fake",
-    )(places, *slabs, xt, xt, xt, codes, lane_info, consts, spots)
-
-
-def turn_kernel(pixels_ref, turned_ref):
-    frames = pixels_ref.shape[0]
-    turned_ref[0] = pixels_ref[...].reshape(frames * 16, 768).T
-
-
-def turn_pixels(pixels):
-    frames, band = pixels.shape[:2]
-    part = min(frames, 32)
-    return pl.pallas_call(
-        turn_kernel,
-        grid=(band, frames // part),
-        in_specs=[pl.BlockSpec((part, 1, 16, 768), lambda r, c: (c, r, 0, 0))],
-        out_specs=pl.BlockSpec((1, 768, part * 16), lambda r, c: (r, 0, c)),
-        out_shape=jax.ShapeDtypeStruct((band, 768, frames * 16), BF16),
-        compiler_params=pltpu.CompilerParams(vmem_limit_bytes=VMEM_LIMIT),
-        cost_estimate=cost(0, 4 * pixels.size),
-        name="turn",
-    )(pixels)
+    )(places, *slabs, pixels, pixels, codes, lane_info, consts, spots)
 
 
 def count_kernel(codes_ref, counts_ref):
@@ -779,6 +912,14 @@
     return lax.ppermute(x, axis, pairs)
 
 
+def neighbours(rows, grp, bands):
+    last = rows.shape[1] - 1
+    if bands == 2:
+        got = swap(lax.dynamic_index_in_dim(rows, jnp.where(grp == 0, last, 0), 1, keepdims=False), "grp", 1)
+        return got, got
+    return passed_along(rows[:, 0], "grp", -1), passed_along(rows[:, last], "grp", 1)
+
+
 def swap(x, axis, bits):
     return lax.ppermute(x, axis, [(i, i ^ bits) for i in range(lax.axis_size(axis))])
 
@@ -801,57 +942,55 @@
     return gathered, swap(gathered, "dp", 1)
 
 
-def hop_kernel(plans, *refs):
-    refs = list(refs)
-    inputs, outputs = refs[: 2 * len(plans)], refs[2 * len(plans) :]
-    for number, (count, scalars, sent) in enumerate(plans):
-        keep_ref, got_ref = inputs[2 * number : 2 * number + 2]
-        half = count // 2
-        for slab in range(count):
-            place, cast, out_ref = slab, F32, outputs[0]
-            if half and slab >= half:
-                place, cast, out_ref = slab - half, sent, outputs[1]
-            out_ref[place] = (keep_ref[slab] + got_ref[slab].astype(F32)).astype(cast)
-            if scalars:
-                got = got_ref[slab, 80:96, 128:256].astype(F32)
-                exact = keep_ref[slab, 80:81, 128:256] + ((got[0:1] + got[1:2]) + got[2:3])
-                out_ref[place, 80:96, 128:256] = scalar_rows(exact, cast == BF16).astype(cast)
-        outputs = outputs[2 if half else 1 :]
-
-
-def hop(*sums):
-    plans, operands, outs = [], [], []
-    for keep, got, scalars, sent in sums:
-        count, rows = keep.shape[0], keep.shape[1]
-        plans.append((count, scalars, sent))
-        operands += [keep, got]
-        outs.append(jax.ShapeDtypeStruct((max(count // 2, 1), rows, 256), F32))
-        if count > 1:
-            outs.append(jax.ShapeDtypeStruct((count // 2, rows, 256), sent))
-    vmem = pl.BlockSpec(memory_space=pltpu.VMEM)
-    return pl.pallas_call(
-        lambda *refs: hop_kernel(plans, *refs),
-        in_specs=[vmem] * len(operands),
-        out_specs=[vmem] * len(outs),
-        out_shape=outs,
-        name="hop",
-    )(*operands)
+def scalar_places(shape):
+    row = lax.broadcasted_iota(jnp.int32, shape, 1)
+    lane = lax.broadcasted_iota(jnp.int32, shape, 2)
+    return row, (row >= 80) & (row < 83) & (lane >= 128)
+
+
+def going(summed, scalars):
+    if scalars:
+        row, held = scalar_places(summed.shape)
+        upper = lax.reduce_precision(summed, 8, 7)
+        middle = lax.reduce_precision(summed - upper, 8, 7)
+        parts = jnp.where(row == 81, summed - upper, jnp.where(row == 82, (summed - upper) - middle, summed))
+        summed = jnp.where(held, parts, summed)
+    return low(summed)
+
+
+def coming(got, scalars):
+    got = got.astype(F32)
+    if scalars:
+        _, held = scalar_places(got.shape)
+        whole = (got[:, 80:81] + got[:, 81:82]) + got[:, 82:83]
+        got = jnp.where(held, jnp.broadcast_to(whole, got.shape), got)
+    return got
+
+
+def split(summed):
+    half = summed.shape[0] // 2
+    return summed[:half], summed[half:]
 
 
 def reduce_both(auto_keep, auto_got, judge_send, judge_keep):
     judge_got = swap(judge_send, "dp", 1)
     auto_got, judge_got = lax.optimization_barrier((auto_got, judge_got))
-    auto_keep, auto_send, judge_keep, judge_send = hop(
-        (auto_keep, auto_got, False, BF16), (judge_keep, judge_got, True, BF16)
-    )
-    auto_got, judge_got = lax.optimization_barrier((swap(auto_send, "dp", 4), swap(judge_send, "dp", 2)))
-    auto_keep, auto_send, judge_keep, judge_send = hop(
-        (auto_keep, auto_got, False, F32), (judge_keep, judge_got, True, BF16)
-    )
-    auto_got, judge_got = lax.optimization_barrier((swap(auto_send, "dp", 8), swap(judge_send, "dp", 4)))
-    auto_keep, judge_keep, judge_send = hop((auto_keep, auto_got, False, F32), (judge_keep, judge_got, True, F32))
-    auto_got, judge_got = lax.optimization_barrier((swap(auto_keep, "grp", 1), swap(judge_send, "dp", 8)))
-    (judge_keep,) = hop((judge_keep, judge_got, True, F32))
+    auto_keep, auto_send = split(auto_keep + coming(auto_got, False))
+    judge_keep, judge_send = split(judge_keep + judge_got)
+    auto_got = swap(going(auto_send, False), "dp", 4)
+    judge_got = swap(going(judge_send, True), "dp", 2)
+    auto_got, judge_got = lax.optimization_barrier((auto_got, judge_got))
+    auto_keep, auto_send = split(auto_keep + coming(auto_got, False))
+    judge_keep, judge_send = split(judge_keep + coming(judge_got, True))
+    auto_got = swap(auto_send, "dp", 8)
+    judge_got = swap(going(judge_send, True), "dp", 4)
+    auto_got, judge_got = lax.optimization_barrier((auto_got, judge_got))
+    auto_keep = auto_keep + auto_got
+    judge_keep, judge_send = split(judge_keep + coming(judge_got, True))
+    auto_got = swap(auto_keep, "grp", 1)
+    judge_got = swap(judge_send, "dp", 8)
+    auto_got, judge_got = lax.optimization_barrier((auto_got, judge_got))
+    judge_keep = judge_keep + judge_got
     judge_got = swap(judge_keep, "grp", 1)
     return auto_keep[0] + auto_got[0], judge_keep[0] + judge_got[0]
 
@@ -952,17 +1091,16 @@
     positions = frames * 16
     count_all = float(frames * parts * 256)
 
-    code_halos = (passed_along(codes[:, 0], "grp", -1), passed_along(codes[:, band - 1], "grp", 1))
+    code_halos = neighbours(codes, grp, bands)
     code_rows = codes.transpose(1, 0, 2).reshape(band, positions).astype(F32)
     counts = count_codes(code_rows)
-    xt = turn_pixels(pixels)
+    halos = neighbours(pixels, grp, bands)
     if shared:
         lane_info, slab = frame_lanes(me * frames, clip_frames, frame_bounds, masters)
-        slabs = gather_slabs(slab, (counts, None, xt))
+        slabs = gather_slabs(slab, (counts, None, code_halos))
     else:
         lane_info, slabs = whole_slabs(me * frames, clip_frames, frame_bounds, masters)
     counts = lax.psum(counts, ("dp", "grp"))
-    halos = (passed_along(xt[0], "grp", -1), passed_along(xt[band - 1], "grp", 1))
 
     places = jnp.stack(
         [grp * band, (grp < bands - 1).astype(jnp.int32), (grp > 0).astype(jnp.int32), me if shared else jnp.int32(0)]
@@ -971,14 +1109,14 @@
     all_codes = jnp.concatenate([above, code_rows, under], axis=0)
     extra = (all_codes, lane_info, *constants())
 
-    fake_outs = run_fake(xt, places, slabs, extra, count_all)
+    fake_outs = run_fake(pixels, places, slabs, extra, count_all)
     halos, counts, fake_outs = lax.optimization_barrier((halos, counts, fake_outs))
     auto, starts = fake_outs[:2], fake_outs[2:7]
     if shared:
         auto_send, auto_keep = auto
-        auto_keep, auto_send = hop((auto_keep, swap(auto_send, "dp", 1), False, BF16))
-        got = swap(auto_send, "dp", 2)
-    judge = run_real(xt, halos, places, slabs, starts, count_all)
+        auto_keep, auto_send = split(auto_keep + swap(auto_send, "dp", 1))
+        got = swap(going(auto_send, False), "dp", 2)
+    judge = run_real(pixels, halos, places, slabs, starts, count_all)
     if shared:
         got, judge = lax.optimization_barrier((got, judge))
         auto_total, judge_total = reduce_both(auto_keep, got, *judge)

time: 319 us -> 278 us (0.87)
  Pallas kernels: 215 us -> 177 us
  waiting for transfers between devices: 31.2 us -> 41 us
  starting transfers between devices: 27 us -> 18.2 us
  local copies, waits for them, and re-layouts: 14.9 us -> 11 us
    pallas_call x7 -> x1, Pallas kernels: 163 us -> 123 us  [run_fake(): pl.pallas_call(fake_kernel(band, lanes, chunks, count_all), grid=(total +...]
    ppermute x4 -> x0, starting transfers between devices: 11.7 us -> none  [passed_along(): return lax.ppermute(x, axis, pairs)]
    ppermute x14 -> x16, waiting for transfers between devices: 31.2 us -> 38.2 us  [swap(): lax.ppermute(x, axis, [(i, i ^ bits) for i in range(lax.axis_size(axis))])]
    unnamed x72 -> x62, local copies, waits for them, and re-layouts: 6.6 us -> 3.23 us
    ppermute x14 -> x16, starting transfers between devices: 15.3 us -> 18.2 us  [swap(): lax.ppermute(x, axis, [(i, i ^ bits) for i in range(lax.axis_size(axis))])]
  transfers between devices with their start and end apart: 19 -> 17, of which waited for: 8 -> 12; matrix products, arithmetic and copies ran while one was open for 4% -> 4% of each run, Pallas kernels for 63% -> 63%
where the time goes in v3:
time: 278 us; the launch traced here: 277 us
  Pallas kernels  177 us (64%)
  waiting for transfers between devices  41 us (15%)
  starting transfers between devices  18.2 us (7%)
  between operations  16.5 us (6%)
  other arithmetic  13.5 us (5%)
  local copies, waits for them, and re-layouts  11 us (4%)
    pallas_call x1, Pallas kernels, run_fake(): pl.pallas_call(fake_kernel(band, lanes, chunks, count_all), grid=(total +...  123 us
    pallas_call x1, Pallas kernels, run_real(): pl.pallas_call(real_kernel(band, lanes, chunks, count_all), grid=(total +...  46.4 us
    ppermute x16, waiting for transfers between devices, swap(): lax.ppermute(x, axis, [(i, i ^ bits) for i in range(lax.axis_size(axis))])  38.2 us
    ppermute x16, starting transfers between devices, swap(): lax.ppermute(x, axis, [(i, i ^ bits) for i in range(lax.axis_size(axis))])  18.2 us
  transfers between devices with their start and end apart: 17, of which 12 were waited for; matrix products, arithmetic and copies ran while one was open for 4% of the time, Pallas kernels for 63%

profile of v3, /device:TPU:0, one launch (start us, length us, event | category | flops | bytes accessed | tf_op | source)
XLA Modules:
  0.0 277.2 jit_solution(13330144985485663823)
XLA Ops:
  8.6 1.3 copy.104
  10.7 0.7 broadcast_in_dim.30.clips_ref
  11.4 2.2 frames.1
  13.7 4.0 %collective-permute-start.1 = (bf16[1,240,256]{2,1,0:T(8,128)(2,1)}, bf16[1,240,256]{2,1,0:T(8,128)(2,1)S(1)}, u32[]{:S(2)}, u32[]{:S(2)}) collective-permute-start(bf16[1,240,256]{2,1,0:T(8,128)(2,1)} %bitcast.55), channel_id=1, source_target_pairs={{0,16},{2,18},{4,20},{6,22},{8,24},{10,26},{12,28},{14,30},{16,0},... | collective-permute-start | bytes 368648 | tf_op jit(solution)/shard_map/ppermute | solution.py:924
  17.7 0.8 convert_bitcast_fusion
  18.7 0.8 convert_element_type.81.codes_ref
  19.5 5.3 %count.1 = f32[256,256]{1,0:T(8,128)} custom-call(f32[8,1,1024]{2,1,0:T(1,128)} %convert_element_type.81.codes_ref), custom_call_target="tpu_custom_call" | custom-call | flops 4096000000 | bytes 32768 | tf_op jit(solution)/shard_map/count/pallas_call | solution.py:842
  24.8 1.6 collective-permute-start.2
  26.4 5.8 %collective-permute-done.2 = bf16[2,240,256]{2,1,0:T(8,128)(2,1)S(1)} collective-permute-done((bf16[2,240,256]{2,1,0:T(8,128)(2,1)S(1)}, bf16[2,240,256]{2,1,0:T(8,128)(2,1)S(1)}, u32[]{:S(2)}, u32[]{:S(2)}) %collective-permute-start.2) | collective-permute-done | bytes 245792 | tf_op jit(solution)/shard_map/ppermute | solution.py:924
  32.3 1.6 collective-permute-start.3
  34.6 1.5 collective-permute-start.4
  36.1 2.1 collective-permute-done.4
  38.2 5.9 %collective-permute-done.3 = bf16[4,240,256]{2,1,0:T(8,128)(2,1)S(1)} collective-permute-done((bf16[4,240,256]{2,1,0:T(8,128)(2,1)S(1)}, bf16[4,240,256]{2,1,0:T(8,128)(2,1)S(1)}, u32[]{:S(2)}, u32[]{:S(2)}) %collective-permute-start.3) | collective-permute-done | bytes 491552 | tf_op jit(solution)/shard_map/ppermute | solution.py:924
  44.4 1.8 dynamic-slice_bitcast_fusion
  46.2 1.6 collective-permute-start
  49.4 122.9 %judge_fake.1 = (f32[8,192,256]{2,1,0:T(8,128)}, f32[8,192,256]{2,1,0:T(8,128)}, f32[1024,256]{1,0:T(8,128)}, f32[128,256]{1,0:T(8,128)}, f32[192,256]{1,0:T(8,1...) custom-call(s32[4]{0:T(128)} %pad_add_fusion.refs_0_, bf16[8,240,256]{2,1,0:T(8,128)(2,1)} %copy-done.1, ...), custom_call_target="tpu_custom_call" | custom-call | flops 131072000000 | bytes 25165824 | tf_op jit(solution)/shard_map/judge_fake/pallas_call | solution.py:814
  172.3 2.8 all-reduce.2.cloned.1.call-done
  175.1 3.6 %collective-permute-done.6 = f32[8,192,256]{2,1,0:T(8,128)S(1)} collective-permute-done((f32[8,192,256]{2,1,0:T(8,128)}, f32[8,192,256]{2,1,0:T(8,128)S(1)}, u32[]{:S(2)}, u32[]{:S(2)}) %collective-permute-start.6) | collective-permute-done | bytes 1572896 | tf_op jit(solution)/shard_map/ppermute | solution.py:924
  178.7 1.6 add.171
  180.4 1.5 collective-permute-start.7
  181.9 46.4 %judge_real.1 = (f32[8,96,256]{2,1,0:T(8,128)}, f32[8,96,256]{2,1,0:T(8,128)}) custom-call(s32[4]{0:T(128)} %pad_add_fusion.refs_0_, bf16[8,240,256]{2,1,0:T(8,128)(2,1)} %copy-done.1, bf16[8,240,256]{2,1,0:T(8,128)(2,1)} %collective-permute-done.5.refs_2_, bf16[64,8,16,768]{3,2,1,0:T(8,128)(2,1)} %refs_4_.3, bf16[64,8,16,768]{3,2,1,0:T(8,128)(2,1)} %refs_4_.3, ...), custom_call_target="tpu_custom_call" | custom-call | flops 44236800000 | bytes 25165824 | tf_op jit(solution)/shard_map/judge_real/pallas_call | solution.py:402
  228.5 2.4 collective-permute-done.8
  231.0 1.5 collective-permute-start.9
  233.5 4.5 %collective-permute-done.9 = bf16[2,192,256]{2,1,0:T(8,128)(2,1)S(1)} collective-permute-done((bf16[2,192,256]{2,1,0:T(8,128)(2,1)S(1)}, bf16[2,192,256]{2,1,0:T(8,128)(2,1)S(1)}, u32[]{:S(2)}, u32[]{:S(2)}) %collective-permute-start.9) | collective-permute-done | bytes 196640 | tf_op jit(solution)/shard_map/ppermute | solution.py:924
  238.0 1.6 collective-permute-done.10
  239.7 1.5 collective-permute-start.11
  242.2 1.2 slice.140
  243.4 3.6 %collective-permute-done.12 = bf16[2,96,256]{2,1,0:T(8,128)(2,1)S(1)} collective-permute-done((bf16[2,96,256]{2,1,0:T(8,128)(2,1)S(1)}, bf16[2,96,256]{2,1,0:T(8,128)(2,1)S(1)}, u32[]{:S(2)}, u32[]{:S(2)}) %collective-permute-start.12) | collective-permute-done | bytes 98336 | tf_op jit(solution)/shard_map/ppermute | solution.py:924
  246.9 3.7 %collective-permute-done.11 = f32[1,192,256]{2,1,0:T(8,128)S(1)} collective-permute-done((f32[1,192,256]{2,1,0:T(8,128)S(1)}, f32[1,192,256]{2,1,0:T(8,128)S(1)}, u32[]{:S(2)}, u32[]{:S(2)}) %collective-permute-start.11) | collective-permute-done | bytes 196640 | tf_op jit(solution)/shard_map/ppermute | solution.py:924
  252.7 4.6 %collective-permute-done.14 = f32[1,96,256]{2,1,0:T(8,128)S(1)} collective-permute-done((f32[1,96,256]{2,1,0:T(8,128)S(1)}, f32[1,96,256]{2,1,0:T(8,128)S(1)}, u32[]{:S(2)}, u32[]{:S(2)}) %collective-permute-start.14) | collective-permute-done | bytes 98336 | tf_op jit(solution)/shard_map/ppermute | solution.py:924
  258.0 1.7 collective-permute-start.15
  264.8 1.9 pad_maximum_fusion.7
  (132 shorter events, 16.3 us)
Async XLA Ops:
  7.2 167.9 %all-reduce.2.cloned.1.call-start = ((), (), s32[]{:S(2)}) async-start(), calls=%async_computation | async-start | bytes 524288 | tf_op jit(solution)/shard_map/psum | solution.py:1103
  13.7 11.1 %collective-permute-start.1 = (bf16[1,240,256]{2,1,0:T(8,128)(2,1)}, bf16[1,240,256]{2,1,0:T(8,128)(2,1)S(1)}, u32[]{:S(2)}, u32[]{:S(2)}) collective-permute-start(bf16[1,240,256]{2,1,0:T(8,128)(2,1)} %bitcast.55), channel_id=1, source_target_pairs={{0,16},{2,18},{4,20},{6,22},{8,24},{10,26},{12,28},{14,30},{16,0},... | collective-permute-start | bytes 368648 | tf_op jit(solution)/shard_map/ppermute | solution.py:924
  24.8 7.5 %collective-permute-start.2 = (bf16[2,240,256]{2,1,0:T(8,128)(2,1)S(1)}, bf16[2,240,256]{2,1,0:T(8,128)(2,1)S(1)}, u32[]{:S(2)}, u32[]{:S(2)}) collective-permute-start(bf16[2,240,256]{2,1,0:T(8,128)(2,1)S(1)} %pad_maximum_fusion.2), channel_id=1, source_target_pairs={{0,8},{2,10},{4,12},{6,14},{8,0},{10,2},{12,4},{14,6},{16,24},{18,... | collective-permute-start | bytes 737288 | tf_op jit(solution)/shard_map/ppermute | solution.py:924
  32.3 11.8 %collective-permute-start.3 = (bf16[4,240,256]{2,1,0:T(8,128)(2,1)S(1)}, bf16[4,240,256]{2,1,0:T(8,128)(2,1)S(1)}, u32[]{:S(2)}, u32[]{:S(2)}) collective-permute-start(bf16[4,240,256]{2,1,0:T(8,128)(2,1)S(1)} %pad_maximum_fusion.1), channel_id=1, source_target_pairs={{0,4},{2,6},{4,0},{6,2},{8,12},{10,14},{12,8},{14,10},{16,20},{18,... | collective-permute-start | bytes 1474568 | tf_op jit(solution)/shard_map/ppermute | solution.py:924
  34.6 3.7 %collective-permute-start.4 = (s32[64,16]{0,1:T(8,128)S(1)}, s32[64,16]{0,1:T(8,128)S(1)}, u32[]{:S(2)}, u32[]{:S(2)}) collective-permute-start(s32[64,16]{0,1:T(8,128)S(1)} %dynamic-slice_bitcast_fusion.1), channel_id=1, source_target_pairs={{0,1},{1,0},{2,3},{3,2},{4,5},{5,4},{6,7},{7,6},{8,9},{9,8},{10,11... | collective-permute-start | bytes 12296 | tf_op jit(solution)/shard_map/ppermute | solution.py:924
  44.3 5.1 %collective-permute-start.5 = (bf16[8,240,256]{2,1,0:T(8,128)(2,1)S(1)}, bf16[8,240,256]{2,1,0:T(8,128)(2,1)}, u32[]{:S(2)}, u32[]{:S(2)}) collective-permute-start(bf16[8,240,256]{2,1,0:T(8,128)(2,1)S(1)} %pad_maximum_fusion.refs_1_), channel_id=1, source_target_pairs={{0,2},{2,0},{4,6},{6,4},{8,10},{10,8},{12,14},{14,12},{16,18},{18,... | collective-permute-start | bytes 2949128 | tf_op jit(solution)/shard_map/ppermute | solution.py:924
  46.2 128.9 %collective-permute-start = (bf16[64,16,768]{2,1,0:T(8,128)(2,1)S(1)}, bf16[64,16,768]{2,1,0:T(8,128)(2,1)}, u32[]{:S(2)}, u32[]{:S(2)}) collective-permute-start(bf16[64,16,768]{2,1,0:T(8,128)(2,1)S(1)} %dynamic-slice_bitcast_fusion), channel_id=1, source_target_pairs={{0,1},{1,0},{2,3},{3,2},{4,5},{5,4},{6,7},{7,6},{8,9},{9,8},{10,11... | collective-permute-start | bytes 4718600 | tf_op jit(solution)/shard_map/ppermute | solution.py:924
  175.1 3.6 %collective-permute-start.6 = (f32[8,192,256]{2,1,0:T(8,128)}, f32[8,192,256]{2,1,0:T(8,128)S(1)}, u32[]{:S(2)}, u32[]{:S(2)}) collective-permute-start(f32[8,192,256]{2,1,0:T(8,128)} %get-tuple-element.73), channel_id=1, source_target_pairs={{0,2},{2,0},{4,6},{6,4},{8,10},{10,8},{12,14},{14,12},{16,18},{18,... | collective-permute-start | bytes 4718600 | tf_op jit(solution)/shard_map/ppermute | solution.py:924
  180.4 48.0 %collective-permute-start.7 = (bf16[4,192,256]{2,1,0:T(8,128)(2,1)S(1)}, bf16[4,192,256]{2,1,0:T(8,128)(2,1)S(1)}, u32[]{:S(2)}, u32[]{:S(2)}) collective-permute-start(bf16[4,192,256]{2,1,0:T(8,128)(2,1)S(1)} %slice.208), channel_id=1, source_target_pairs={{0,4},{2,6},{4,0},{6,2},{8,12},{10,14},{12,8},{14,10},{16,20},{18,... | collective-permute-start | bytes 1179656 | tf_op jit(solution)/shard_map/ppermute | solution.py:924
  228.3 2.6 collective-permute-start.8
  231.0 7.0 %collective-permute-start.9 = (bf16[2,192,256]{2,1,0:T(8,128)(2,1)S(1)}, bf16[2,192,256]{2,1,0:T(8,128)(2,1)S(1)}, u32[]{:S(2)}, u32[]{:S(2)}) collective-permute-start(bf16[2,192,256]{2,1,0:T(8,128)(2,1)S(1)} %slice.209), channel_id=1, source_target_pairs={{0,8},{2,10},{4,12},{6,14},{8,0},{10,2},{12,4},{14,6},{16,24},{18,... | collective-permute-start | bytes 589832 | tf_op jit(solution)/shard_map/ppermute | solution.py:924
  232.9 6.7 %collective-permute-start.10 = (bf16[4,96,256]{2,1,0:T(8,128)(2,1)S(1)}, bf16[4,96,256]{2,1,0:T(8,128)(2,1)S(1)}, u32[]{:S(2)}, u32[]{:S(2)}) collective-permute-start(bf16[4,96,256]{2,1,0:T(8,128)(2,1)S(1)} %fusion), channel_id=1, source_target_pairs={{0,4},{2,6},{4,0},{6,2},{8,12},{10,14},{12,8},{14,10},{16,20},{18,... | collective-permute-start | bytes 589832 | tf_op jit(solution)/shard_map/ppermute | solution.py:924
  239.7 11.0 %collective-permute-start.11 = (f32[1,192,256]{2,1,0:T(8,128)S(1)}, f32[1,192,256]{2,1,0:T(8,128)S(1)}, u32[]{:S(2)}, u32[]{:S(2)}) collective-permute-start(f32[1,192,256]{2,1,0:T(8,128)S(1)} %slice.149), channel_id=1, source_target_pairs={{0,16},{2,18},{4,20},{6,22},{8,24},{10,26},{12,28},{14,30},{16,0},... | collective-permute-start | bytes 589832 | tf_op jit(solution)/shard_map/ppermute | solution.py:924
  241.5 5.4 %collective-permute-start.12 = (bf16[2,96,256]{2,1,0:T(8,128)(2,1)S(1)}, bf16[2,96,256]{2,1,0:T(8,128)(2,1)S(1)}, u32[]{:S(2)}, u32[]{:S(2)}) collective-permute-start(bf16[2,96,256]{2,1,0:T(8,128)(2,1)S(1)} %fusion.6), channel_id=1, source_target_pairs={{0,8},{2,10},{4,12},{6,14},{8,0},{10,2},{12,4},{14,6},{16,24},{18,... | collective-permute-start | bytes 294920 | tf_op jit(solution)/shard_map/ppermute | solution.py:924
  243.4 16.3 %copy-start.5 = (f32[4,16,256]{2,1,0:T(8,128)S(1)}, f32[4,16,256]{2,1,0:T(8,128)}, u32[]{:S(2)}) copy-start(f32[4,16,256]{2,1,0:T(8,128)} %matrices.1) | copy-start | bytes 196612
  243.4 16.3 %copy-start.9 = (f32[4,16,256]{2,1,0:T(8,128)S(1)}, f32[4,16,256]{2,1,0:T(8,128)}, u32[]{:S(2)}) copy-start(f32[4,16,256]{2,1,0:T(8,128)} %param.51) | copy-start | bytes 196612
  243.4 16.3 %copy-start.10 = (f32[4,16,256]{2,1,0:T(8,128)S(1)}, f32[4,16,256]{2,1,0:T(8,128)}, u32[]{:S(2)}) copy-start(f32[4,16,256]{2,1,0:T(8,128)} %param.43) | copy-start | bytes 196612
  250.8 6.8 %collective-permute-start.13 = (f32[1,192,256]{2,1,0:T(8,128)S(1)}, f32[1,192,256]{2,1,0:T(8,128)S(1)}, u32[]{:S(2)}, u32[]{:S(2)}) collective-permute-start(f32[1,192,256]{2,1,0:T(8,128)S(1)} %slice_add_fusion.2), channel_id=1, source_target_pairs={{0,1},{1,0},{2,3},{3,2},{4,5},{5,4},{6,7},{7,6},{8,9},{9,8},{10,11... | collective-permute-start | bytes 589832 | tf_op jit(solution)/shard_map/ppermute | solution.py:924
  251.0 15.7 %copy-start.15 = (f32[48,4]{0,1:T(4,128)S(1)}, f32[48,4]{0,1:T(4,128)}, u32[]{:S(2)}) copy-start(f32[48,4]{0,1:T(4,128)} %param.38) | copy-start | bytes 2308
  251.0 15.7 %copy-start.22 = (f32[48,4]{0,1:T(4,128)S(1)}, f32[48,4]{0,1:T(4,128)}, u32[]{:S(2)}) copy-start(f32[48,4]{0,1:T(4,128)} %param.54) | copy-start | bytes 2308
  251.0 15.7 %copy-start.23 = (f32[48,4]{0,1:T(4,128)S(1)}, f32[48,4]{0,1:T(4,128)}, u32[]{:S(2)}) copy-start(f32[48,4]{0,1:T(4,128)} %param.46) | copy-start | bytes 2308
  251.1 6.2 %collective-permute-start.14 = (f32[1,96,256]{2,1,0:T(8,128)S(1)}, f32[1,96,256]{2,1,0:T(8,128)S(1)}, u32[]{:S(2)}, u32[]{:S(2)}) collective-permute-start(f32[1,96,256]{2,1,0:T(8,128)S(1)} %slice.159), channel_id=1, source_target_pairs={{0,16},{2,18},{4,20},{6,22},{8,24},{10,26},{12,28},{14,30},{16,0},... | collective-permute-start | bytes 294920 | tf_op jit(solution)/shard_map/ppermute | solution.py:924
  251.8 15.5 %copy-start.13 = (f32[128,16]{0,1:T(8,128)S(1)}, f32[128,16]{0,1:T(8,128)}, u32[]{:S(2)}) copy-start(f32[128,16]{0,1:T(8,128)} %param.40) | copy-start | bytes 24580
  251.8 15.5 %copy-start.16 = (f32[128,16]{0,1:T(8,128)S(1)}, f32[128,16]{0,1:T(8,128)}, u32[]{:S(2)}) copy-start(f32[128,16]{0,1:T(8,128)} %param.56) | copy-start | bytes 24580
  251.8 15.5 %copy-start.17 = (f32[128,16]{0,1:T(8,128)S(1)}, f32[128,16]{0,1:T(8,128)}, u32[]{:S(2)}) copy-start(f32[128,16]{0,1:T(8,128)} %param.48) | copy-start | bytes 24580
  251.8 16.1 %copy-start.21 = (f32[16]{0:T(128)S(1)}, f32[16]{0:T(128)}, u32[]{:S(2)}) copy-start(f32[16]{0:T(128)} %param.41) | copy-start | bytes 196
  251.8 16.1 %copy-start.26 = (f32[16]{0:T(128)S(1)}, f32[16]{0:T(128)}, u32[]{:S(2)}) copy-start(f32[16]{0:T(128)} %param.57) | copy-start | bytes 196
  251.8 16.1 %copy-start.27 = (f32[16]{0:T(128)S(1)}, f32[16]{0:T(128)}, u32[]{:S(2)}) copy-start(f32[16]{0:T(128)} %param.49) | copy-start | bytes 196
  251.9 16.6 %copy-start.6 = (f32[128,128]{1,0:T(8,128)S(1)}, f32[128,128]{1,0:T(8,128)}, u32[]{:S(2)}) copy-start(f32[128,128]{1,0:T(8,128)} %mid_conv.1) | copy-start | bytes 196612
  251.9 16.6 %copy-start.11 = (f32[128,128]{1,0:T(8,128)S(1)}, f32[128,128]{1,0:T(8,128)}, u32[]{:S(2)}) copy-start(f32[128,128]{1,0:T(8,128)} %param.55) | copy-start | bytes 196612
  251.9 16.6 %copy-start.12 = (f32[128,128]{1,0:T(8,128)S(1)}, f32[128,128]{1,0:T(8,128)}, u32[]{:S(2)}) copy-start(f32[128,128]{1,0:T(8,128)} %param.47) | copy-start | bytes 196612
  258.0 5.6 %collective-permute-start.15 = (f32[1,96,256]{2,1,0:T(8,128)S(1)}, f32[1,96,256]{2,1,0:T(8,128)S(1)}, u32[]{:S(2)}, u32[]{:S(2)}) collective-permute-start(f32[1,96,256]{2,1,0:T(8,128)S(1)} %slice_add_fusion.3), channel_id=1, source_target_pairs={{0,1},{1,0},{2,3},{3,2},{4,5},{5,4},{6,7},{7,6},{8,9},{9,8},{10,11... | collective-permute-start | bytes 294920 | tf_op jit(solution)/shard_map/ppermute | solution.py:924
  (13 other events, 111.6 us)
Sparse Core Ops, SparseCore 0:
  49.5 125.5 all-reduce.1

commit v4 on v3

--- a/solution.py
+++ b/solution.py
@@ -608,14 +608,14 @@
                 yield
 
         def back_middle():
-            for group in range(4):
-                rows = slice(256 * group, 256 * group + 256)
+            for group in range(2):
+                rows = slice(512 * group, 512 * group + 512)
                 gwm_ref[rows, :] += nt(act[rows, :], g2_disc[...])
                 yield
 
         def back_project():
-            for group in range(4):
-                rows = slice(group * 192, group * 192 + 192)
+            for group in range(2):
+                rows = slice(group * 384, group * 384 + 384)
                 gproj_ref[1, rows, :] += nt(gradlow_s[rows, :], outlow_s[back_three])
                 yield
 
@@ -673,6 +673,16 @@
             stream_s[:, part] = low(grad_stream)
             yield
 
+        def back_fill():
+            first, project, weights = back_first(), back_project(), back_weights()
+            for piece in (first, project, first, weights, first, weights, project, first, weights, weights, weights):
+                next(piece)
+                yield
+
+        def back_stream():
+            gprojt_ref[...] += nn(stream_s[...], xe_ref[...].reshape(lanes, 768))
+            yield
+
         def back_weights():
             gblocks_ref[3] += nt(saved_s[3][back_three], outer_s[1])
             yield
@@ -685,11 +695,6 @@
             yield
             gblocks_ref[0] += nt(encoded_s[2][...], inner_s[0])
             yield
-            for start in range(0, 768, 256):
-                x = xe_ref[:, 0, :, start : start + 256].reshape(lanes, 256)
-                gprojt_ref[:, start : start + 256] += nn(stream_s[...], x)
-                yield
-
         def shift():
             for ref, new in ((g2_disc, new_disc), (g2_gen, new_gen)):
                 ref[0:128, :] = ref[128:256, :]
@@ -703,19 +708,20 @@
                 *((front_block(part), 5) for part in halves),
                 *((back_encode(part), 5) for part in halves),
                 (front_turn(), 6),
+                (back_middle(), 2),
             )
             interleave(
-                (back_recon(), 4, 0.0, 0.8), (back_disc(), 4 * len(halves)), (front_recon(), 4 * len(halves), 0.2, 1.0)
+                (back_recon(), 4, 0.0, 0.6),
+                (back_disc(), 4 * len(halves), 0.0, 0.6),
+                (front_recon(), 4 * len(halves), 0.1, 0.8),
+                (front_first(), 4 * len(halves), 0.3, 1.0),
             )
             interleave(
-                *((back_chain(part), 10) for part in halves),
-                (back_middle(), 4, 0.0, 0.8),
-                (front_first(), 4 * len(halves), 0.2, 1.0),
-                (back_first(), 4),
-                (back_project(), 4),
+                *((back_chain(part), 10, 0.0, 0.9 + 0.1 * number) for number, part in enumerate(halves)),
+                *((front_middle(part), 7, 0.1, 1.0) for part in halves),
+                (back_fill(), 11, 0.05, 1.0),
             )
-            interleave(*((front_middle(part), 7) for part in halves), (back_weights(), 8))
-            interleave((front_last(), 1))
+            interleave((front_last(), 1), (back_stream(), 1))
             shift()
 
         @pl.when(front_ok & jnp.logical_not(back_ok))
@@ -733,9 +739,9 @@
             interleave((back_gen(), 4 * len(halves)), *((back_encode(part), 5) for part in halves))
             interleave((back_recon(), 4), (back_disc(), 4 * len(halves)))
             interleave(
-                *((back_chain(part), 10) for part in halves), (back_middle(), 4), (back_first(), 4), (back_project(), 4)
+                *((back_chain(part), 10) for part in halves), (back_middle(), 2), (back_first(), 4), (back_project(), 2)
             )
-            interleave((back_weights(), 1))
+            interleave((back_weights(), 1), (back_stream(), 1))
 
         @pl.when(stage == total)
         def write():
@@ -852,15 +858,20 @@
 
 def frame_kernel(place_ref, clips_ref, bounds_ref, project, matrices, fsq_pair, gain_pair, first_conv, mid_conv, last_conv, head_map, lane_ref, slab_ref, turned_s):
     lanes = lane_ref.shape[1]
-    clips = clips_ref[...]
-    number = clips.shape[0]
-    ahead = lax.broadcasted_iota(jnp.int32, (number, number), 1) < lax.broadcasted_iota(jnp.int32, (number, number), 0)
-    starts = nn(low(jnp.where(ahead, 1.0, 0.0)), low(clips))
+    clips = clips_ref[...].astype(F32)
+    number = clips.shape[1]
+    column = lax.broadcasted_iota(jnp.int32, (number, number), 1)
+    row = lax.broadcasted_iota(jnp.int32, (number, number), 0)
+    first = jnp.sum(jnp.where(column < row, clips, 0.0), axis=1, keepdims=True)
+    size = jnp.sum(jnp.where(column == row, clips, 0.0), axis=1, keepdims=True)
     frame = (place_ref[0] + lax.broadcasted_iota(jnp.int32, (1, lanes), 1) // 16).astype(F32)
-    first, size = wide(starts, lanes), wide(clips, lanes)
     mine = (first <= frame) & (frame < first + size)
     weight = 1.0 / jnp.sum(jnp.where(mine, size, 0.0), axis=0, keepdims=True)
-    height, width = bounds_ref[0:1, :], bounds_ref[1:2, :]
+    frames = bounds_ref.shape[1]
+    spread = lax.broadcasted_iota(jnp.int32, (frames, lanes), 1) // 16
+    spread = low(jnp.where(spread == lax.broadcasted_iota(jnp.int32, (frames, lanes), 0), 1.0, 0.0))
+    extents = nn(low(bounds_ref[...].astype(F32)), spread)
+    height, width = extents[0:1, :], extents[1:2, :]
     lane_ref[0:1, :] = height
     lane_ref[1:2, :] = width
     lane_ref[2:3, :] = weight
@@ -875,7 +886,8 @@
     slab_ref[224:240, 0:128] = low(last_conv[...])
     turned_s[...] = jnp.zeros_like(turned_s)
     for index in range(2):
-        turned_s[16 * index : 16 * index + 6, :] = fsq_pair[index]
+        for digit in range(6):
+            turned_s[16 * index + digit : 16 * index + digit + 1, :] = fsq_pair[digit, index : index + 1, :]
     turned_s[32:33, :] = head_map[...]
     turned_s[33:35, :] = gain_pair[...]
     turned_s[48:96, 0:4] = first_conv[...].T
@@ -889,10 +901,10 @@
 
 def frame_lanes(first, clip_frames, frame_bounds, masters):
     lanes = frame_bounds.shape[0] * 16
-    clips = jnp.broadcast_to(clip_frames.astype(F32)[:, None], (clip_frames.shape[0], 128))
-    bounds = jnp.repeat(frame_bounds.T.astype(F32), 16, axis=1)
+    clips = clip_frames.reshape(1, -1)
+    bounds = frame_bounds.T
     operands = list(masters)
-    operands[2] = operands[2].transpose(0, 2, 1)
+    operands[2] = operands[2].transpose(2, 0, 1)
     operands[4] = operands[4].T
     operands[6] = operands[6].T
     operands[7] = operands[7][None, :]
@@ -1094,13 +1106,14 @@
     code_halos = neighbours(codes, grp, bands)
     code_rows = codes.transpose(1, 0, 2).reshape(band, positions).astype(F32)
     counts = count_codes(code_rows)
+    both_counts = counts + swap(counts, "grp", 1) if bands == 2 else lax.psum(counts, "grp")
     halos = neighbours(pixels, grp, bands)
     if shared:
         lane_info, slab = frame_lanes(me * frames, clip_frames, frame_bounds, masters)
-        slabs = gather_slabs(slab, (counts, None, code_halos))
+        slabs = gather_slabs(slab, (counts, None, (code_halos, both_counts)))
     else:
         lane_info, slabs = whole_slabs(me * frames, clip_frames, frame_bounds, masters)
-    counts = lax.psum(counts, ("dp", "grp"))
+    counts = lax.psum(both_counts, "dp")
 
     places = jnp.stack(
         [grp * band, (grp < bands - 1).astype(jnp.int32), (grp > 0).astype(jnp.int32), me if shared else jnp.int32(0)]
@@ -1142,7 +1155,7 @@
         *(result[0] for result in results),
         *(result[1] for result in results),
         *(result[2] for result in results),
-        jnp.stack([losses[0], fake_outs[6][3, 0]]),
+        jnp.where(jnp.arange(2) == 0, losses[0], fake_outs[6][3, 0]),
         losses[1:3],
         perplexity,
     )

time: 278 us -> 269 us (0.968)
  waiting for transfers between devices: 41 us -> 36.2 us
    ppermute x16 -> x17, waiting for transfers between devices: 38.2 us -> 36.1 us  [swap(): lax.ppermute(x, axis, [(i, i ^ bits) for i in range(lax.axis_size(axis))])]
    ppermute x16 -> x17, starting transfers between devices: 18.2 us -> 20.1 us  [swap(): lax.ppermute(x, axis, [(i, i ^ bits) for i in range(lax.axis_size(axis))])]
  transfers between devices with their start and end apart: 17 -> 18, of which waited for: 12 -> 10; matrix products, arithmetic and copies ran while one was open for 4% -> 5% of each run, Pallas kernels for 63% -> 64%
where the time goes in v4:
time: 269 us; the launch traced here: 268 us
  Pallas kernels  175 us (65%)
  waiting for transfers between devices  36.2 us (13%)
  starting transfers between devices  20.1 us (7%)
  between operations  16.5 us (6%)
  other arithmetic  12.8 us (5%)
  local copies, waits for them, and re-layouts  8.22 us (3%)
    pallas_call x1, Pallas kernels, run_fake(): pl.pallas_call(fake_kernel(band, lanes, chunks, count_all), grid=(total +...  121 us
    pallas_call x1, Pallas kernels, run_real(): pl.pallas_call(real_kernel(band, lanes, chunks, count_all), grid=(total +...  46.4 us
    ppermute x17, waiting for transfers between devices, swap(): lax.ppermute(x, axis, [(i, i ^ bits) for i in range(lax.axis_size(axis))])  36.1 us
    ppermute x17, starting transfers between devices, swap(): lax.ppermute(x, axis, [(i, i ^ bits) for i in range(lax.axis_size(axis))])  20.1 us
  transfers between devices with their start and end apart: 18, of which 10 were waited for; matrix products, arithmetic and copies ran while one was open for 5% of the time, Pallas kernels for 64%

profile of v4, /device:TPU:0, one launch (start us, length us, event | category | flops | bytes accessed | tf_op | source)
XLA Modules:
  0.0 268.4 jit_solution(12130544643191228404)
XLA Ops:
  7.3 2.1 frames.1
  9.4 4.0 %collective-permute-start.2 = (bf16[1,240,256]{2,1,0:T(8,128)(2,1)}, bf16[1,240,256]{2,1,0:T(8,128)(2,1)S(1)}, u32[]{:S(2)}, u32[]{:S(2)}) collective-permute-start(bf16[1,240,256]{2,1,0:T(8,128)(2,1)} %bitcast.53), channel_id=1, source_target_pairs={{0,16},{2,18},{4,20},{6,22},{8,24},{10,26},{12,28},{14,30},{16,0},... | collective-permute-start | bytes 368648 | tf_op jit(solution)/shard_map/ppermute | solution.py:936
  13.4 0.8 convert_bitcast_fusion
  14.4 0.8 convert_element_type.69.codes_ref
  15.1 5.3 %count.1 = f32[256,256]{1,0:T(8,128)} custom-call(f32[8,1,1024]{2,1,0:T(1,128)} %convert_element_type.69.codes_ref), custom_call_target="tpu_custom_call" | custom-call | flops 4096000000 | bytes 32768 | tf_op jit(solution)/shard_map/count/pallas_call | solution.py:848
  20.5 1.6 collective-permute-start.3
  22.1 5.8 %collective-permute-done.3 = bf16[2,240,256]{2,1,0:T(8,128)(2,1)S(1)} collective-permute-done((bf16[2,240,256]{2,1,0:T(8,128)(2,1)S(1)}, bf16[2,240,256]{2,1,0:T(8,128)(2,1)S(1)}, u32[]{:S(2)}, u32[]{:S(2)}) %collective-permute-start.3) | collective-permute-done | bytes 245792 | tf_op jit(solution)/shard_map/ppermute | solution.py:936
  28.0 1.6 collective-permute-start.4
  29.6 1.5 collective-permute-start.1
  31.1 0.7 dynamic-slice_bitcast_fusion.1
  32.3 4.1 %collective-permute-done.1 = f32[256,256]{1,0:T(8,128)S(1)} collective-permute-done((f32[256,256]{1,0:T(8,128)}, f32[256,256]{1,0:T(8,128)S(1)}, u32[]{:S(2)}, u32[]{:S(2)}) %collective-permute-start.1) | collective-permute-done | bytes 262176 | tf_op jit(solution)/shard_map/ppermute | solution.py:936
  36.4 0.7 add.174
  37.2 2.6 collective-permute-done.4
  40.0 1.8 dynamic-slice_bitcast_fusion
  41.8 1.6 collective-permute-start
  45.0 120.7 %judge_fake.1 = (f32[8,192,256]{2,1,0:T(8,128)}, f32[8,192,256]{2,1,0:T(8,128)}, f32[1024,256]{1,0:T(8,128)}, f32[128,256]{1,0:T(8,128)}, f32[192,256]{1,0:T(8,1...) custom-call(s32[4]{0:T(128)} %pad_add_fusion.refs_0_, bf16[8,240,256]{2,1,0:T(8,128)(2,1)} %copy-done.1, ...), custom_call_target="tpu_custom_call" | custom-call | flops 131072000000 | bytes 25165824 | tf_op jit(solution)/shard_map/judge_fake/pallas_call | solution.py:820
  165.9 3.6 %collective-permute-done.7 = f32[8,192,256]{2,1,0:T(8,128)S(1)} collective-permute-done((f32[8,192,256]{2,1,0:T(8,128)}, f32[8,192,256]{2,1,0:T(8,128)S(1)}, u32[]{:S(2)}, u32[]{:S(2)}) %collective-permute-start.7) | collective-permute-done | bytes 1572896 | tf_op jit(solution)/shard_map/ppermute | solution.py:936
  169.5 1.6 add.175
  171.1 1.6 collective-permute-start.8
  172.7 46.4 %judge_real.1 = (f32[8,96,256]{2,1,0:T(8,128)}, f32[8,96,256]{2,1,0:T(8,128)}) custom-call(s32[4]{0:T(128)} %pad_add_fusion.refs_0_, bf16[8,240,256]{2,1,0:T(8,128)(2,1)} %copy-done.1, bf16[8,240,256]{2,1,0:T(8,128)(2,1)} %collective-permute-done.6.refs_2_, bf16[64,8,16,768]{3,2,1,0:T(8,128)(2,1)} %refs_4_.3, bf16[64,8,16,768]{3,2,1,0:T(8,128)(2,1)} %refs_4_.3, ...), custom_call_target="tpu_custom_call" | custom-call | flops 44236800000 | bytes 25165824 | tf_op jit(solution)/shard_map/judge_real/pallas_call | solution.py:402
  219.3 2.4 collective-permute-done.9
  221.8 1.6 collective-permute-start.10
  224.4 4.4 %collective-permute-done.10 = bf16[2,192,256]{2,1,0:T(8,128)(2,1)S(1)} collective-permute-done((bf16[2,192,256]{2,1,0:T(8,128)(2,1)S(1)}, bf16[2,192,256]{2,1,0:T(8,128)(2,1)S(1)}, u32[]{:S(2)}, u32[]{:S(2)}) %collective-permute-start.10) | collective-permute-done | bytes 196640 | tf_op jit(solution)/shard_map/ppermute | solution.py:936
  228.8 1.7 collective-permute-done.11
  230.6 2.7 %collective-permute-start.12 = (f32[1,192,256]{2,1,0:T(8,128)S(1)}, f32[1,192,256]{2,1,0:T(8,128)S(1)}, u32[]{:S(2)}, u32[]{:S(2)}) collective-permute-start(f32[1,192,256]{2,1,0:T(8,128)S(1)} %slice.146), channel_id=1, source_target_pairs={{0,16},{2,18},{4,20},{6,22},{8,24},{10,26},{12,28},{14,30},{16,0},... | collective-permute-start | bytes 589832 | tf_op jit(solution)/shard_map/ppermute | solution.py:936
  234.3 1.2 slice.137
  235.5 3.3 %collective-permute-done.13 = bf16[2,96,256]{2,1,0:T(8,128)(2,1)S(1)} collective-permute-done((bf16[2,96,256]{2,1,0:T(8,128)(2,1)S(1)}, bf16[2,96,256]{2,1,0:T(8,128)(2,1)S(1)}, u32[]{:S(2)}, u32[]{:S(2)}) %collective-permute-start.13) | collective-permute-done | bytes 98336 | tf_op jit(solution)/shard_map/ppermute | solution.py:936
  238.8 2.8 %collective-permute-done.12 = f32[1,192,256]{2,1,0:T(8,128)S(1)} collective-permute-done((f32[1,192,256]{2,1,0:T(8,128)S(1)}, f32[1,192,256]{2,1,0:T(8,128)S(1)}, u32[]{:S(2)}, u32[]{:S(2)}) %collective-permute-start.12) | collective-permute-done | bytes 196640 | tf_op jit(solution)/shard_map/ppermute | solution.py:936
  243.7 5.2 %collective-permute-done.15 = f32[1,96,256]{2,1,0:T(8,128)S(1)} collective-permute-done((f32[1,96,256]{2,1,0:T(8,128)S(1)}, f32[1,96,256]{2,1,0:T(8,128)S(1)}, u32[]{:S(2)}, u32[]{:S(2)}) %collective-permute-start.15) | collective-permute-done | bytes 98336 | tf_op jit(solution)/shard_map/ppermute | solution.py:936
  249.2 1.7 collective-permute-start.16
  251.7 0.7 multiply_subtract_fusion
  256.1 1.8 compare_select_fusion
  (131 shorter events, 13.0 us)
Async XLA Ops:
  7.2 158.6 %all-reduce.2.cloned.1.call-start = ((), (), s32[]{:S(2)}) async-start(), calls=%async_computation | async-start | bytes 524288 | tf_op jit(solution)/shard_map/psum | solution.py:1116
  9.4 11.1 %collective-permute-start.2 = (bf16[1,240,256]{2,1,0:T(8,128)(2,1)}, bf16[1,240,256]{2,1,0:T(8,128)(2,1)S(1)}, u32[]{:S(2)}, u32[]{:S(2)}) collective-permute-start(bf16[1,240,256]{2,1,0:T(8,128)(2,1)} %bitcast.53), channel_id=1, source_target_pairs={{0,16},{2,18},{4,20},{6,22},{8,24},{10,26},{12,28},{14,30},{16,0},... | collective-permute-start | bytes 368648 | tf_op jit(solution)/shard_map/ppermute | solution.py:936
  20.4 16.0 %copy-start.4 = (f32[256,256]{1,0:T(8,128)S(1)}, f32[256,256]{1,0:T(8,128)}, u32[]{:S(2)}) copy-start(f32[256,256]{1,0:T(8,128)} %count.1) | copy-start | bytes 786436
  20.5 7.5 %collective-permute-start.3 = (bf16[2,240,256]{2,1,0:T(8,128)(2,1)S(1)}, bf16[2,240,256]{2,1,0:T(8,128)(2,1)S(1)}, u32[]{:S(2)}, u32[]{:S(2)}) collective-permute-start(bf16[2,240,256]{2,1,0:T(8,128)(2,1)S(1)} %pad_maximum_fusion.2), channel_id=1, source_target_pairs={{0,8},{2,10},{4,12},{6,14},{8,0},{10,2},{12,4},{14,6},{16,24},{18,... | collective-permute-start | bytes 737288 | tf_op jit(solution)/shard_map/ppermute | solution.py:936
  28.0 11.8 %collective-permute-start.4 = (bf16[4,240,256]{2,1,0:T(8,128)(2,1)S(1)}, bf16[4,240,256]{2,1,0:T(8,128)(2,1)S(1)}, u32[]{:S(2)}, u32[]{:S(2)}) collective-permute-start(bf16[4,240,256]{2,1,0:T(8,128)(2,1)S(1)} %pad_maximum_fusion.1), channel_id=1, source_target_pairs={{0,4},{2,6},{4,0},{6,2},{8,12},{10,14},{12,8},{14,10},{16,20},{18,... | collective-permute-start | bytes 1474568 | tf_op jit(solution)/shard_map/ppermute | solution.py:936
  29.6 6.9 %collective-permute-start.1 = (f32[256,256]{1,0:T(8,128)}, f32[256,256]{1,0:T(8,128)S(1)}, u32[]{:S(2)}, u32[]{:S(2)}) collective-permute-start(f32[256,256]{1,0:T(8,128)} %count.1), channel_id=1, source_target_pairs={{0,1},{1,0},{2,3},{3,2},{4,5},{5,4},{6,7},{7,6},{8,9},{9,8},{10,11... | collective-permute-start | bytes 786440 | tf_op jit(solution)/shard_map/ppermute | solution.py:936
  31.8 5.4 %collective-permute-start.5 = (s32[64,16]{0,1:T(8,128)S(1)}, s32[64,16]{0,1:T(8,128)S(1)}, u32[]{:S(2)}, u32[]{:S(2)}) collective-permute-start(s32[64,16]{0,1:T(8,128)S(1)} %dynamic-slice_bitcast_fusion.1), channel_id=1, source_target_pairs={{0,1},{1,0},{2,3},{3,2},{4,5},{5,4},{6,7},{7,6},{8,9},{9,8},{10,11... | collective-permute-start | bytes 12296 | tf_op jit(solution)/shard_map/ppermute | solution.py:936
  39.9 5.1 %collective-permute-start.6 = (bf16[8,240,256]{2,1,0:T(8,128)(2,1)S(1)}, bf16[8,240,256]{2,1,0:T(8,128)(2,1)}, u32[]{:S(2)}, u32[]{:S(2)}) collective-permute-start(bf16[8,240,256]{2,1,0:T(8,128)(2,1)S(1)} %pad_maximum_fusion.refs_1_), channel_id=1, source_target_pairs={{0,2},{2,0},{4,6},{6,4},{8,10},{10,8},{12,14},{14,12},{16,18},{18,... | collective-permute-start | bytes 2949128 | tf_op jit(solution)/shard_map/ppermute | solution.py:936
  41.8 123.9 %collective-permute-start = (bf16[64,16,768]{2,1,0:T(8,128)(2,1)S(1)}, bf16[64,16,768]{2,1,0:T(8,128)(2,1)}, u32[]{:S(2)}, u32[]{:S(2)}) collective-permute-start(bf16[64,16,768]{2,1,0:T(8,128)(2,1)S(1)} %dynamic-slice_bitcast_fusion), channel_id=1, source_target_pairs={{0,1},{1,0},{2,3},{3,2},{4,5},{5,4},{6,7},{7,6},{8,9},{9,8},{10,11... | collective-permute-start | bytes 4718600 | tf_op jit(solution)/shard_map/ppermute | solution.py:936
  165.8 3.7 %collective-permute-start.7 = (f32[8,192,256]{2,1,0:T(8,128)}, f32[8,192,256]{2,1,0:T(8,128)S(1)}, u32[]{:S(2)}, u32[]{:S(2)}) collective-permute-start(f32[8,192,256]{2,1,0:T(8,128)} %get-tuple-element.73), channel_id=1, source_target_pairs={{0,2},{2,0},{4,6},{6,4},{8,10},{10,8},{12,14},{14,12},{16,18},{18,... | collective-permute-start | bytes 4718600 | tf_op jit(solution)/shard_map/ppermute | solution.py:936
  171.1 48.0 %collective-permute-start.8 = (bf16[4,192,256]{2,1,0:T(8,128)(2,1)S(1)}, bf16[4,192,256]{2,1,0:T(8,128)(2,1)S(1)}, u32[]{:S(2)}, u32[]{:S(2)}) collective-permute-start(bf16[4,192,256]{2,1,0:T(8,128)(2,1)S(1)} %slice.205), channel_id=1, source_target_pairs={{0,4},{2,6},{4,0},{6,2},{8,12},{10,14},{12,8},{14,10},{16,20},{18,... | collective-permute-start | bytes 1179656 | tf_op jit(solution)/shard_map/ppermute | solution.py:936
  219.1 2.6 collective-permute-start.9
  221.8 7.0 %collective-permute-start.10 = (bf16[2,192,256]{2,1,0:T(8,128)(2,1)S(1)}, bf16[2,192,256]{2,1,0:T(8,128)(2,1)S(1)}, u32[]{:S(2)}, u32[]{:S(2)}) collective-permute-start(bf16[2,192,256]{2,1,0:T(8,128)(2,1)S(1)} %slice.206), channel_id=1, source_target_pairs={{0,8},{2,10},{4,12},{6,14},{8,0},{10,2},{12,4},{14,6},{16,24},{18,... | collective-permute-start | bytes 589832 | tf_op jit(solution)/shard_map/ppermute | solution.py:936
  223.8 6.7 %collective-permute-start.11 = (bf16[4,96,256]{2,1,0:T(8,128)(2,1)S(1)}, bf16[4,96,256]{2,1,0:T(8,128)(2,1)S(1)}, u32[]{:S(2)}, u32[]{:S(2)}) collective-permute-start(bf16[4,96,256]{2,1,0:T(8,128)(2,1)S(1)} %fusion), channel_id=1, source_target_pairs={{0,4},{2,6},{4,0},{6,2},{8,12},{10,14},{12,8},{14,10},{16,20},{18,... | collective-permute-start | bytes 589832 | tf_op jit(solution)/shard_map/ppermute | solution.py:936
  230.6 11.0 %collective-permute-start.12 = (f32[1,192,256]{2,1,0:T(8,128)S(1)}, f32[1,192,256]{2,1,0:T(8,128)S(1)}, u32[]{:S(2)}, u32[]{:S(2)}) collective-permute-start(f32[1,192,256]{2,1,0:T(8,128)S(1)} %slice.146), channel_id=1, source_target_pairs={{0,16},{2,18},{4,20},{6,22},{8,24},{10,26},{12,28},{14,30},{16,0},... | collective-permute-start | bytes 589832 | tf_op jit(solution)/shard_map/ppermute | solution.py:936
  233.7 5.1 %collective-permute-start.13 = (bf16[2,96,256]{2,1,0:T(8,128)(2,1)S(1)}, bf16[2,96,256]{2,1,0:T(8,128)(2,1)S(1)}, u32[]{:S(2)}, u32[]{:S(2)}) collective-permute-start(bf16[2,96,256]{2,1,0:T(8,128)(2,1)S(1)} %fusion.6), channel_id=1, source_target_pairs={{0,8},{2,10},{4,12},{6,14},{8,0},{10,2},{12,4},{14,6},{16,24},{18,... | collective-permute-start | bytes 294920 | tf_op jit(solution)/shard_map/ppermute | solution.py:936
  235.5 15.5 %copy-start.11 = (f32[4,16,256]{2,1,0:T(8,128)S(1)}, f32[4,16,256]{2,1,0:T(8,128)}, u32[]{:S(2)}) copy-start(f32[4,16,256]{2,1,0:T(8,128)} %param.43) | copy-start | bytes 196612
  241.8 7.1 %collective-permute-start.14 = (f32[1,192,256]{2,1,0:T(8,128)S(1)}, f32[1,192,256]{2,1,0:T(8,128)S(1)}, u32[]{:S(2)}, u32[]{:S(2)}) collective-permute-start(f32[1,192,256]{2,1,0:T(8,128)S(1)} %slice_add_fusion.2), channel_id=1, source_target_pairs={{0,1},{1,0},{2,3},{3,2},{4,5},{5,4},{6,7},{7,6},{8,9},{9,8},{10,11... | collective-permute-start | bytes 589832 | tf_op jit(solution)/shard_map/ppermute | solution.py:936
  242.0 15.9 %copy-start.16 = (f32[48,4]{0,1:T(4,128)S(1)}, f32[48,4]{0,1:T(4,128)}, u32[]{:S(2)}) copy-start(f32[48,4]{0,1:T(4,128)} %param.38) | copy-start | bytes 2308
  242.0 15.9 %copy-start.23 = (f32[48,4]{0,1:T(4,128)S(1)}, f32[48,4]{0,1:T(4,128)}, u32[]{:S(2)}) copy-start(f32[48,4]{0,1:T(4,128)} %param.54) | copy-start | bytes 2308
  242.0 15.9 %copy-start.24 = (f32[48,4]{0,1:T(4,128)S(1)}, f32[48,4]{0,1:T(4,128)}, u32[]{:S(2)}) copy-start(f32[48,4]{0,1:T(4,128)} %param.46) | copy-start | bytes 2308
  242.1 6.8 %collective-permute-start.15 = (f32[1,96,256]{2,1,0:T(8,128)S(1)}, f32[1,96,256]{2,1,0:T(8,128)S(1)}, u32[]{:S(2)}, u32[]{:S(2)}) collective-permute-start(f32[1,96,256]{2,1,0:T(8,128)S(1)} %slice.156), channel_id=1, source_target_pairs={{0,16},{2,18},{4,20},{6,22},{8,24},{10,26},{12,28},{14,30},{16,0},... | collective-permute-start | bytes 294920 | tf_op jit(solution)/shard_map/ppermute | solution.py:936
  242.8 15.7 %copy-start.14 = (f32[128,16]{0,1:T(8,128)S(1)}, f32[128,16]{0,1:T(8,128)}, u32[]{:S(2)}) copy-start(f32[128,16]{0,1:T(8,128)} %param.40) | copy-start | bytes 24580
  242.8 15.7 %copy-start.17 = (f32[128,16]{0,1:T(8,128)S(1)}, f32[128,16]{0,1:T(8,128)}, u32[]{:S(2)}) copy-start(f32[128,16]{0,1:T(8,128)} %param.56) | copy-start | bytes 24580
  242.8 15.7 %copy-start.18 = (f32[128,16]{0,1:T(8,128)S(1)}, f32[128,16]{0,1:T(8,128)}, u32[]{:S(2)}) copy-start(f32[128,16]{0,1:T(8,128)} %param.48) | copy-start | bytes 24580
  242.8 16.4 %copy-start.22 = (f32[16]{0:T(128)S(1)}, f32[16]{0:T(128)}, u32[]{:S(2)}) copy-start(f32[16]{0:T(128)} %param.41) | copy-start | bytes 196
  242.8 16.4 %copy-start.27 = (f32[16]{0:T(128)S(1)}, f32[16]{0:T(128)}, u32[]{:S(2)}) copy-start(f32[16]{0:T(128)} %param.57) | copy-start | bytes 196
  242.8 16.3 %copy-start.28 = (f32[16]{0:T(128)S(1)}, f32[16]{0:T(128)}, u32[]{:S(2)}) copy-start(f32[16]{0:T(128)} %param.49) | copy-start | bytes 196
  242.9 16.9 %copy-start.7 = (f32[128,128]{1,0:T(8,128)S(1)}, f32[128,128]{1,0:T(8,128)}, u32[]{:S(2)}) copy-start(f32[128,128]{1,0:T(8,128)} %mid_conv.1) | copy-start | bytes 196612
  242.9 16.9 %copy-start.12 = (f32[128,128]{1,0:T(8,128)S(1)}, f32[128,128]{1,0:T(8,128)}, u32[]{:S(2)}) copy-start(f32[128,128]{1,0:T(8,128)} %param.55) | copy-start | bytes 196612
  242.9 16.9 %copy-start.13 = (f32[128,128]{1,0:T(8,128)S(1)}, f32[128,128]{1,0:T(8,128)}, u32[]{:S(2)}) copy-start(f32[128,128]{1,0:T(8,128)} %param.47) | copy-start | bytes 196612
  249.2 5.7 %collective-permute-start.16 = (f32[1,96,256]{2,1,0:T(8,128)S(1)}, f32[1,96,256]{2,1,0:T(8,128)S(1)}, u32[]{:S(2)}, u32[]{:S(2)}) collective-permute-start(f32[1,96,256]{2,1,0:T(8,128)S(1)} %slice_add_fusion.3), channel_id=1, source_target_pairs={{0,1},{1,0},{2,3},{3,2},{4,5},{5,4},{6,7},{7,6},{8,9},{9,8},{10,11... | collective-permute-start | bytes 294920 | tf_op jit(solution)/shard_map/ppermute | solution.py:936
  (15 other events, 144.2 us)
Sparse Core Ops, SparseCore 0:
  45.1 89.1 all-reduce.1

commit v5 on v4

--- a/solution.py
+++ b/solution.py
@@ -201,7 +201,7 @@
     yield
 
 
-def real_kernel(band, lanes, chunks, count_all):
+def real_kernel(band, lanes, chunks, count_all, share):
     rows_n = band + 1
     total = chunks * rows_n
 
@@ -354,7 +354,12 @@
                 first_s[16 * owner : 16 * owner + 4, :] = first[4 * owner : 4 * owner + 4, :]
             lastt_s[...] = gwl_ref[...].T
             scalars = jnp.zeros((1, 128), F32)
-            sums = (jnp.sum(fake_loss[2:3, :]), jnp.sum(fake_loss[1:2, :]), jnp.sum(fake_loss[0:1, :]) + jnp.sum(loss_ref[0:1, :]))
+            sums = (
+                jnp.sum(fake_loss[2:3, :]),
+                jnp.sum(fake_loss[3:4, 0:1]) * share,
+                jnp.sum(fake_loss[1:2, :]),
+                jnp.sum(fake_loss[0:1, :]) + jnp.sum(loss_ref[0:1, :]),
+            )
             for number, item in enumerate(sums):
                 scalars = jnp.where(lax.broadcasted_iota(jnp.int32, (1, 128), 1) == number, item, scalars)
             for owner, core, chip in slab_targets(me):
@@ -400,7 +405,7 @@
     scratch += [((256, 128), F32), ((256, 128), F32), ((8, lanes), F32)]
     scratch += [((128, lanes), BF16), ((256, lanes), BF16)]
     return pl.pallas_call(
-        real_kernel(band, lanes, chunks, count_all),
+        real_kernel(band, lanes, chunks, count_all, 1.0 / (lax.axis_size("dp") * lax.axis_size("grp"))),
         grid=(total + 1,),
         in_specs=specs,
         out_specs=[pl.BlockSpec(item.shape, lambda t, n=len(item.shape): (0,) * n) for item in outs],
@@ -706,20 +711,18 @@
             interleave(
                 (back_gen(), 4 * len(halves)),
                 *((front_block(part), 5) for part in halves),
-                *((back_encode(part), 5) for part in halves),
                 (front_turn(), 6),
                 (back_middle(), 2),
             )
             interleave(
-                (back_recon(), 4, 0.0, 0.6),
-                (back_disc(), 4 * len(halves), 0.0, 0.6),
-                (front_recon(), 4 * len(halves), 0.1, 0.8),
-                (front_first(), 4 * len(halves), 0.3, 1.0),
-            )
-            interleave(
-                *((back_chain(part), 10, 0.0, 0.9 + 0.1 * number) for number, part in enumerate(halves)),
-                *((front_middle(part), 7, 0.1, 1.0) for part in halves),
-                (back_fill(), 11, 0.05, 1.0),
+                (back_recon(), 4, 0.0, 0.2),
+                (back_disc(), 4 * len(halves), 0.0, 0.25),
+                (front_recon(), 4 * len(halves), 0.02, 0.42),
+                (front_first(), 4 * len(halves), 0.12, 0.53),
+                *((back_encode(part), 5, 0.0, 0.45) for part in halves),
+                *((back_chain(part), 10, 0.22, 0.95) for part in halves),
+                *((front_middle(part), 7, 0.54, 1.0) for part in halves),
+                (back_fill(), 11, 0.3, 1.0),
             )
             interleave((front_last(), 1), (back_stream(), 1))
             shift()
@@ -1060,7 +1063,7 @@
     for index, axis in enumerate(AXES):
         whole = jnp.concatenate([share[index] for share in shares], axis=axis)
         totals.append(lax.psum_scatter(whole, "dp", scatter_dimension=axis, tiled=True))
-    scalars = judge[1][0, 80, 128:131]
+    scalars = judge[1][0, 80, 128:132]
     totals.append(lax.psum(scalars, "dp"))
     return lax.psum(tuple(totals), "grp")
 
@@ -1134,7 +1137,7 @@
         got, judge = lax.optimization_barrier((got, judge))
         auto_total, judge_total = reduce_both(auto_keep, got, *judge)
         totals = (*unpack_auto(auto_total), *unpack_judge_grads(judge_total))
-        losses = judge_total[80, 128:131]
+        losses = judge_total[80, 128:132]
     else:
         *totals, losses = whole_grads(auto, judge)
 
@@ -1155,8 +1158,8 @@
         *(result[0] for result in results),
         *(result[1] for result in results),
         *(result[2] for result in results),
-        jnp.where(jnp.arange(2) == 0, losses[0], fake_outs[6][3, 0]),
-        losses[1:3],
+        losses[0:2],
+        losses[2:4],
         perplexity,
     )
 

time: 269 us -> 262 us (0.974)
  Pallas kernels: 175 us -> 170 us
    pallas_call x1, Pallas kernels: 121 us -> 116 us  [run_fake(): pl.pallas_call(fake_kernel(band, lanes, chunks, count_all), grid=(total +...]
where the time goes in v5:
time: 262 us; the launch traced here: 261 us
  Pallas kernels  170 us (65%)
  waiting for transfers between devices  37.4 us (14%)
  starting transfers between devices  20.1 us (8%)
  between operations  16.6 us (6%)
  other arithmetic  11 us (4%)
  local copies, waits for them, and re-layouts  6.52 us (2%)
    pallas_call x1, Pallas kernels, run_fake(): pl.pallas_call(fake_kernel(band, lanes, chunks, count_all), grid=(total +...  116 us
    pallas_call x1, Pallas kernels, run_real(): pl.pallas_call(real_kernel(band, lanes, chunks, count_all, 1.0 / (lax.axi...  46.4 us
    ppermute x17, waiting for transfers between devices, swap(): lax.ppermute(x, axis, [(i, i ^ bits) for i in range(lax.axis_size(axis))])  37.4 us
    ppermute x17, starting transfers between devices, swap(): lax.ppermute(x, axis, [(i, i ^ bits) for i in range(lax.axis_size(axis))])  20.1 us
    pallas_call x1, Pallas kernels, count_codes(): pl.pallas_call(count_kernel, grid=(parts,), in_specs=[pl.BlockSpec((1, 1,...  5.29 us
  transfers between devices with their start and end apart: 18, of which 10 were waited for; matrix products, arithmetic and copies ran while one was open for 5% of the time, Pallas kernels for 64%

profile of v5, /device:TPU:0, one launch (start us, length us, event | category | flops | bytes accessed | tf_op | source)
XLA Modules:
  0.0 261.5 jit_solution(4960458332184280092)
XLA Ops:
  7.3 2.1 frames.1
  9.4 4.0 %collective-permute-start.2 = (bf16[1,240,256]{2,1,0:T(8,128)(2,1)}, bf16[1,240,256]{2,1,0:T(8,128)(2,1)S(1)}, u32[]{:S(2)}, u32[]{:S(2)}) collective-permute-start(bf16[1,240,256]{2,1,0:T(8,128)(2,1)} %bitcast.53), channel_id=1, source_target_pairs={{0,16},{2,18},{4,20},{6,22},{8,24},{10,26},{12,28},{14,30},{16,0},... | collective-permute-start | bytes 368648 | tf_op jit(solution)/shard_map/ppermute | solution.py:939
  13.4 0.8 convert_bitcast_fusion
  14.4 0.8 convert_element_type.69.codes_ref
  15.1 5.3 %count.1 = f32[256,256]{1,0:T(8,128)} custom-call(f32[8,1,1024]{2,1,0:T(1,128)} %convert_element_type.69.codes_ref), custom_call_target="tpu_custom_call" | custom-call | flops 4096000000 | bytes 32768 | tf_op jit(solution)/shard_map/count/pallas_call | solution.py:851
  20.5 1.6 collective-permute-start.3
  22.1 5.8 %collective-permute-done.3 = bf16[2,240,256]{2,1,0:T(8,128)(2,1)S(1)} collective-permute-done((bf16[2,240,256]{2,1,0:T(8,128)(2,1)S(1)}, bf16[2,240,256]{2,1,0:T(8,128)(2,1)S(1)}, u32[]{:S(2)}, u32[]{:S(2)}) %collective-permute-start.3) | collective-permute-done | bytes 245792 | tf_op jit(solution)/shard_map/ppermute | solution.py:939
  28.0 1.6 collective-permute-start.4
  29.6 1.5 collective-permute-start.1
  31.1 0.7 dynamic-slice_bitcast_fusion.1
  32.3 4.2 %collective-permute-done.1 = f32[256,256]{1,0:T(8,128)S(1)} collective-permute-done((f32[256,256]{1,0:T(8,128)}, f32[256,256]{1,0:T(8,128)S(1)}, u32[]{:S(2)}, u32[]{:S(2)}) %collective-permute-start.1) | collective-permute-done | bytes 262176 | tf_op jit(solution)/shard_map/ppermute | solution.py:939
  36.4 0.7 add.174
  37.2 2.7 %collective-permute-done.4 = bf16[4,240,256]{2,1,0:T(8,128)(2,1)S(1)} collective-permute-done((bf16[4,240,256]{2,1,0:T(8,128)(2,1)S(1)}, bf16[4,240,256]{2,1,0:T(8,128)(2,1)S(1)}, u32[]{:S(2)}, u32[]{:S(2)}) %collective-permute-start.4) | collective-permute-done | bytes 491552 | tf_op jit(solution)/shard_map/ppermute | solution.py:939
  40.0 1.8 dynamic-slice_bitcast_fusion
  41.9 1.6 collective-permute-start
  45.0 116.0 %judge_fake.1 = (f32[8,192,256]{2,1,0:T(8,128)}, f32[8,192,256]{2,1,0:T(8,128)}, f32[1024,256]{1,0:T(8,128)}, f32[128,256]{1,0:T(8,128)}, f32[192,256]{1,0:T(8,1...) custom-call(s32[4]{0:T(128)} %pad_add_fusion.refs_0_, bf16[8,240,256]{2,1,0:T(8,128)(2,1)} %copy-done.1, ...), custom_call_target="tpu_custom_call" | custom-call | flops 131072000000 | bytes 25165824 | tf_op jit(solution)/shard_map/judge_fake/pallas_call | solution.py:823
  161.2 3.6 %collective-permute-done.7 = f32[8,192,256]{2,1,0:T(8,128)S(1)} collective-permute-done((f32[8,192,256]{2,1,0:T(8,128)}, f32[8,192,256]{2,1,0:T(8,128)S(1)}, u32[]{:S(2)}, u32[]{:S(2)}) %collective-permute-start.7) | collective-permute-done | bytes 1572896 | tf_op jit(solution)/shard_map/ppermute | solution.py:939
  164.8 1.6 add.175
  166.5 1.6 collective-permute-start.8
  168.0 46.4 %judge_real.1 = (f32[8,96,256]{2,1,0:T(8,128)}, f32[8,96,256]{2,1,0:T(8,128)}) custom-call(s32[4]{0:T(128)} %pad_add_fusion.refs_0_, bf16[8,240,256]{2,1,0:T(8,128)(2,1)} %copy-done.1, bf16[8,240,256]{2,1,0:T(8,128)(2,1)} %collective-permute-done.6.refs_2_, bf16[64,8,16,768]{3,2,1,0:T(8,128)(2,1)} %refs_4_.3, bf16[64,8,16,768]{3,2,1,0:T(8,128)(2,1)} %refs_4_.3, ...), custom_call_target="tpu_custom_call" | custom-call | flops 44236800000 | bytes 25165824 | tf_op jit(solution)/shard_map/judge_real/pallas_call | solution.py:407
  214.6 2.4 collective-permute-done.9
  217.1 1.6 collective-permute-start.10
  219.7 4.4 %collective-permute-done.10 = bf16[2,192,256]{2,1,0:T(8,128)(2,1)S(1)} collective-permute-done((bf16[2,192,256]{2,1,0:T(8,128)(2,1)S(1)}, bf16[2,192,256]{2,1,0:T(8,128)(2,1)S(1)}, u32[]{:S(2)}, u32[]{:S(2)}) %collective-permute-start.10) | collective-permute-done | bytes 196640 | tf_op jit(solution)/shard_map/ppermute | solution.py:939
  224.1 1.7 collective-permute-done.11
  225.9 2.7 %collective-permute-start.12 = (f32[1,192,256]{2,1,0:T(8,128)S(1)}, f32[1,192,256]{2,1,0:T(8,128)S(1)}, u32[]{:S(2)}, u32[]{:S(2)}) collective-permute-start(f32[1,192,256]{2,1,0:T(8,128)S(1)} %slice.145), channel_id=1, source_target_pairs={{0,16},{2,18},{4,20},{6,22},{8,24},{10,26},{12,28},{14,30},{16,0},... | collective-permute-start | bytes 589832 | tf_op jit(solution)/shard_map/ppermute | solution.py:939
  229.7 4.4 %collective-permute-done.13 = bf16[2,96,256]{2,1,0:T(8,128)(2,1)S(1)} collective-permute-done((bf16[2,96,256]{2,1,0:T(8,128)(2,1)S(1)}, bf16[2,96,256]{2,1,0:T(8,128)(2,1)S(1)}, u32[]{:S(2)}, u32[]{:S(2)}) %collective-permute-start.13) | collective-permute-done | bytes 98336 | tf_op jit(solution)/shard_map/ppermute | solution.py:939
  234.1 2.9 %collective-permute-done.12 = f32[1,192,256]{2,1,0:T(8,128)S(1)} collective-permute-done((f32[1,192,256]{2,1,0:T(8,128)S(1)}, f32[1,192,256]{2,1,0:T(8,128)S(1)}, u32[]{:S(2)}, u32[]{:S(2)}) %collective-permute-start.12) | collective-permute-done | bytes 196640 | tf_op jit(solution)/shard_map/ppermute | solution.py:939
  239.0 5.2 %collective-permute-done.15 = f32[1,96,256]{2,1,0:T(8,128)S(1)} collective-permute-done((f32[1,96,256]{2,1,0:T(8,128)S(1)}, f32[1,96,256]{2,1,0:T(8,128)S(1)}, u32[]{:S(2)}, u32[]{:S(2)}) %collective-permute-start.15) | collective-permute-done | bytes 98336 | tf_op jit(solution)/shard_map/ppermute | solution.py:939
  244.6 1.7 collective-permute-start.16
  246.3 0.7 multiply_subtract_fusion.2
  247.0 0.7 multiply_subtract_fusion
  252.8 0.7 multiply_subtract_fusion.1
  (128 shorter events, 11.2 us)
Async XLA Ops:
  7.2 153.9 %all-reduce.2.cloned.1.call-start = ((), (), s32[]{:S(2)}) async-start(), calls=%async_computation | async-start | bytes 524288 | tf_op jit(solution)/shard_map/psum | solution.py:1119
  9.4 11.1 %collective-permute-start.2 = (bf16[1,240,256]{2,1,0:T(8,128)(2,1)}, bf16[1,240,256]{2,1,0:T(8,128)(2,1)S(1)}, u32[]{:S(2)}, u32[]{:S(2)}) collective-permute-start(bf16[1,240,256]{2,1,0:T(8,128)(2,1)} %bitcast.53), channel_id=1, source_target_pairs={{0,16},{2,18},{4,20},{6,22},{8,24},{10,26},{12,28},{14,30},{16,0},... | collective-permute-start | bytes 368648 | tf_op jit(solution)/shard_map/ppermute | solution.py:939
  20.4 16.0 %copy-start.4 = (f32[256,256]{1,0:T(8,128)S(1)}, f32[256,256]{1,0:T(8,128)}, u32[]{:S(2)}) copy-start(f32[256,256]{1,0:T(8,128)} %count.1) | copy-start | bytes 786436
  20.5 7.5 %collective-permute-start.3 = (bf16[2,240,256]{2,1,0:T(8,128)(2,1)S(1)}, bf16[2,240,256]{2,1,0:T(8,128)(2,1)S(1)}, u32[]{:S(2)}, u32[]{:S(2)}) collective-permute-start(bf16[2,240,256]{2,1,0:T(8,128)(2,1)S(1)} %pad_maximum_fusion.2), channel_id=1, source_target_pairs={{0,8},{2,10},{4,12},{6,14},{8,0},{10,2},{12,4},{14,6},{16,24},{18,... | collective-permute-start | bytes 737288 | tf_op jit(solution)/shard_map/ppermute | solution.py:939
  28.0 11.8 %collective-permute-start.4 = (bf16[4,240,256]{2,1,0:T(8,128)(2,1)S(1)}, bf16[4,240,256]{2,1,0:T(8,128)(2,1)S(1)}, u32[]{:S(2)}, u32[]{:S(2)}) collective-permute-start(bf16[4,240,256]{2,1,0:T(8,128)(2,1)S(1)} %pad_maximum_fusion.1), channel_id=1, source_target_pairs={{0,4},{2,6},{4,0},{6,2},{8,12},{10,14},{12,8},{14,10},{16,20},{18,... | collective-permute-start | bytes 1474568 | tf_op jit(solution)/shard_map/ppermute | solution.py:939
  29.6 6.9 %collective-permute-start.1 = (f32[256,256]{1,0:T(8,128)}, f32[256,256]{1,0:T(8,128)S(1)}, u32[]{:S(2)}, u32[]{:S(2)}) collective-permute-start(f32[256,256]{1,0:T(8,128)} %count.1), channel_id=1, source_target_pairs={{0,1},{1,0},{2,3},{3,2},{4,5},{5,4},{6,7},{7,6},{8,9},{9,8},{10,11... | collective-permute-start | bytes 786440 | tf_op jit(solution)/shard_map/ppermute | solution.py:939
  31.8 5.4 %collective-permute-start.5 = (s32[64,16]{0,1:T(8,128)S(1)}, s32[64,16]{0,1:T(8,128)S(1)}, u32[]{:S(2)}, u32[]{:S(2)}) collective-permute-start(s32[64,16]{0,1:T(8,128)S(1)} %dynamic-slice_bitcast_fusion.1), channel_id=1, source_target_pairs={{0,1},{1,0},{2,3},{3,2},{4,5},{5,4},{6,7},{7,6},{8,9},{9,8},{10,11... | collective-permute-start | bytes 12296 | tf_op jit(solution)/shard_map/ppermute | solution.py:939
  40.0 5.1 %collective-permute-start.6 = (bf16[8,240,256]{2,1,0:T(8,128)(2,1)S(1)}, bf16[8,240,256]{2,1,0:T(8,128)(2,1)}, u32[]{:S(2)}, u32[]{:S(2)}) collective-permute-start(bf16[8,240,256]{2,1,0:T(8,128)(2,1)S(1)} %pad_maximum_fusion.refs_1_), channel_id=1, source_target_pairs={{0,2},{2,0},{4,6},{6,4},{8,10},{10,8},{12,14},{14,12},{16,18},{18,... | collective-permute-start | bytes 2949128 | tf_op jit(solution)/shard_map/ppermute | solution.py:939
  41.9 119.2 %collective-permute-start = (bf16[64,16,768]{2,1,0:T(8,128)(2,1)S(1)}, bf16[64,16,768]{2,1,0:T(8,128)(2,1)}, u32[]{:S(2)}, u32[]{:S(2)}) collective-permute-start(bf16[64,16,768]{2,1,0:T(8,128)(2,1)S(1)} %dynamic-slice_bitcast_fusion), channel_id=1, source_target_pairs={{0,1},{1,0},{2,3},{3,2},{4,5},{5,4},{6,7},{7,6},{8,9},{9,8},{10,11... | collective-permute-start | bytes 4718600 | tf_op jit(solution)/shard_map/ppermute | solution.py:939
  161.1 3.7 %collective-permute-start.7 = (f32[8,192,256]{2,1,0:T(8,128)}, f32[8,192,256]{2,1,0:T(8,128)S(1)}, u32[]{:S(2)}, u32[]{:S(2)}) collective-permute-start(f32[8,192,256]{2,1,0:T(8,128)} %get-tuple-element.73), channel_id=1, source_target_pairs={{0,2},{2,0},{4,6},{6,4},{8,10},{10,8},{12,14},{14,12},{16,18},{18,... | collective-permute-start | bytes 4718600 | tf_op jit(solution)/shard_map/ppermute | solution.py:939
  166.5 48.0 %collective-permute-start.8 = (bf16[4,192,256]{2,1,0:T(8,128)(2,1)S(1)}, bf16[4,192,256]{2,1,0:T(8,128)(2,1)S(1)}, u32[]{:S(2)}, u32[]{:S(2)}) collective-permute-start(bf16[4,192,256]{2,1,0:T(8,128)(2,1)S(1)} %slice.205), channel_id=1, source_target_pairs={{0,4},{2,6},{4,0},{6,2},{8,12},{10,14},{12,8},{14,10},{16,20},{18,... | collective-permute-start | bytes 1179656 | tf_op jit(solution)/shard_map/ppermute | solution.py:939
  214.4 2.6 collective-permute-start.9
  217.1 7.0 %collective-permute-start.10 = (bf16[2,192,256]{2,1,0:T(8,128)(2,1)S(1)}, bf16[2,192,256]{2,1,0:T(8,128)(2,1)S(1)}, u32[]{:S(2)}, u32[]{:S(2)}) collective-permute-start(bf16[2,192,256]{2,1,0:T(8,128)(2,1)S(1)} %slice.206), channel_id=1, source_target_pairs={{0,8},{2,10},{4,12},{6,14},{8,0},{10,2},{12,4},{14,6},{16,24},{18,... | collective-permute-start | bytes 589832 | tf_op jit(solution)/shard_map/ppermute | solution.py:939
  219.1 6.7 %collective-permute-start.11 = (bf16[4,96,256]{2,1,0:T(8,128)(2,1)S(1)}, bf16[4,96,256]{2,1,0:T(8,128)(2,1)S(1)}, u32[]{:S(2)}, u32[]{:S(2)}) collective-permute-start(bf16[4,96,256]{2,1,0:T(8,128)(2,1)S(1)} %fusion), channel_id=1, source_target_pairs={{0,4},{2,6},{4,0},{6,2},{8,12},{10,14},{12,8},{14,10},{16,20},{18,... | collective-permute-start | bytes 589832 | tf_op jit(solution)/shard_map/ppermute | solution.py:939
  225.9 11.0 %collective-permute-start.12 = (f32[1,192,256]{2,1,0:T(8,128)S(1)}, f32[1,192,256]{2,1,0:T(8,128)S(1)}, u32[]{:S(2)}, u32[]{:S(2)}) collective-permute-start(f32[1,192,256]{2,1,0:T(8,128)S(1)} %slice.145), channel_id=1, source_target_pairs={{0,16},{2,18},{4,20},{6,22},{8,24},{10,26},{12,28},{14,30},{16,0},... | collective-permute-start | bytes 589832 | tf_op jit(solution)/shard_map/ppermute | solution.py:939
  229.0 17.4 %copy-start.6 = (f32[4,16,256]{2,1,0:T(8,128)S(1)}, f32[4,16,256]{2,1,0:T(8,128)}, u32[]{:S(2)}) copy-start(f32[4,16,256]{2,1,0:T(8,128)} %matrices.1) | copy-start | bytes 196612
  229.0 17.3 %copy-start.10 = (f32[4,16,256]{2,1,0:T(8,128)S(1)}, f32[4,16,256]{2,1,0:T(8,128)}, u32[]{:S(2)}) copy-start(f32[4,16,256]{2,1,0:T(8,128)} %param.51) | copy-start | bytes 196612
  229.0 17.3 %copy-start.11 = (f32[4,16,256]{2,1,0:T(8,128)S(1)}, f32[4,16,256]{2,1,0:T(8,128)}, u32[]{:S(2)}) copy-start(f32[4,16,256]{2,1,0:T(8,128)} %param.43) | copy-start | bytes 196612
  229.0 5.1 %collective-permute-start.13 = (bf16[2,96,256]{2,1,0:T(8,128)(2,1)S(1)}, bf16[2,96,256]{2,1,0:T(8,128)(2,1)S(1)}, u32[]{:S(2)}, u32[]{:S(2)}) collective-permute-start(bf16[2,96,256]{2,1,0:T(8,128)(2,1)S(1)} %fusion.6), channel_id=1, source_target_pairs={{0,8},{2,10},{4,12},{6,14},{8,0},{10,2},{12,4},{14,6},{16,24},{18,... | collective-permute-start | bytes 294920 | tf_op jit(solution)/shard_map/ppermute | solution.py:939
  237.1 7.1 %collective-permute-start.14 = (f32[1,192,256]{2,1,0:T(8,128)S(1)}, f32[1,192,256]{2,1,0:T(8,128)S(1)}, u32[]{:S(2)}, u32[]{:S(2)}) collective-permute-start(f32[1,192,256]{2,1,0:T(8,128)S(1)} %slice_add_fusion.2), channel_id=1, source_target_pairs={{0,1},{1,0},{2,3},{3,2},{4,5},{5,4},{6,7},{7,6},{8,9},{9,8},{10,11... | collective-permute-start | bytes 589832 | tf_op jit(solution)/shard_map/ppermute | solution.py:939
  237.3 13.6 %copy-start.16 = (f32[48,4]{0,1:T(4,128)S(1)}, f32[48,4]{0,1:T(4,128)}, u32[]{:S(2)}) copy-start(f32[48,4]{0,1:T(4,128)} %param.38) | copy-start | bytes 2308
  237.4 13.6 %copy-start.23 = (f32[48,4]{0,1:T(4,128)S(1)}, f32[48,4]{0,1:T(4,128)}, u32[]{:S(2)}) copy-start(f32[48,4]{0,1:T(4,128)} %param.54) | copy-start | bytes 2308
  237.4 13.6 %copy-start.24 = (f32[48,4]{0,1:T(4,128)S(1)}, f32[48,4]{0,1:T(4,128)}, u32[]{:S(2)}) copy-start(f32[48,4]{0,1:T(4,128)} %param.46) | copy-start | bytes 2308
  237.4 6.8 %collective-permute-start.15 = (f32[1,96,256]{2,1,0:T(8,128)S(1)}, f32[1,96,256]{2,1,0:T(8,128)S(1)}, u32[]{:S(2)}, u32[]{:S(2)}) collective-permute-start(f32[1,96,256]{2,1,0:T(8,128)S(1)} %slice.155), channel_id=1, source_target_pairs={{0,16},{2,18},{4,20},{6,22},{8,24},{10,26},{12,28},{14,30},{16,0},... | collective-permute-start | bytes 294920 | tf_op jit(solution)/shard_map/ppermute | solution.py:939
  238.1 13.4 %copy-start.18 = (f32[128,16]{0,1:T(8,128)S(1)}, f32[128,16]{0,1:T(8,128)}, u32[]{:S(2)}) copy-start(f32[128,16]{0,1:T(8,128)} %param.48) | copy-start | bytes 24580
  238.1 14.1 %copy-start.22 = (f32[16]{0:T(128)S(1)}, f32[16]{0:T(128)}, u32[]{:S(2)}) copy-start(f32[16]{0:T(128)} %param.41) | copy-start | bytes 196
  238.1 14.1 %copy-start.27 = (f32[16]{0:T(128)S(1)}, f32[16]{0:T(128)}, u32[]{:S(2)}) copy-start(f32[16]{0:T(128)} %param.57) | copy-start | bytes 196
  238.2 14.1 %copy-start.28 = (f32[16]{0:T(128)S(1)}, f32[16]{0:T(128)}, u32[]{:S(2)}) copy-start(f32[16]{0:T(128)} %param.49) | copy-start | bytes 196
  238.2 14.6 %copy-start.7 = (f32[128,128]{1,0:T(8,128)S(1)}, f32[128,128]{1,0:T(8,128)}, u32[]{:S(2)}) copy-start(f32[128,128]{1,0:T(8,128)} %mid_conv.1) | copy-start | bytes 196612
  238.2 14.6 %copy-start.12 = (f32[128,128]{1,0:T(8,128)S(1)}, f32[128,128]{1,0:T(8,128)}, u32[]{:S(2)}) copy-start(f32[128,128]{1,0:T(8,128)} %param.55) | copy-start | bytes 196612
  238.2 14.6 %copy-start.13 = (f32[128,128]{1,0:T(8,128)S(1)}, f32[128,128]{1,0:T(8,128)}, u32[]{:S(2)}) copy-start(f32[128,128]{1,0:T(8,128)} %param.47) | copy-start | bytes 196612
  244.6 5.7 %collective-permute-start.16 = (f32[1,96,256]{2,1,0:T(8,128)S(1)}, f32[1,96,256]{2,1,0:T(8,128)S(1)}, u32[]{:S(2)}, u32[]{:S(2)}) collective-permute-start(f32[1,96,256]{2,1,0:T(8,128)S(1)} %slice_add_fusion.3), channel_id=1, source_target_pairs={{0,1},{1,0},{2,3},{3,2},{4,5},{5,4},{6,7},{7,6},{8,9},{9,8},{10,11... | collective-permute-start | bytes 294920 | tf_op jit(solution)/shard_map/ppermute | solution.py:939
  (15 other events, 140.4 us)
Sparse Core Ops, SparseCore 0:
  45.2 89.1 all-reduce.1
